TPU v7x, 256 devices: a whole 4x4x8 slice. The times are simulated.
256 devices in a mesh: plane: 32 (over x, z), depth: 8 (over y, core).
Axes of the slice: x: 4, y: 4, z: 8, core: 2. Of those that a mesh axis runs over, the one named last changes fastest.
Arguments:
- density: float32 [64, 262144], P(None, ('plane', 'depth')), may hold values from 0.01 to 1
- energy: float32 [64, 262144], P(None, ('plane', 'depth')), may hold values from 0.1 to 10
- links: int32 [27, 262144], P(None, ('plane', 'depth')), may hold values from 0 to 3584, as said below
- send_index: int32 [32, 8, 4, 512], P('plane', 'depth'), may hold values from 0 to 1023
- send_live: int32 [32, 8, 4], P('plane', 'depth'), may hold values from 128 to 512, as said below
- face_index: int32 [32, 8, 2, 256], P('plane', 'depth'), may hold values from 0 to 1023
Outputs:
- conductivity: float32 [64, 262144], P(None, ('plane', 'depth'))
- sensitivity: float32 [64, 262144], P(None, ('plane', 'depth'))
Inputs may be any that keep to these rules, and one draw needn't show every extreme that they name: `links`: the slot 13 of every block names the block itself; column 3584 stands for a neighbour outside the design domain. `send_live`: every brick has one plane neighbour whose list is full.
All inputs are finite; a program needn't handle non-finite values.
Results may differ from a plain program's by a relative error of at most 0.0003.
Values sent between devices are 32-bit elements; how exact they have to be, the bound alone decides.
No kernel may reach another device: no remote copies, remote signals or barrier semaphores. Data moves between devices by JAX's collectives and lax.ppermute only.
A program may use at most 64 MiB of HBM per device.

v0:
```python
import jax
import jax.numpy as jnp
from jax import lax
from jax.sharding import PartitionSpec as P

REACH = 2


radius = 3.0
floor_value = 0.001
penalty = 3.0


def passed_along(shard, axis, by):
    count = lax.axis_size(axis)
    pairs = [(i, i + by) for i in range(count) if 0 <= i + by < count]
    return lax.ppermute(shard, axis, pairs)


def padded(shard, sides, width):
    for axis, dim in sides:
        count, length = (lax.axis_size(axis), shard.shape[dim])
        up = [(i, (i + 1) % count) for i in range(count - 1)]
        down = [(j, i) for i, j in up]
        last = lax.slice_in_dim(shard, length - width, length, axis=dim)
        first = lax.slice_in_dim(shard, 0, width, axis=dim)
        before = lax.ppermute(last, axis, up)
        after = lax.ppermute(first, axis, down)
        shard = jnp.concatenate([before, shard, after], axis=dim)
    return shard


def cone_table():
    voxels = jnp.arange(64)
    places = jnp.stack([voxels // 16, voxels // 4 % 4, voxels % 4], axis=-1).astype(jnp.float32)
    slots = jnp.arange(27)
    moved = (
        jnp.stack([slots // 9 - 1, slots // 3 % 3 - 1, slots % 3 - 1], axis=-1).astype(jnp.float32)
        * 4.0
    )
    apart = places[None, :, None, :] - places[None, None, :, :] - moved[:, None, None, :]
    return jnp.maximum(0.0, radius - jnp.sqrt(jnp.sum(apart * apart, axis=-1)))


def local_rows(ext_rows, link_table, energy_rows, table):
    width = ext_rows.shape[0]
    row_sums = jnp.sum(table, axis=2)
    valid = (link_table != width - 1).astype(jnp.float32)
    weight_sum = jnp.dot(valid.T, row_sums, precision=lax.Precision.HIGHEST)
    picked = jnp.take(ext_rows, link_table, axis=0)
    filtered = jnp.einsum("kbj,kij->bi", picked, table, precision=lax.Precision.HIGHEST)
    filtered = filtered / weight_sum
    conductivity = floor_value + filtered * filtered * filtered * (1.0 - floor_value)
    scaled = -penalty * (1.0 - floor_value) * filtered * filtered * energy_rows / weight_sum
    spread = jnp.einsum("bi,kij->kbj", scaled, table, precision=lax.Precision.HIGHEST)
    back = (
        jnp.zeros((width, 64), jnp.float32).at[link_table.reshape(-1)].add(spread.reshape(-1, 64))
    )
    return (conductivity, back)


def on_device(density, energy, links, send_index, send_live, face_index):
    table = cone_table()
    blocks = density.shape[1]
    dens_rows = density.T
    energy_rows = energy.T
    indices = send_index[0, 0]
    counts = send_live[0, 0]
    faces_at = face_index[0, 0]
    capacity = indices.shape[1]
    keep = (jnp.arange(capacity)[None, :] < counts[:, None]).astype(jnp.float32)
    payload = jnp.take(dens_rows, indices, axis=0) * keep[:, :, None]
    offsets = [offset for offset in range(-REACH, REACH + 1) if offset != 0]
    received = [
        passed_along(payload[member], "plane", offset) for member, offset in enumerate(offsets)
    ]
    face_load = jnp.take(dens_rows, faces_at, axis=0)
    rims = padded(face_load, (("depth", 0),), 1)
    ext_rows = jnp.concatenate(
        [dens_rows] + received + [rims[0], rims[3], jnp.zeros((1, 64), jnp.float32)], axis=0
    )
    conductivity, back = local_rows(ext_rows, links, energy_rows, table)
    sens = back[:blocks]
    groups_back = [
        back[blocks + member * capacity : blocks + (member + 1) * capacity]
        for member in range(len(offsets))
    ]
    returned = [
        passed_along(groups_back[member], "plane", -offset) for member, offset in enumerate(offsets)
    ]
    low_start = blocks + len(offsets) * capacity
    face_count = faces_at.shape[1]
    face_back = jnp.stack(
        [
            back[low_start : low_start + face_count],
            back[low_start + face_count : low_start + 2 * face_count],
        ]
    )
    rims_back = padded(face_back, (("depth", 0),), 1)
    values = [returned[member] * keep[member][:, None] for member in range(len(offsets))] + [
        rims_back[0],
        rims_back[3],
    ]
    places = [indices[member] for member in range(len(offsets))] + [faces_at[0], faces_at[1]]
    sens = sens.at[jnp.concatenate(places)].add(jnp.concatenate(values, axis=0))
    return (conductivity.T, sens.T)


def solution(mesh):
    in_specs = (
        P(None, ("plane", "depth")),
        P(None, ("plane", "depth")),
        P(None, ("plane", "depth")),
        P("plane", "depth", None, None),
        P("plane", "depth", None),
        P("plane", "depth", None, None),
    )
    out_specs = (P(None, ("plane", "depth")), P(None, ("plane", "depth")))
    return jax.shard_map(
        on_device, mesh=mesh, in_specs=in_specs, out_specs=out_specs, check_vma=False
    )
```

profile of v0, /device:TPU:8, one launch (start us, length us, event | category | flops | bytes accessed | tf_op | source)
XLA Modules:
  0.0 365.6 jit_solution(13922247318034231117)
XLA Ops:
  0.6 1.1 copy.26
  1.8 0.7 fusion.29
  2.5 0.8 fusion.30
  3.3 5.5 %gather_fusion = f32[2048,64]{1,0:T(8,128)S(1)} fusion(f32[1024,64]{1,0:T(8,128)S(1)} %bitcast.85, s32[2048]{0:T(1024)S(1)} %broadcast_clamp_fusion.1), kind=kCustom, calls=%fused_computation | custom fusion | bytes 1056768 | tf_op jit(solution)/shard_map/jit(_take)/gather | solution.py:72
  8.8 0.0 copy-start.4
  8.8 0.7 select_multiply_fusion
  9.5 1.0 slice_bitcast_fusion
  10.5 1.3 collective-permute-start
  11.7 1.3 collective-permute-start.1
  13.0 5.3 %collective-permute-start.2 = (f32[512,64]{1,0:T(8,128)}, f32[512,64]{1,0:T(8,128)}, u32[]{:S(2)}, u32[]{:S(2)}) collective-permute-start(f32[512,64]{1,0:T(8,128)} %get-tuple-element.15), channel_id=1, source_target_pairs={{0,8},{8,16},{16,24},{24,32},{32,40},{40,48},{48,56},{56,64},{64,7... | collective-permute-start | bytes 393224 | tf_op jit(solution)/shard_map/ppermute | solution.py:17
  18.3 5.1 %collective-permute-start.3 = (f32[512,64]{1,0:T(8,128)}, f32[512,64]{1,0:T(8,128)S(1)}, u32[]{:S(2)}, u32[]{:S(2)}) collective-permute-start(f32[512,64]{1,0:T(8,128)} %get-tuple-element.14), channel_id=1, source_target_pairs={{0,16},{8,24},{16,32},{24,40},{32,48},{40,56},{48,64},{56,72},{64,... | collective-permute-start | bytes 393224 | tf_op jit(solution)/shard_map/ppermute | solution.py:17
  23.5 0.0 copy-start.1
  23.5 1.0 gather_fusion.1
  24.6 0.0 copy-start.3
  24.6 0.1 broadcast_select_fusion
  24.7 0.7 fusion.46
  25.4 1.9 collective-permute-start.4
  27.5 0.6 fusion.47
  28.2 0.1 broadcast_subtract_fusion
  28.3 0.1 copy.28
  28.4 0.5 multiply_reduce_fusion
  28.9 0.4 fusion.12
  29.3 0.3 fusion.25
  29.6 0.1 copy.38
  29.7 0.8 compare_select_fusion
  30.6 0.0 collective-permute-done
  30.6 3.6 collective-permute-start.5
  34.3 1.0 constant_dynamic-update-slice_fusion.3
  35.2 0.0 collective-permute-done.1
  35.2 1.0 constant_dynamic-update-slice_fusion.2
  36.2 0.0 collective-permute-done.2
  36.2 1.0 constant_dynamic-update-slice_fusion.1
  37.2 0.0 collective-permute-done.3
  37.2 0.0 collective-permute-done.4
  37.2 0.9 bitcast_dynamic-update-slice_fusion.3
  38.2 0.0 collective-permute-done.5
  38.2 91.5 %gather_fusion.2 = f32[27648,64]{1,0:T(8,128)} fusion(f32[3585,64]{1,0:T(8,128)S(1)} %dynamic-update-slice.19, s32[27648]{0:T(1024)S(1)} %broadcast_clamp_fusion), kind=kCustom, calls=%fused_computation.2 | custom fusion | bytes 14266368 | tf_op jit(solution)/shard_map/jit(_take)/gather | solution.py:50
  129.7 11.8 %copy.27 = f32[27,1024,64]{1,2,0:T(8,128)} copy(f32[27,1024,64]{2,1,0:T(8,128)} %bitcast.87) | data formatting | bytes 14155776 | tf_op jit(solution)/shard_map/jit(_take)/gather | solution.py:50
  141.5 8.4 %fusion.18 = (f32[64,1024]{1,0:T(8,128)}, f32[1024,64]{0,1:T(8,128)S(1)}) fusion(f32[1024,64]{0,1:T(8,128)S(1)} %fusion.25, f32[27,64,64]{2,1,0:T(8,128)S(1)} %multiply_reduce_fusion, f32[27,1024,64]{1,2,0:T(8,128)} %copy.27, pred[27,1024]{1,0:T(8,128)(4,1)S(1)} %compare_and_fusion), kind=kOutput, calls=%fused_computation.27 | convolution fusion | flops 1361272832 | bytes 8334336 | tf_op jit(solution)/shard_map/kbj,kij->bi/dot_general | solution.py:51
  149.8 0.0 copy-done.2
  149.8 7.8 %convolution_bitcast_fusion = f32[27,1024,64]{1,2,0:T(8,128)} fusion(f32[27,64,64]{2,1,0:T(8,128)S(1)} %multiply_reduce_fusion, f32[1024,64]{0,1:T(8,128)S(1)} %fusion.25, f32[1024,64]{0,1:T(8,128)S(1)} %get-tuple-element.25, f32[64,1024]{1,0:T(8,128)S(1)} %copy-done.2), kind=kOutput, calls=%fused_computation.9 | convolution fusion | flops 1359437824 | bytes 8306688 | tf_op jit(solution)/shard_map/bi,kij->kbj/dot_general | solution.py:55
  157.6 10.7 %copy.34 = f32[27,1024,64]{2,1,0:T(8,128)} copy(f32[27,1024,64]{1,2,0:T(8,128)} %convolution_bitcast_fusion) | data formatting | bytes 14155776 | tf_op jit(solution)/shard_map/reshape | solution.py:57
  168.3 147.7 %scatter_custom_fusion = f32[3585,64]{1,0:T(8,128)S(1)} fusion(s32[27648]{0:T(1024)} %bitcast.93, f32[27648,64]{1,0:T(8,128)} %bitcast.88, f32[]{:T(128)} %constant.125.clone.1), kind=kCustom, calls=%fused_computation.14 | custom fusion | flops 1769472 | bytes 918272 | tf_op jit(solution)/shard_map/scatter-add | solution.py:57
  316.0 0.1 fusion.45
  316.1 6.4 %collective-permute-start.6 = (f32[512,64]{1,0:T(8,128)S(1)}, f32[512,64]{1,0:T(8,128)S(1)}, u32[]{:S(2)}, u32[]{:S(2)}) collective-permute-start(f32[512,64]{1,0:T(8,128)S(1)} %get-tuple-element.13), channel_id=1, source_target_pairs={{0,16},{8,24},{16,32},{24,40},{32,48},{40,56},{48,64},{56,72},{64,... | collective-permute-start | bytes 393224 | tf_op jit(solution)/shard_map/ppermute | solution.py:17
  322.5 3.5 collective-permute-start.7
  326.0 1.3 collective-permute-start.8
  327.3 1.3 collective-permute-start.9
  328.6 1.9 collective-permute-start.10
  330.6 0.0 slice-start
  330.6 0.0 collective-permute-done.6
  330.6 3.7 %collective-permute-start.11 = (f32[1,256,64]{2,1,0:T(8,128)S(1)}, f32[1,256,64]{2,1,0:T(8,128)S(1)}, u32[]{:S(2)}, u32[]{:S(2)}) collective-permute-start(f32[1,256,64]{2,1,0:T(8,128)S(1)} %get-tuple-element.8), channel_id=1, source_target_pairs={{1,0},{2,1},{3,2},{4,3},{5,4},{6,5},{7,6},{9,8},{10,9},{11,10},{12... | collective-permute-start | bytes 196616 | tf_op jit(solution)/shard_map/ppermute | solution.py:28
  334.4 0.1 multiply_dynamic-update-slice_fusion.3
  334.5 5.6 %collective-permute-done.7 = f32[512,64]{1,0:T(8,128)S(1)} collective-permute-done((f32[512,64]{1,0:T(8,128)S(1)}, f32[512,64]{1,0:T(8,128)S(1)}, u32[]{:S(2)}, u32[]{:S(2)}) %collective-permute-start.7) | collective-permute-done | bytes 131104 | tf_op jit(solution)/shard_map/ppermute | solution.py:17
  340.1 0.0 copy-done.5
  340.1 0.1 multiply_dynamic-update-slice_fusion.2
  340.2 0.0 collective-permute-done.8
  340.2 0.1 multiply_dynamic-update-slice_fusion.1
  340.4 9.7 %collective-permute-done.9 = f32[512,64]{1,0:T(8,128)S(1)} collective-permute-done((f32[512,64]{1,0:T(8,128)S(1)}, f32[512,64]{1,0:T(8,128)S(1)}, u32[]{:S(2)}, u32[]{:S(2)}) %collective-permute-start.9) | collective-permute-done | bytes 131104 | tf_op jit(solution)/shard_map/ppermute | solution.py:17
  350.1 0.1 multiply_dynamic-update-slice_fusion
  350.2 0.0 collective-permute-done.10
  350.3 0.0 collective-permute-done.11
  350.3 14.4 %scatter_fusion = f32[1024,64]{1,0:T(8,128)S(1)} fusion(f32[1024,64]{1,0:T(8,128)S(1)} %slice-done, s32[2560]{0:T(1024)S(1)} %fusion.28, f32[2560,64]{1,0:T(8,128)S(1)} %bitcast_dynamic-update-slice_fusion), kind=kCustom, calls=%fused_computation.4 | custom fusion | flops 163840 | bytes 1976320 | tf_op jit(solution)/shard_map/scatter-add | solution.py:105
  364.7 0.9 copy.32
  (41 shorter events, 0.5 us)
Async XLA Ops:
  8.8 14.7 %copy-start.4 = (s32[1,1,2,256]{3,2,1,0:T(2,128)S(1)}, s32[1,1,2,256]{3,2,1,0:T(2,128)}, u32[]{:S(2)}) copy-start(s32[1,1,2,256]{3,2,1,0:T(2,128)} %param.11) | copy-start | bytes 6148
  10.5 20.1 %collective-permute-start = (f32[512,64]{1,0:T(8,128)}, f32[512,64]{1,0:T(8,128)}, u32[]{:S(2)}, u32[]{:S(2)}) collective-permute-start(f32[512,64]{1,0:T(8,128)} %get-tuple-element.17), channel_id=1, source_target_pairs={{16,0},{24,8},{32,16},{40,24},{48,32},{56,40},{64,48},{72,56},{80,... | collective-permute-start | bytes 393224 | tf_op jit(solution)/shard_map/ppermute | solution.py:17
  11.7 23.5 %collective-permute-start.1 = (f32[512,64]{1,0:T(8,128)}, f32[512,64]{1,0:T(8,128)}, u32[]{:S(2)}, u32[]{:S(2)}) collective-permute-start(f32[512,64]{1,0:T(8,128)} %get-tuple-element.16), channel_id=1, source_target_pairs={{8,0},{16,8},{24,16},{32,24},{40,32},{48,40},{56,48},{64,56},{72,6... | collective-permute-start | bytes 393224 | tf_op jit(solution)/shard_map/ppermute | solution.py:17
  13.0 23.2 %collective-permute-start.2 = (f32[512,64]{1,0:T(8,128)}, f32[512,64]{1,0:T(8,128)}, u32[]{:S(2)}, u32[]{:S(2)}) collective-permute-start(f32[512,64]{1,0:T(8,128)} %get-tuple-element.15), channel_id=1, source_target_pairs={{0,8},{8,16},{16,24},{24,32},{32,40},{40,48},{48,56},{56,64},{64,7... | collective-permute-start | bytes 393224 | tf_op jit(solution)/shard_map/ppermute | solution.py:17
  18.3 18.9 %collective-permute-start.3 = (f32[512,64]{1,0:T(8,128)}, f32[512,64]{1,0:T(8,128)S(1)}, u32[]{:S(2)}, u32[]{:S(2)}) collective-permute-start(f32[512,64]{1,0:T(8,128)} %get-tuple-element.14), channel_id=1, source_target_pairs={{0,16},{8,24},{16,32},{24,40},{32,48},{40,56},{48,64},{56,72},{64,... | collective-permute-start | bytes 393224 | tf_op jit(solution)/shard_map/ppermute | solution.py:17
  23.5 4.0 %copy-start.1 = (s32[27,1024]{1,0:T(8,128)S(1)}, s32[27,1024]{1,0:T(8,128)}, u32[]{:S(2)}) copy-start(s32[27,1024]{1,0:T(8,128)} %param.8) | copy-start | bytes 331780
  24.6 3.6 copy-start.3
  25.4 11.8 %collective-permute-start.4 = (f32[1,256,64]{2,1,0:T(8,128)}, f32[1,256,64]{2,1,0:T(8,128)}, u32[]{:S(2)}, u32[]{:S(2)}) collective-permute-start(f32[1,256,64]{2,1,0:T(8,128)} %get-tuple-element.19), channel_id=1, source_target_pairs={{0,1},{1,2},{2,3},{3,4},{4,5},{5,6},{6,7},{8,9},{9,10},{10,11},{11... | collective-permute-start | bytes 196616 | tf_op jit(solution)/shard_map/ppermute | solution.py:27
  30.6 7.6 %collective-permute-start.5 = (f32[1,256,64]{2,1,0:T(8,128)}, f32[1,256,64]{2,1,0:T(8,128)S(1)}, u32[]{:S(2)}, u32[]{:S(2)}) collective-permute-start(f32[1,256,64]{2,1,0:T(8,128)} %get-tuple-element.18), channel_id=1, source_target_pairs={{1,0},{2,1},{3,2},{4,3},{5,4},{6,5},{7,6},{9,8},{10,9},{11,10},{12... | collective-permute-start | bytes 196616 | tf_op jit(solution)/shard_map/ppermute | solution.py:28
  141.4 8.4 %copy-start.2 = (f32[64,1024]{1,0:T(8,128)S(1)}, f32[64,1024]{1,0:T(8,128)}, u32[]{:S(2)}) copy-start(f32[64,1024]{1,0:T(8,128)} %param.7) | copy-start | bytes 786436
  316.0 12.6 %copy-start = (f32[3585,64]{1,0:T(8,128)}, f32[3585,64]{1,0:T(8,128)S(1)}, u32[]{:S(2)}) copy-start(f32[3585,64]{1,0:T(8,128)S(1)} %scatter_custom_fusion) | copy-start | bytes 2753284
  316.0 18.4 %copy-start.6 = (f32[1,512]{1,0:T(1,128)S(1)}, f32[1,512]{1,0:T(1,128)}, u32[]{:S(2)}) copy-start(f32[1,512]{1,0:T(1,128)} %get-tuple-element.23) | copy-start | bytes 6148
  316.0 24.1 %copy-start.5 = (f32[1,512]{1,0:T(1,128)S(1)}, f32[1,512]{1,0:T(1,128)}, u32[]{:S(2)}) copy-start(f32[1,512]{1,0:T(1,128)} %get-tuple-element.22) | copy-start | bytes 6148
  316.1 14.5 %collective-permute-start.6 = (f32[512,64]{1,0:T(8,128)S(1)}, f32[512,64]{1,0:T(8,128)S(1)}, u32[]{:S(2)}, u32[]{:S(2)}) collective-permute-start(f32[512,64]{1,0:T(8,128)S(1)} %get-tuple-element.13), channel_id=1, source_target_pairs={{0,16},{8,24},{16,32},{24,40},{32,48},{40,56},{48,64},{56,72},{64,... | collective-permute-start | bytes 393224 | tf_op jit(solution)/shard_map/ppermute | solution.py:17
  322.5 17.6 %collective-permute-start.7 = (f32[512,64]{1,0:T(8,128)S(1)}, f32[512,64]{1,0:T(8,128)S(1)}, u32[]{:S(2)}, u32[]{:S(2)}) collective-permute-start(f32[512,64]{1,0:T(8,128)S(1)} %get-tuple-element.12), channel_id=1, source_target_pairs={{0,8},{8,16},{16,24},{24,32},{32,40},{40,48},{48,56},{56,64},{64,7... | collective-permute-start | bytes 393224 | tf_op jit(solution)/shard_map/ppermute | solution.py:17
  326.0 14.2 %collective-permute-start.8 = (f32[512,64]{1,0:T(8,128)S(1)}, f32[512,64]{1,0:T(8,128)S(1)}, u32[]{:S(2)}, u32[]{:S(2)}) collective-permute-start(f32[512,64]{1,0:T(8,128)S(1)} %get-tuple-element.11), channel_id=1, source_target_pairs={{8,0},{16,8},{24,16},{32,24},{40,32},{48,40},{56,48},{64,56},{72,6... | collective-permute-start | bytes 393224 | tf_op jit(solution)/shard_map/ppermute | solution.py:17
  327.3 22.8 %collective-permute-start.9 = (f32[512,64]{1,0:T(8,128)S(1)}, f32[512,64]{1,0:T(8,128)S(1)}, u32[]{:S(2)}, u32[]{:S(2)}) collective-permute-start(f32[512,64]{1,0:T(8,128)S(1)} %get-tuple-element.10), channel_id=1, source_target_pairs={{16,0},{24,8},{32,16},{40,24},{48,32},{56,40},{64,48},{72,56},{80,... | collective-permute-start | bytes 393224 | tf_op jit(solution)/shard_map/ppermute | solution.py:17
  328.6 21.6 %collective-permute-start.10 = (f32[1,256,64]{2,1,0:T(8,128)S(1)}, f32[1,256,64]{2,1,0:T(8,128)S(1)}, u32[]{:S(2)}, u32[]{:S(2)}) collective-permute-start(f32[1,256,64]{2,1,0:T(8,128)S(1)} %get-tuple-element.9), channel_id=1, source_target_pairs={{0,1},{1,2},{2,3},{3,4},{4,5},{5,6},{6,7},{8,9},{9,10},{10,11},{11... | collective-permute-start | bytes 196616 | tf_op jit(solution)/shard_map/ppermute | solution.py:27
  330.6 19.7 %slice-start = ((f32[3585,64]{1,0:T(8,128)}), f32[1024,64]{1,0:T(8,128)S(1)}, s32[]{:S(2)}) async-start(f32[3585,64]{1,0:T(8,128)} %copy-done), calls=%async_computation | async-start | bytes 1048576 | tf_op jit(solution)/shard_map/slice | solution.py:83
  330.6 19.7 %collective-permute-start.11 = (f32[1,256,64]{2,1,0:T(8,128)S(1)}, f32[1,256,64]{2,1,0:T(8,128)S(1)}, u32[]{:S(2)}, u32[]{:S(2)}) collective-permute-start(f32[1,256,64]{2,1,0:T(8,128)S(1)} %get-tuple-element.8), channel_id=1, source_target_pairs={{1,0},{2,1},{3,2},{4,3},{5,4},{6,5},{7,6},{9,8},{10,9},{11,10},{12... | collective-permute-start | bytes 196616 | tf_op jit(solution)/shard_map/ppermute | solution.py:28
where the time goes:
time: 367 us; the launch traced here: 366 us
  other arithmetic  167 us (46%)
  local copies, waits for them, and re-layouts  129 us (35%)
  starting transfers between devices  36.7 us (10%)
  matrix products  16.4 us (4%)
  waiting for transfers between devices  15.3 us (4%)
    scatter-add x1, other arithmetic, local_rows(): jnp.zeros((width, 64), jnp.float32).at[link_table.reshape(-1)]  148 us
    gather x2, local copies, waits for them, and re-layouts, local_rows(): picked = jnp.take(ext_rows, link_table, axis=0)  103 us
    ppermute x8, starting transfers between devices, passed_along(): return lax.ppermute(shard, axis, pairs)  25.4 us
    ppermute x8, waiting for transfers between devices, passed_along(): return lax.ppermute(shard, axis, pairs)  15.3 us
    scatter-add x1, other arithmetic, on_device(): sens = sens.at[jnp.concatenate(places)].add(jnp.concatenate(values, axis=0))  14.4 us
    reshape x1, local copies, waits for them, and re-layouts, local_rows(): spread.reshape(-1, 64)  10.7 us
    dot_general x1, matrix products, local_rows(): jnp.einsum('kbj,kij->bi', picked, table, precision=lax.Precision.HIGHEST)  8.38 us
    dot_general x1, matrix products, local_rows(): jnp.einsum('bi,kij->kbj', scaled, table, precision=lax.Precision.HIGHEST)  7.75 us
  transfers between devices with their start and end apart: 12, of which 2 were waited for; matrix products, arithmetic and copies ran while one was open for 3% of the time, Pallas kernels for 0%

commit v1 on v0

v1 whole, which is shorter than its diff:
```python
import jax
import jax.numpy as jnp
import numpy as np
from jax import lax
from jax.experimental import pallas as pl
from jax.experimental.pallas import tpu as pltpu
from jax.sharding import PartitionSpec as P

REACH = 2
TILE = 256
radius = 3.0
floor_value = 0.001
penalty = 3.0

F32 = jnp.float32
BF16 = jnp.bfloat16

ORDERS = ((0, 1, 2), (2, 0, 1), (1, 2, 0))


def cone_table():
    voxels = np.arange(64)
    places = np.stack([voxels // 16, voxels // 4 % 4, voxels % 4], axis=-1)
    slots = np.arange(27)
    moved = np.stack([slots // 9 - 1, slots // 3 % 3 - 1, slots % 3 - 1], axis=-1) * 4
    apart = places[None, :, None, :] - places[None, None, :, :] - moved[:, None, None, :]
    squares = np.sum(apart * apart, axis=-1).astype(np.float32)
    return np.maximum(np.float32(0.0), np.float32(radius) - np.sqrt(squares))


def order_voxels(order):
    rows = np.arange(64)
    coords = np.zeros((3, 64), np.int64)
    coords[order[0]], coords[order[1]], coords[order[2]] = rows // 16, rows // 4 % 4, rows % 4
    return coords[0] * 16 + coords[1] * 4 + coords[2]


def slot_of(offset):
    return (offset[0] + 1) * 9 + (offset[1] + 1) * 3 + offset[2] + 1


def layout():
    faces, edges, corners = [], [], []
    for at, order in enumerate(ORDERS):
        for sign in (-1, 1):
            offset = [0, 0, 0]
            offset[order[0]] = sign
            faces.append((slot_of(offset), at, sign))
    for at, order in enumerate(ORDERS):
        for one in (-1, 1):
            for two in (-1, 1):
                offset = [0, 0, 0]
                offset[order[0]], offset[order[1]] = one, two
                edges.append((slot_of(offset), at, one, two))
    for a in (-1, 1):
        for b in (-1, 1):
            for c in (-1, 1):
                corners.append(slot_of((a, b, c)))
    return faces, edges, corners


FACES, EDGES, CORNERS = layout()
SLOTS = [f[0] for f in FACES] + [e[0] for e in EDGES] + CORNERS


def face_start(sign, forward):
    return 32 if (sign > 0) == forward else 0


def edge_starts(one, two, forward):
    first = 2 if (one > 0) == forward else 0
    second = 2 if (two > 0) == forward else 0
    return [(first + i) * 16 + second * 4 for i in range(2)]


def slot_rows(forward):
    voxels = [order_voxels(order) for order in ORDERS]
    out = []
    for slot, at, sign in FACES:
        start = face_start(sign, forward)
        out.append((slot, voxels[at][start : start + 32]))
    for slot, at, one, two in EDGES:
        rows = np.concatenate([voxels[at][s : s + 8] for s in edge_starts(one, two, forward)])
        out.append((slot, rows))
    return out


def pieces_np(table):
    high = table.astype(jnp.bfloat16)
    low = (table - high.astype(np.float32)).astype(jnp.bfloat16)
    return high, low


def three(table):
    high, low = pieces_np(table)
    return np.concatenate([high, low, high], axis=1)


def corner_rows(table, forward):
    out = []
    for slot in CORNERS:
        part = table[slot] if forward else table[slot].T
        counts = (part > 0).sum(axis=1)
        main = int(np.argmax(counts))
        rest = [int(v) for v in np.nonzero(counts)[0] if v != main]
        out.append((part, main, rest))
    return out


def constants():
    table = cone_table()
    fold_fwd = [table[slot][rows] for slot, rows in slot_rows(True)]
    fold_bwd = [table[slot].T[rows] for slot, rows in slot_rows(False)]
    cor_fwd, cor_bwd = corner_rows(table, True), corner_rows(table, False)
    fold_fwd += [np.stack([part[main] for part, main, rest in cor_fwd])]
    fold_fwd += [np.stack([part[rest[0]] for part, main, rest in cor_fwd])]
    for part, main, rest in cor_bwd:
        fold_bwd += [np.tile(np.stack([part[main], part[rest[0]]]), (8, 1))]
    spots = []
    for at in (1, 2):
        spot = np.zeros((64, 64), np.float32)
        spot[order_voxels(ORDERS[at]), np.arange(64)] = 1
        spots.append(spot)
    cf = np.zeros((64, 16), np.float32)
    for m, (part, main, rest) in enumerate(cor_fwd):
        cf[main, m] = 1
        cf[rest, 8 + m] = 1
    join_fwd = np.concatenate(spots + [cf], axis=1)
    join_fwd = np.concatenate([join_fwd, join_fwd], axis=1).astype(jnp.bfloat16)
    joins = []
    for parity in range(2):
        cb = np.zeros((64, 64), np.float32)
        for m, (part, main, rest) in enumerate(cor_bwd):
            for piece in range(2):
                cb[main, m * 8 + parity * 4 + piece * 2] = 1
                cb[rest, m * 8 + parity * 4 + piece * 2 + 1] = 1
        join = np.concatenate(spots + [cb], axis=1)
        joins.append(np.concatenate([join, join], axis=1))
    sums = table.sum(axis=2).T
    high, low = pieces_np(sums)
    return dict(
        fold_fwd=three(np.concatenate(fold_fwd)),
        fold_bwd=three(np.concatenate(fold_bwd)),
        own=three(table[13]),
        own_t=three(table[13].T),
        join_fwd=join_fwd,
        join_bwd=np.concatenate(joins).astype(jnp.bfloat16),
        sums=np.concatenate([high, low], axis=1),
    )


def split2(value):
    high = value.astype(BF16)
    return high, (value - high.astype(F32)).astype(BF16)


def pieces(value):
    high, low = split2(value)
    return jnp.concatenate([high, high, low], axis=0)


def dot(a, b):
    return jnp.dot(a, b, preferred_element_type=F32)


def dot_nt(a, b):
    return lax.dot_general(a, b, (((1,), (1,)), ((), ())), preferred_element_type=F32)


def one_hot(low):
    shape = (TILE, low.shape[1])
    hit = lax.broadcasted_iota(jnp.int32, shape, 0) == jnp.broadcast_to(low, shape)
    return hit.astype(F32).astype(BF16)


def order_links(links_ref, rows_ref):
    for at, slot in enumerate(SLOTS):
        rows_ref[at : at + 1, :] = links_ref[slot : slot + 1, :]


def gather_filtered(chunks, first, rows_ref, fold_ref, join_ref, tf, te, yc, pf, pe):
    count = len(chunks)
    faces, edges = len(FACES), len(EDGES)
    blocks = rows_ref.shape[1]
    for h, chunk in enumerate(chunks):
        y = dot(fold_ref[...], pieces(chunk))
        high, low = split2(y[:384])
        for f in range(faces):
            tf[f, h * 32 : h * 32 + 32, 0:TILE] = high[f * 32 : f * 32 + 32]
            tf[f, h * 32 : h * 32 + 32, TILE : 2 * TILE] = low[f * 32 : f * 32 + 32]
        for e in range(edges):
            at = 192 + e * 16
            te[e, h * 16 : h * 16 + 16, 0:TILE] = high[at : at + 16]
            te[e, h * 16 : h * 16 + 16, TILE : 2 * TILE] = low[at : at + 16]
        yc[:, h * TILE : h * TILE + TILE] = y[384:400]

    def make(table, out, rows, base):
        def step(s, carry):
            for nb in range(blocks // TILE):
                cols = slice(nb * TILE, nb * TILE + TILE)
                idx = rows_ref[pl.ds(base + s, 1), cols]
                hot = one_hot(idx & (TILE - 1))
                upper = jnp.broadcast_to((idx >> 8) - first, (rows, TILE))
                got = dot(table[s, :, 0:TILE], hot) + dot(table[s, :, TILE : 2 * TILE], hot)
                acc = jnp.zeros((rows, TILE), F32)
                for h in range(count):
                    acc = jnp.where(upper == h, got[h * rows : h * rows + rows], acc)
                out[s, :, cols] = acc
            return carry

        return step

    lax.fori_loop(0, faces, make(tf, pf, 32, 0), 0)
    lax.fori_loop(0, edges, make(te, pe, 16, faces), 0)
    corner = [[], []]
    for bg in range(blocks // 128):
        idx = rows_ref[18:26, bg * 128 : bg * 128 + 128]
        low, upper = idx & 127, (idx >> 7) - 2 * first
        acc = [jnp.zeros((8, 128), F32), jnp.zeros((8, 128), F32)]
        for h in range(2 * count):
            hit = upper == h
            for c in range(2):
                got = jnp.take_along_axis(yc[c * 8 : c * 8 + 8, h * 128 : h * 128 + 128], low, axis=1)
                acc[c] = jnp.where(hit, got, acc[c])
        for c in range(2):
            corner[c].append(acc[c])
    corner = [jnp.concatenate(c, axis=1) for c in corner]
    totals = order_totals(lambda f: pf[f], lambda e: pe[e], True)
    high, low = split2(jnp.concatenate([totals[1], totals[2]] + corner, axis=0))
    return totals[0] + dot(join_ref[...], jnp.concatenate([high, low], axis=0))


def order_totals(face, edge, forward):
    totals = []
    for at in range(3):
        runs = [None] * 8
        for f, (_, order, sign) in enumerate(FACES):
            if order == at:
                value, start = face(f), face_start(sign, forward)
                for i in range(4):
                    runs[start // 8 + i] = value[i * 8 : i * 8 + 8]
        for e, (_, order, one, two) in enumerate(EDGES):
            if order == at:
                value = edge(e)
                for i, start in enumerate(edge_starts(one, two, forward)):
                    runs[start // 8] = runs[start // 8] + value[i * 8 : i * 8 + 8]
        totals.append(jnp.concatenate(runs, axis=0))
    return totals


def scatter_back(scaled, first, count, rows_ref, fold_ref, join_ref, sf, se, sc, zf, ze, zc):
    faces, edges, corners = len(FACES), len(EDGES), len(CORNERS)
    blocks = rows_ref.shape[1]
    spread = dot(fold_ref[...], pieces(scaled))
    high, low = split2(spread)
    for f in range(faces):
        sf[f, 0:32, :] = high[f * 32 : f * 32 + 32]
        sf[f, 32:64, :] = low[f * 32 : f * 32 + 32]
    for e in range(edges):
        at = 192 + e * 16
        se[e, 0:16, :] = high[at : at + 16]
        se[e, 16:32, :] = low[at : at + 16]
    is_high = lax.broadcasted_iota(jnp.int32, (16, blocks), 0) % 4 < 2
    for m in range(corners):
        part = spread[384 + m * 16 : 384 + m * 16 + 16]
        top = part.astype(BF16).astype(F32)
        sc[m, :, :] = jnp.where(is_high, top, part - top).astype(BF16)

    def make(values, out, rows, base):
        def step(s, carry):
            idx = rows_ref[pl.ds(base + s, 1), :]
            hot = one_hot(idx & (TILE - 1))
            upper = (idx >> 8) - first
            value = values[s]
            parts = [value * (upper == h).astype(F32).astype(BF16) for h in range(count)]
            got = dot_nt(jnp.concatenate(parts, axis=0), hot)
            for h in range(count):
                at = h * 2 * rows
                out[s, h * rows : h * rows + rows, :] = got[at : at + rows] + got[at + rows : at + 2 * rows]
            return carry

        return step

    lax.fori_loop(0, faces, make(sf, zf, 32, 0), 0)
    lax.fori_loop(0, edges, make(se, ze, 16, faces), 0)
    fours = (count + 3) // 4

    def corner_step(m, carry):
        idx = rows_ref[pl.ds(18 + m, 1), :]
        hot = one_hot(idx & (TILE - 1))
        upper = jnp.broadcast_to((idx >> 8) - first, (16, blocks))
        quarter = lax.broadcasted_iota(jnp.int32, (16, blocks), 0) // 4
        value = sc[m]
        parts = [
            value * (upper == quarter + 4 * q).astype(F32).astype(BF16) for q in range(fours)
        ]
        zc[m, :, :] = dot_nt(jnp.concatenate(parts, axis=0), hot)
        return carry

    lax.fori_loop(0, corners, corner_step, 0)
    out = []
    for h in range(count):
        totals = order_totals(
            lambda f: zf[f, h * 32 : h * 32 + 32, :], lambda e: ze[e, h * 16 : h * 16 + 16, :], False
        )
        at = h // 2 * 8
        tops = [zc[m, at : at + 8, :] for m in range(corners)]
        high, low = split2(jnp.concatenate([totals[1], totals[2]] + tops, axis=0))
        join = join_ref[h % 2 * 64 : h % 2 * 64 + 64, :]
        out.append(totals[0] + dot(join, jnp.concatenate([high, low], axis=0)))
    return out


def payload_kernel(live_ref, density_ref, index_ref, face_ref, *outs):
    density = density_ref[...]
    high, low = split2(density)
    heads = density.shape[1] // TILE
    table = jnp.concatenate(
        [
            jnp.concatenate([p[:, h * TILE : h * TILE + TILE] for h in range(heads)], axis=0)
            for p in (high, low)
        ],
        axis=1,
    )

    def pick(idx, upper):
        hot = one_hot(idx & (TILE - 1))
        got = dot(table[:, 0:TILE], hot) + dot(table[:, TILE : 2 * TILE], hot)
        upper = jnp.broadcast_to(upper, (64, idx.shape[1]))
        acc = jnp.zeros((64, idx.shape[1]), F32)
        for h in range(heads):
            acc = jnp.where(upper == h, got[h * 64 : h * 64 + 64], acc)
        return acc

    groups = index_ref.shape[0]
    for g in range(groups):
        idx = index_ref[g : g + 1, :]
        at = lax.broadcasted_iota(jnp.int32, idx.shape, 1)
        outs[g][...] = pick(idx, jnp.where(at < live_ref[g], idx >> 8, -1))
    for side in range(2):
        idx = face_ref[side : side + 1, :]
        outs[groups + side][...] = pick(idx, idx >> 8)


def local_kernel(
    density_ref, links_ref, fold_ref, join_ref, own_ref, sums_ref, part_ref, weight_ref, rows_ref, *scratch
):
    order_links(links_ref, rows_ref)
    density = density_ref[...]
    heads = density.shape[1] // TILE
    chunks = [density[:, h * TILE : h * TILE + TILE] for h in range(heads)]
    part = gather_filtered(chunks, 0, rows_ref, fold_ref, join_ref, *scratch)
    part_ref[...] = part + dot(own_ref[...], pieces(density))
    valid = (links_ref[...] != 14 * TILE).astype(F32).astype(BF16)
    weight_ref[...] = dot(sums_ref[...], jnp.concatenate([valid, valid], axis=0))


def remote_kernel(
    r0, r1, r2, r3, low_ref, high_ref, links_ref, part_ref, weight_ref, energy_ref,
    fold_ref, join_ref, fold_b_ref, join_b_ref,
    cond_ref, scaled_ref, b0, b1, b2, b3, lb, ub, rows_ref, *scratch,
):
    order_links(links_ref, rows_ref)
    chunks = []
    for ref in (r0, r1, r2, r3, low_ref, high_ref):
        for at in range(0, ref.shape[1], TILE):
            chunks.append(ref[:, at : at + TILE])
    total = gather_filtered(chunks, 4, rows_ref, fold_ref, join_ref, *scratch[:5])
    weight = weight_ref[...]
    filtered = (part_ref[...] + total) / weight
    square = filtered * filtered
    cond_ref[...] = floor_value + square * filtered * (1.0 - floor_value)
    scaled = -penalty * (1.0 - floor_value) * square * energy_ref[...] / weight
    scaled_ref[...] = scaled
    back = scatter_back(scaled, 4, len(chunks), rows_ref, fold_b_ref, join_b_ref, *scratch[5:])
    at = 0
    for ref in (b0, b1, b2, b3, lb, ub):
        for start in range(0, ref.shape[1], TILE):
            ref[:, start : start + TILE] = back[at]
            at += 1


def own_kernel(scaled_ref, links_ref, fold_b_ref, join_b_ref, own_ref, sens_ref, rows_ref, *scratch):
    order_links(links_ref, rows_ref)
    scaled = scaled_ref[...]
    heads = scaled.shape[1] // TILE
    back = scatter_back(scaled, 0, heads, rows_ref, fold_b_ref, join_b_ref, *scratch)
    sens_ref[...] = jnp.concatenate(back, axis=1) + dot(own_ref[...], pieces(scaled))


def final_kernel(live_ref, sens_ref, index_ref, face_ref, v0, v1, v2, v3, v4, v5, out_ref):
    heads = sens_ref.shape[1] // TILE
    groups = index_ref.shape[0]
    total = jnp.zeros((heads * 128, TILE), F32)
    for g, ref in enumerate((v0, v1, v2, v3, v4, v5)):
        if g < groups:
            idx = index_ref[g : g + 1, :]
            at = lax.broadcasted_iota(jnp.int32, idx.shape, 1)
            upper = jnp.where(at < live_ref[g], idx >> 8, -1)
        else:
            idx = face_ref[g - groups : g - groups + 1, :]
            upper = idx >> 8
        hot = one_hot(idx & (TILE - 1))
        value = jnp.concatenate(split2(ref[...]), axis=0)
        parts = [value * (upper == h).astype(F32).astype(BF16) for h in range(heads)]
        total = total + dot_nt(jnp.concatenate(parts, axis=0), hot)
    for h in range(heads):
        cols = slice(h * TILE, h * TILE + TILE)
        both = total[h * 128 : h * 128 + 64] + total[h * 128 + 64 : h * 128 + 128]
        out_ref[:, cols] = sens_ref[:, cols] + both


def params():
    return pltpu.CompilerParams(vmem_limit_bytes=48 * 1024 * 1024)


def cost(us):
    return pl.CostEstimate(flops=int(us * 5e8), bytes_accessed=int(us * 2e6), transcendentals=0)


def gather_scratch(count, blocks):
    return [
        pltpu.VMEM((6, count * 32, 2 * TILE), BF16),
        pltpu.VMEM((12, count * 16, 2 * TILE), BF16),
        pltpu.VMEM((16, count * TILE), F32),
        pltpu.VMEM((6, 32, blocks), F32),
        pltpu.VMEM((12, 16, blocks), F32),
    ]


def scatter_scratch(count, blocks):
    return [
        pltpu.VMEM((6, 64, blocks), BF16),
        pltpu.VMEM((12, 32, blocks), BF16),
        pltpu.VMEM((8, 16, blocks), BF16),
        pltpu.VMEM((6, count * 32, TILE), F32),
        pltpu.VMEM((12, count * 16, TILE), F32),
        pltpu.VMEM((8, (count + 3) // 4 * 16, TILE), F32),
    ]


def passed_along(shard, axis, by):
    count = lax.axis_size(axis)
    pairs = [(i, i + by) for i in range(count) if 0 <= i + by < count]
    return lax.ppermute(shard, axis, pairs)


def on_device(density, energy, links, send_index, send_live, face_index):
    const = {name: jnp.asarray(value) for name, value in constants().items()}
    blocks = density.shape[1]
    indices, counts, faces_at = send_index[0, 0], send_live[0, 0], face_index[0, 0]
    capacity, face_count = indices.shape[1], faces_at.shape[1]
    whole = jax.ShapeDtypeStruct((64, blocks), F32)
    listed = jax.ShapeDtypeStruct((64, capacity), F32)
    faced = jax.ShapeDtypeStruct((64, face_count), F32)
    vmem = pl.BlockSpec(memory_space=pltpu.VMEM)
    smem = pl.BlockSpec(memory_space=pltpu.SMEM)
    ordered = pltpu.VMEM((32, blocks), jnp.int32)
    offsets = [offset for offset in range(-REACH, REACH + 1) if offset != 0]

    loads = pl.pallas_call(
        payload_kernel,
        out_shape=[listed] * 4 + [faced] * 2,
        in_specs=[smem, vmem, vmem, vmem],
        out_specs=[vmem] * 6,
        compiler_params=params(),
        cost_estimate=cost(3),
    )(counts, density, indices, faces_at)
    received = [passed_along(loads[m], "plane", offset) for m, offset in enumerate(offsets)]
    from_low = passed_along(loads[5], "depth", 1)
    from_high = passed_along(loads[4], "depth", -1)
    part, weight = pl.pallas_call(
        local_kernel,
        out_shape=[whole, whole],
        in_specs=[vmem] * 6,
        out_specs=[vmem] * 2,
        scratch_shapes=[ordered] + gather_scratch(4, blocks),
        compiler_params=params(),
        cost_estimate=cost(8),
    )(density, links, const["fold_fwd"], const["join_fwd"], const["own"], const["sums"])
    conductivity, scaled, *groups_back = pl.pallas_call(
        remote_kernel,
        out_shape=[whole, whole] + [listed] * 4 + [faced] * 2,
        in_specs=[vmem] * 14,
        out_specs=[vmem] * 8,
        scratch_shapes=[ordered] + gather_scratch(10, blocks) + scatter_scratch(10, blocks),
        compiler_params=params(),
        cost_estimate=cost(20),
    )(
        *received, from_low, from_high, links, part, weight, energy,
        const["fold_fwd"], const["join_fwd"], const["fold_bwd"], const["join_bwd"],
    )
    returned = [passed_along(groups_back[m], "plane", -offset) for m, offset in enumerate(offsets)]
    to_one = passed_along(groups_back[4], "depth", -1)
    to_zero = passed_along(groups_back[5], "depth", 1)
    sens = pl.pallas_call(
        own_kernel,
        out_shape=whole,
        in_specs=[vmem] * 5,
        out_specs=vmem,
        scratch_shapes=[ordered] + scatter_scratch(4, blocks),
        compiler_params=params(),
        cost_estimate=cost(8),
    )(scaled, links, const["fold_bwd"], const["join_bwd"], const["own_t"])
    sens = pl.pallas_call(
        final_kernel,
        out_shape=whole,
        in_specs=[smem] + [vmem] * 9,
        out_specs=vmem,
        compiler_params=params(),
        cost_estimate=cost(3),
    )(counts, sens, indices, faces_at, *returned, to_zero, to_one)
    return (conductivity, sens)


def solution(mesh):
    in_specs = (
        P(None, ("plane", "depth")),
        P(None, ("plane", "depth")),
        P(None, ("plane", "depth")),
        P("plane", "depth", None, None),
        P("plane", "depth", None),
        P("plane", "depth", None, None),
    )
    out_specs = (P(None, ("plane", "depth")), P(None, ("plane", "depth")))
    return jax.shard_map(
        on_device, mesh=mesh, in_specs=in_specs, out_specs=out_specs, check_vma=False
    )
```

time: 367 us -> 91.3 us (0.25)
  the two profiles are of different devices: /device:TPU:8 before, /device:TPU:14 now
where the time goes in v1:
time: 91.3 us; the launch traced here: 90.8 us
  Pallas kernels  42.7 us (47%)
  starting transfers between devices  42.6 us (47%)
  local copies, waits for them, and re-layouts  2.37 us (3%)
  waiting for transfers between devices  2.16 us (2%)
  between operations  0.96 us (1%)
    ppermute x12, starting transfers between devices, passed_along(): return lax.ppermute(shard, axis, pairs)  42.6 us
    pallas_call x1, Pallas kernels, on_device(): pl.pallas_call(remote_kernel, out_shape=[whole, whole] + [listed] * 4 + [...  22.3 us
    pallas_call x1, Pallas kernels, on_device(): pl.pallas_call(own_kernel, out_shape=whole, in_specs=[vmem] * 5, out_spec...  9.04 us
    pallas_call x1, Pallas kernels, on_device(): pl.pallas_call(local_kernel, out_shape=[whole, whole], in_specs=[vmem] *...  7.62 us
    unnamed x28, local copies, waits for them, and re-layouts  2.37 us
    ppermute x12, waiting for transfers between devices, passed_along(): return lax.ppermute(shard, axis, pairs)  2.16 us
    pallas_call x1, Pallas kernels, on_device(): pl.pallas_call(final_kernel, out_shape=whole, in_specs=[smem] + [vmem] *...  2.14 us
  transfers between devices with their start and end apart: 12, of which 1 were waited for; matrix products, arithmetic and copies ran while one was open for 0% of the time, Pallas kernels for 18%

profile of v1, /device:TPU:14, one launch (start us, length us, event | category | flops | bytes accessed | tf_op | source)
XLA Modules:
  0.0 90.8 jit_solution(11915555249449388082)
XLA Ops:
  0.6 0.0 copy-start.6
  0.6 0.0 copy-start.7
  0.7 0.7 copy-done.6
  1.3 0.0 copy-done.7
  1.3 0.0 copy-start
  1.3 0.9 %copy-done = f32[64,1024]{1,0:T(8,128)S(1)} copy-done((f32[64,1024]{1,0:T(8,128)S(1)}, f32[64,1024]{1,0:T(8,128)}, u32[]{:S(2)}) %copy-start) | copy-done | bytes 262168
  2.3 0.0 copy-start.4
  2.3 0.7 copy-done.4
  3.0 0.0 copy-start.1
  3.0 0.0 copy-start.3
  3.0 0.0 copy-start.9
  3.0 0.0 copy-start.11
  3.0 0.0 copy-start.12
  3.0 0.0 copy-start.13
  3.0 1.6 %shard_map.140 = (f32[64,512]{1,0:T(8,128)S(1)}, f32[64,512]{1,0:T(8,128)S(1)}, f32[64,512]{1,0:T(8,128)S(1)}, f32[64,512]{1,0:T(8,128)S(1)}, f32[64,256]{1,0:T(8,128)S(1)}, /*index=5*/f32[64,256]{1,0:T(8,128)S(1)}) custom-call(s32[4]{0:T(128)S(1)} %bitcast.7, f32[64,1024]{1,0:T(8,128)S(1)} %copy-done, s32[4,512]{1,0:T(4,128)S(1)} %bitcast.3, ...), custom_call_target="tpu_custom_call" | custom-call | flops 1500000000 | bytes 6000000 | tf_op jit(solution)/shard_map/pallas_call | solution.py:461
  4.6 1.9 %collective-permute-start.4 = (f32[64,256]{1,0:T(8,128)S(1)}, f32[64,256]{1,0:T(8,128)S(1)}, u32[]{:S(2)}, u32[]{:S(2)}) collective-permute-start(f32[64,256]{1,0:T(8,128)S(1)} %get-tuple-element.22), channel_id=1, source_target_pairs={{0,1},{1,2},{2,3},{3,4},{4,5},{5,6},{6,7},{8,9},{9,10},{10,11},{11... | collective-permute-start | bytes 196616 | tf_op jit(solution)/shard_map/ppermute | solution.py:445
  6.5 3.6 %collective-permute-start.5 = (f32[64,256]{1,0:T(8,128)S(1)}, f32[64,256]{1,0:T(8,128)S(1)}, u32[]{:S(2)}, u32[]{:S(2)}) collective-permute-start(f32[64,256]{1,0:T(8,128)S(1)} %get-tuple-element.23), channel_id=1, source_target_pairs={{1,0},{2,1},{3,2},{4,3},{5,4},{6,5},{7,6},{9,8},{10,9},{11,10},{12... | collective-permute-start | bytes 196616 | tf_op jit(solution)/shard_map/ppermute | solution.py:445
  10.2 8.5 %collective-permute-start = (f32[64,512]{1,0:T(8,128)S(1)}, f32[64,512]{1,0:T(8,128)S(1)}, u32[]{:S(2)}, u32[]{:S(2)}) collective-permute-start(f32[64,512]{1,0:T(8,128)S(1)} %get-tuple-element.18), channel_id=1, source_target_pairs={{16,0},{24,8},{32,16},{40,24},{48,32},{56,40},{64,48},{72,56},{80,... | collective-permute-start | bytes 393224 | tf_op jit(solution)/shard_map/ppermute | solution.py:445
  18.7 2.9 %collective-permute-start.1 = (f32[64,512]{1,0:T(8,128)S(1)}, f32[64,512]{1,0:T(8,128)S(1)}, u32[]{:S(2)}, u32[]{:S(2)}) collective-permute-start(f32[64,512]{1,0:T(8,128)S(1)} %get-tuple-element.19), channel_id=1, source_target_pairs={{8,0},{16,8},{24,16},{32,24},{40,32},{48,40},{56,48},{64,56},{72,6... | collective-permute-start | bytes 393224 | tf_op jit(solution)/shard_map/ppermute | solution.py:445
  21.6 2.9 %collective-permute-start.2 = (f32[64,512]{1,0:T(8,128)S(1)}, f32[64,512]{1,0:T(8,128)S(1)}, u32[]{:S(2)}, u32[]{:S(2)}) collective-permute-start(f32[64,512]{1,0:T(8,128)S(1)} %get-tuple-element.20), channel_id=1, source_target_pairs={{0,8},{8,16},{16,24},{24,32},{32,40},{40,48},{48,56},{56,64},{64,7... | collective-permute-start | bytes 393224 | tf_op jit(solution)/shard_map/ppermute | solution.py:445
  24.5 0.0 collective-permute-done.4.low_ref
  24.5 0.0 copy-start.2
  24.5 0.0 copy-start.8
  24.6 0.0 copy-start.10
  24.6 2.5 %collective-permute-start.3 = (f32[64,512]{1,0:T(8,128)S(1)}, f32[64,512]{1,0:T(8,128)S(1)}, u32[]{:S(2)}, u32[]{:S(2)}) collective-permute-start(f32[64,512]{1,0:T(8,128)S(1)} %get-tuple-element.21), channel_id=1, source_target_pairs={{0,16},{8,24},{16,32},{24,40},{32,48},{40,56},{48,64},{56,72},{64,... | collective-permute-start | bytes 393224 | tf_op jit(solution)/shard_map/ppermute | solution.py:445
  27.1 0.0 copy-done.1
  27.1 0.0 copy-done.3
  27.1 0.0 copy-done.9
  27.1 0.0 copy-done.11
  27.1 0.0 copy-done.12
  27.1 0.0 copy-done.13
  27.1 7.6 %shard_map.141 = (f32[64,1024]{1,0:T(8,128)S(1)}, f32[64,1024]{1,0:T(8,128)S(1)}) custom-call(f32[64,1024]{1,0:T(8,128)S(1)} %copy-done.1, s32[27,1024]{1,0:T(8,128)S(1)} %copy-done.3, bf16[400,192]{1,0:T(8,128)(2,1)S(1)} %copy-done.9, bf16[64,288]{1,0:T(8,128)(2,1)S(1)} %copy-done.11, bf16[64,192]{1,0:T(8,128)(2,1)S(1)} %copy-done.12, ...), custom_call_target="tpu_custom_call" | custom-call | flops 4000000000 | bytes 16000000 | tf_op jit(solution)/shard_map/pallas_call | solution.py:472
  34.8 0.0 collective-permute-done.5.high_ref
  34.8 0.0 collective-permute-done.r0
  34.8 0.0 collective-permute-done.1.r1
  34.8 0.0 collective-permute-done.2.r2
  34.8 2.1 %collective-permute-done.3.r3 = f32[64,512]{1,0:T(8,128)S(1)} collective-permute-done((f32[64,512]{1,0:T(8,128)S(1)}, f32[64,512]{1,0:T(8,128)S(1)}, u32[]{:S(2)}, u32[]{:S(2)}) %collective-permute-start.3) | collective-permute-done | bytes 131104 | tf_op jit(solution)/shard_map/ppermute | solution.py:445
  36.9 0.0 copy-done.2
  36.9 0.0 copy-done.8
  36.9 0.0 copy-done.10
  36.9 22.3 %shard_map.142 = (f32[64,1024]{1,0:T(8,128)}, f32[64,1024]{1,0:T(8,128)S(1)}, f32[64,512]{1,0:T(8,128)S(1)}, f32[64,512]{1,0:T(8,128)S(1)}, f32[64,512]{1,0:T(8,...) custom-call(f32[64,512]{1,0:T(8,128)S(1)} %collective-permute-done.r0, ...), custom_call_target="tpu_custom_call" | custom-call | flops 10000000000 | bytes 40000000 | tf_op jit(solution)/shard_map/pallas_call | solution.py:481
  59.3 1.9 %collective-permute-start.10 = (f32[64,256]{1,0:T(8,128)S(1)}, f32[64,256]{1,0:T(8,128)S(1)}, u32[]{:S(2)}, u32[]{:S(2)}) collective-permute-start(f32[64,256]{1,0:T(8,128)S(1)} %get-tuple-element.32), channel_id=1, source_target_pairs={{0,1},{1,2},{2,3},{3,4},{4,5},{5,6},{6,7},{8,9},{9,10},{10,11},{11... | collective-permute-start | bytes 196616 | tf_op jit(solution)/shard_map/ppermute | solution.py:445
  61.2 3.6 %collective-permute-start.11 = (f32[64,256]{1,0:T(8,128)S(1)}, f32[64,256]{1,0:T(8,128)S(1)}, u32[]{:S(2)}, u32[]{:S(2)}) collective-permute-start(f32[64,256]{1,0:T(8,128)S(1)} %get-tuple-element.33), channel_id=1, source_target_pairs={{1,0},{2,1},{3,2},{4,3},{5,4},{6,5},{7,6},{9,8},{10,9},{11,10},{12... | collective-permute-start | bytes 196616 | tf_op jit(solution)/shard_map/ppermute | solution.py:445
  64.8 1.9 %collective-permute-start.6 = (f32[64,512]{1,0:T(8,128)S(1)}, f32[64,512]{1,0:T(8,128)S(1)}, u32[]{:S(2)}, u32[]{:S(2)}) collective-permute-start(f32[64,512]{1,0:T(8,128)S(1)} %get-tuple-element.28), channel_id=1, source_target_pairs={{0,16},{8,24},{16,32},{24,40},{32,48},{40,56},{48,64},{56,72},{64,... | collective-permute-start | bytes 393224 | tf_op jit(solution)/shard_map/ppermute | solution.py:445
  66.8 2.1 %collective-permute-start.7 = (f32[64,512]{1,0:T(8,128)S(1)}, f32[64,512]{1,0:T(8,128)S(1)}, u32[]{:S(2)}, u32[]{:S(2)}) collective-permute-start(f32[64,512]{1,0:T(8,128)S(1)} %get-tuple-element.29), channel_id=1, source_target_pairs={{0,8},{8,16},{16,24},{24,32},{32,40},{40,48},{48,56},{56,64},{64,7... | collective-permute-start | bytes 393224 | tf_op jit(solution)/shard_map/ppermute | solution.py:445
  68.8 5.9 %collective-permute-start.8 = (f32[64,512]{1,0:T(8,128)S(1)}, f32[64,512]{1,0:T(8,128)S(1)}, u32[]{:S(2)}, u32[]{:S(2)}) collective-permute-start(f32[64,512]{1,0:T(8,128)S(1)} %get-tuple-element.30), channel_id=1, source_target_pairs={{8,0},{16,8},{24,16},{32,24},{40,32},{48,40},{56,48},{64,56},{72,6... | collective-permute-start | bytes 393224 | tf_op jit(solution)/shard_map/ppermute | solution.py:445
  74.7 0.0 collective-permute-done.10.v4
  74.7 4.8 %collective-permute-start.9 = (f32[64,512]{1,0:T(8,128)S(1)}, f32[64,512]{1,0:T(8,128)S(1)}, u32[]{:S(2)}, u32[]{:S(2)}) collective-permute-start(f32[64,512]{1,0:T(8,128)S(1)} %get-tuple-element.31), channel_id=1, source_target_pairs={{16,0},{24,8},{32,16},{40,24},{48,32},{56,40},{64,48},{72,56},{80,... | collective-permute-start | bytes 393224 | tf_op jit(solution)/shard_map/ppermute | solution.py:445
  79.6 0.0 copy-start.5
  79.6 9.0 %shard_map.143.sens_ref = f32[64,1024]{1,0:T(8,128)S(1)} custom-call(f32[64,1024]{1,0:T(8,128)S(1)} %get-tuple-element.27.scaled_ref, s32[27,1024]{1,0:T(8,128)S(1)} %copy-done.3, bf16[512,192]{1,0:T(8,128)(2,1)S(1)} %copy-done.8, bf16[128,384]{1,0:T(8,128)(2,1)S(1)} %copy-done.10, bf16[64,192]{1,0:T(8,128)(2,1)S(1)} %copy-done.12), custom_call_target="tpu_custom_call" | custom-call | flops 4000000000 | bytes 16000000 | tf_op jit(solution)/shard_map/pallas_call | solution.py:496
  88.6 0.0 collective-permute-done.11.v5
  88.6 0.0 collective-permute-done.6.v0
  88.6 0.0 collective-permute-done.7.v1
  88.7 0.0 collective-permute-done.8.v2
  88.7 0.0 collective-permute-done.9.v3
  88.7 0.0 copy-done.5
  88.7 2.1 %shard_map.144 = f32[64,1024]{1,0:T(8,128)} custom-call(s32[4]{0:T(128)S(1)} %bitcast.8, f32[64,1024]{1,0:T(8,128)S(1)} %shard_map.143.sens_ref, s32[4,512]{1,0:T(4,128)S(1)} %bitcast.4, s32[2,256]{1,0:T(2,128)S(1)} %bitcast.6, f32[64,512]{1,0:T(8,128)S(1)} %collective-permute-done.6.v0, f32[64,512]{1,0:T(8,128)S(1)} %collective-permute-done.7.v1, ...), custom_call_target="tpu_custom_call" | custom-call | flops 1500000000 | bytes 6000000 | tf_op jit(solution)/shard_map/pallas_call | solution.py:505
Async XLA Ops:
  0.6 0.7 copy-start.6
  0.6 0.7 copy-start.7
  1.3 1.0 %copy-start = (f32[64,1024]{1,0:T(8,128)S(1)}, f32[64,1024]{1,0:T(8,128)}, u32[]{:S(2)}) copy-start(f32[64,1024]{1,0:T(8,128)} %density_ref.3) | copy-start | bytes 786436
  2.3 0.7 copy-start.4
  3.0 24.1 %copy-start.1 = (f32[64,1024]{1,0:T(8,128)S(1)}, f32[64,1024]{1,0:T(8,128)}, u32[]{:S(2)}) copy-start(f32[64,1024]{1,0:T(8,128)} %density_ref.3) | copy-start | bytes 786436
  3.0 24.1 %copy-start.3 = (s32[27,1024]{1,0:T(8,128)S(1)}, s32[27,1024]{1,0:T(8,128)}, u32[]{:S(2)}) copy-start(s32[27,1024]{1,0:T(8,128)} %links_ref.5) | copy-start | bytes 331780
  3.0 24.1 %copy-start.9 = (bf16[400,192]{1,0:T(8,128)(2,1)S(1)}, bf16[400,192]{1,0:T(8,128)(2,1)}, u32[]{:S(2)}) copy-start(bf16[400,192]{1,0:T(8,128)(2,1)} %constant.12.clone.fold_ref) | copy-start | bytes 460804
  3.0 24.1 %copy-start.11 = (bf16[64,288]{1,0:T(8,128)(2,1)S(1)}, bf16[64,288]{1,0:T(8,128)(2,1)}, u32[]{:S(2)}) copy-start(bf16[64,288]{1,0:T(8,128)(2,1)} %constant.15.clone.join_ref) | copy-start | bytes 110596
  3.0 24.1 %copy-start.12 = (bf16[64,192]{1,0:T(8,128)(2,1)S(1)}, bf16[64,192]{1,0:T(8,128)(2,1)}, u32[]{:S(2)}) copy-start(bf16[64,192]{1,0:T(8,128)(2,1)} %constant.14.clone.own_ref) | copy-start | bytes 73732
  3.0 24.1 %copy-start.13 = (bf16[64,54]{1,0:T(8,128)(2,1)S(1)}, bf16[64,54]{1,0:T(8,128)(2,1)}, u32[]{:S(2)}) copy-start(bf16[64,54]{1,0:T(8,128)(2,1)} %constant.17.clone.sums_ref) | copy-start | bytes 20740
  4.6 19.9 %collective-permute-start.4 = (f32[64,256]{1,0:T(8,128)S(1)}, f32[64,256]{1,0:T(8,128)S(1)}, u32[]{:S(2)}, u32[]{:S(2)}) collective-permute-start(f32[64,256]{1,0:T(8,128)S(1)} %get-tuple-element.22), channel_id=1, source_target_pairs={{0,1},{1,2},{2,3},{3,4},{4,5},{5,6},{6,7},{8,9},{9,10},{10,11},{11... | collective-permute-start | bytes 196616 | tf_op jit(solution)/shard_map/ppermute | solution.py:445
  6.5 28.2 %collective-permute-start.5 = (f32[64,256]{1,0:T(8,128)S(1)}, f32[64,256]{1,0:T(8,128)S(1)}, u32[]{:S(2)}, u32[]{:S(2)}) collective-permute-start(f32[64,256]{1,0:T(8,128)S(1)} %get-tuple-element.23), channel_id=1, source_target_pairs={{1,0},{2,1},{3,2},{4,3},{5,4},{6,5},{7,6},{9,8},{10,9},{11,10},{12... | collective-permute-start | bytes 196616 | tf_op jit(solution)/shard_map/ppermute | solution.py:445
  10.2 24.6 %collective-permute-start = (f32[64,512]{1,0:T(8,128)S(1)}, f32[64,512]{1,0:T(8,128)S(1)}, u32[]{:S(2)}, u32[]{:S(2)}) collective-permute-start(f32[64,512]{1,0:T(8,128)S(1)} %get-tuple-element.18), channel_id=1, source_target_pairs={{16,0},{24,8},{32,16},{40,24},{48,32},{56,40},{64,48},{72,56},{80,... | collective-permute-start | bytes 393224 | tf_op jit(solution)/shard_map/ppermute | solution.py:445
  18.7 16.1 %collective-permute-start.1 = (f32[64,512]{1,0:T(8,128)S(1)}, f32[64,512]{1,0:T(8,128)S(1)}, u32[]{:S(2)}, u32[]{:S(2)}) collective-permute-start(f32[64,512]{1,0:T(8,128)S(1)} %get-tuple-element.19), channel_id=1, source_target_pairs={{8,0},{16,8},{24,16},{32,24},{40,32},{48,40},{56,48},{64,56},{72,6... | collective-permute-start | bytes 393224 | tf_op jit(solution)/shard_map/ppermute | solution.py:445
  21.6 13.2 %collective-permute-start.2 = (f32[64,512]{1,0:T(8,128)S(1)}, f32[64,512]{1,0:T(8,128)S(1)}, u32[]{:S(2)}, u32[]{:S(2)}) collective-permute-start(f32[64,512]{1,0:T(8,128)S(1)} %get-tuple-element.20), channel_id=1, source_target_pairs={{0,8},{8,16},{16,24},{24,32},{32,40},{40,48},{48,56},{56,64},{64,7... | collective-permute-start | bytes 393224 | tf_op jit(solution)/shard_map/ppermute | solution.py:445
  24.5 12.4 %copy-start.2 = (f32[64,1024]{1,0:T(8,128)S(1)}, f32[64,1024]{1,0:T(8,128)}, u32[]{:S(2)}) copy-start(f32[64,1024]{1,0:T(8,128)} %energy_ref.1) | copy-start | bytes 786436
  24.5 12.4 %copy-start.8 = (bf16[512,192]{1,0:T(8,128)(2,1)S(1)}, bf16[512,192]{1,0:T(8,128)(2,1)}, u32[]{:S(2)}) copy-start(bf16[512,192]{1,0:T(8,128)(2,1)} %constant.13.clone.fold_b_ref) | copy-start | bytes 589828
  24.6 12.4 %copy-start.10 = (bf16[128,384]{1,0:T(8,128)(2,1)S(1)}, bf16[128,384]{1,0:T(8,128)(2,1)}, u32[]{:S(2)}) copy-start(bf16[128,384]{1,0:T(8,128)(2,1)} %constant.16.clone.join_b_ref) | copy-start | bytes 294916
  24.6 12.4 %collective-permute-start.3 = (f32[64,512]{1,0:T(8,128)S(1)}, f32[64,512]{1,0:T(8,128)S(1)}, u32[]{:S(2)}, u32[]{:S(2)}) collective-permute-start(f32[64,512]{1,0:T(8,128)S(1)} %get-tuple-element.21), channel_id=1, source_target_pairs={{0,16},{8,24},{16,32},{24,40},{32,48},{40,56},{48,64},{56,72},{64,... | collective-permute-start | bytes 393224 | tf_op jit(solution)/shard_map/ppermute | solution.py:445
  59.3 15.5 %collective-permute-start.10 = (f32[64,256]{1,0:T(8,128)S(1)}, f32[64,256]{1,0:T(8,128)S(1)}, u32[]{:S(2)}, u32[]{:S(2)}) collective-permute-start(f32[64,256]{1,0:T(8,128)S(1)} %get-tuple-element.32), channel_id=1, source_target_pairs={{0,1},{1,2},{2,3},{3,4},{4,5},{5,6},{6,7},{8,9},{9,10},{10,11},{11... | collective-permute-start | bytes 196616 | tf_op jit(solution)/shard_map/ppermute | solution.py:445
  61.2 27.4 %collective-permute-start.11 = (f32[64,256]{1,0:T(8,128)S(1)}, f32[64,256]{1,0:T(8,128)S(1)}, u32[]{:S(2)}, u32[]{:S(2)}) collective-permute-start(f32[64,256]{1,0:T(8,128)S(1)} %get-tuple-element.33), channel_id=1, source_target_pairs={{1,0},{2,1},{3,2},{4,3},{5,4},{6,5},{7,6},{9,8},{10,9},{11,10},{12... | collective-permute-start | bytes 196616 | tf_op jit(solution)/shard_map/ppermute | solution.py:445
  64.8 23.8 %collective-permute-start.6 = (f32[64,512]{1,0:T(8,128)S(1)}, f32[64,512]{1,0:T(8,128)S(1)}, u32[]{:S(2)}, u32[]{:S(2)}) collective-permute-start(f32[64,512]{1,0:T(8,128)S(1)} %get-tuple-element.28), channel_id=1, source_target_pairs={{0,16},{8,24},{16,32},{24,40},{32,48},{40,56},{48,64},{56,72},{64,... | collective-permute-start | bytes 393224 | tf_op jit(solution)/shard_map/ppermute | solution.py:445
  66.8 21.9 %collective-permute-start.7 = (f32[64,512]{1,0:T(8,128)S(1)}, f32[64,512]{1,0:T(8,128)S(1)}, u32[]{:S(2)}, u32[]{:S(2)}) collective-permute-start(f32[64,512]{1,0:T(8,128)S(1)} %get-tuple-element.29), channel_id=1, source_target_pairs={{0,8},{8,16},{16,24},{24,32},{32,40},{40,48},{48,56},{56,64},{64,7... | collective-permute-start | bytes 393224 | tf_op jit(solution)/shard_map/ppermute | solution.py:445
  68.8 19.8 %collective-permute-start.8 = (f32[64,512]{1,0:T(8,128)S(1)}, f32[64,512]{1,0:T(8,128)S(1)}, u32[]{:S(2)}, u32[]{:S(2)}) collective-permute-start(f32[64,512]{1,0:T(8,128)S(1)} %get-tuple-element.30), channel_id=1, source_target_pairs={{8,0},{16,8},{24,16},{32,24},{40,32},{48,40},{56,48},{64,56},{72,6... | collective-permute-start | bytes 393224 | tf_op jit(solution)/shard_map/ppermute | solution.py:445
  74.7 13.9 %collective-permute-start.9 = (f32[64,512]{1,0:T(8,128)S(1)}, f32[64,512]{1,0:T(8,128)S(1)}, u32[]{:S(2)}, u32[]{:S(2)}) collective-permute-start(f32[64,512]{1,0:T(8,128)S(1)} %get-tuple-element.31), channel_id=1, source_target_pairs={{16,0},{24,8},{32,16},{40,24},{48,32},{56,40},{64,48},{72,56},{80,... | collective-permute-start | bytes 393224 | tf_op jit(solution)/shard_map/ppermute | solution.py:445
  79.6 9.1 %copy-start.5 = (s32[1,1,4,512]{3,2,1,0:T(4,128)S(1)}, s32[1,1,4,512]{3,2,1,0:T(4,128)}, u32[]{:S(2)}) copy-start(s32[1,1,4,512]{3,2,1,0:T(4,128)} %param.16) | copy-start | bytes 24580

commit v2 on v1

--- a/solution.py
+++ b/solution.py
@@ -210,8 +210,8 @@
 
         return step
 
-    lax.fori_loop(0, faces, make(tf, pf, 32, 0), 0)
-    lax.fori_loop(0, edges, make(te, pe, 16, faces), 0)
+    lax.fori_loop(0, faces, make(tf, pf, 32, 0), 0, unroll=True)
+    lax.fori_loop(0, edges, make(te, pe, 16, faces), 0, unroll=True)
     corner = [[], []]
     for bg in range(blocks // 128):
         idx = rows_ref[18:26, bg * 128 : bg * 128 + 128]
@@ -281,8 +281,8 @@
 
         return step
 
-    lax.fori_loop(0, faces, make(sf, zf, 32, 0), 0)
-    lax.fori_loop(0, edges, make(se, ze, 16, faces), 0)
+    lax.fori_loop(0, faces, make(sf, zf, 32, 0), 0, unroll=True)
+    lax.fori_loop(0, edges, make(se, ze, 16, faces), 0, unroll=True)
     fours = (count + 3) // 4
 
     def corner_step(m, carry):
@@ -297,7 +297,7 @@
         zc[m, :, :] = dot_nt(jnp.concatenate(parts, axis=0), hot)
         return carry
 
-    lax.fori_loop(0, corners, corner_step, 0)
+    lax.fori_loop(0, corners, corner_step, 0, unroll=True)
     out = []
     for h in range(count):
         totals = order_totals(
@@ -339,7 +339,7 @@
         outs[g][...] = pick(idx, jnp.where(at < live_ref[g], idx >> 8, -1))
     for side in range(2):
         idx = face_ref[side : side + 1, :]
-        outs[groups + side][...] = pick(idx, idx >> 8)
+        outs[groups + side][...] = pick(idx, jnp.where(live_ref[groups + side] > 0, idx >> 8, -1))
 
 
 def local_kernel(
@@ -399,7 +399,7 @@
             upper = jnp.where(at < live_ref[g], idx >> 8, -1)
         else:
             idx = face_ref[g - groups : g - groups + 1, :]
-            upper = idx >> 8
+            upper = jnp.where(live_ref[g] > 0, idx >> 8, -1)
         hot = one_hot(idx & (TILE - 1))
         value = jnp.concatenate(split2(ref[...]), axis=0)
         parts = [value * (upper == h).astype(F32).astype(BF16) for h in range(heads)]
@@ -441,22 +441,28 @@
 
 def passed_along(shard, axis, by):
     count = lax.axis_size(axis)
-    pairs = [(i, i + by) for i in range(count) if 0 <= i + by < count]
+    pairs = [(i, (i + by) % count) for i in range(count)]
     return lax.ppermute(shard, axis, pairs)
 
 
 def on_device(density, energy, links, send_index, send_live, face_index):
     const = {name: jnp.asarray(value) for name, value in constants().items()}
     blocks = density.shape[1]
-    indices, counts, faces_at = send_index[0, 0], send_live[0, 0], face_index[0, 0]
+    offsets = [offset for offset in range(-REACH, REACH + 1) if offset != 0]
+    indices, faces_at = send_index[0, 0], face_index[0, 0]
     capacity, face_count = indices.shape[1], faces_at.shape[1]
+    targets = jnp.concatenate(
+        [lax.axis_index("plane") + np.array(offsets), lax.axis_index("depth") + np.array([-1, 1])]
+    )
+    ends = np.array([lax.axis_size("plane")] * len(offsets) + [lax.axis_size("depth")] * 2)
+    counts = jnp.concatenate([send_live[0, 0], np.array([face_count] * 2, np.int32)])
+    counts = jnp.where((targets >= 0) & (targets < ends), counts, 0)
     whole = jax.ShapeDtypeStruct((64, blocks), F32)
     listed = jax.ShapeDtypeStruct((64, capacity), F32)
     faced = jax.ShapeDtypeStruct((64, face_count), F32)
     vmem = pl.BlockSpec(memory_space=pltpu.VMEM)
     smem = pl.BlockSpec(memory_space=pltpu.SMEM)
     ordered = pltpu.VMEM((32, blocks), jnp.int32)
-    offsets = [offset for offset in range(-REACH, REACH + 1) if offset != 0]
 
     loads = pl.pallas_call(
         payload_kernel,

time: 91.3 us -> 63.5 us (0.70)
  the two profiles are of different devices: /device:TPU:14 before, /device:TPU:8 now
where the time goes in v2:
time: 63.5 us; the launch traced here: 63.2 us
  Pallas kernels  27.8 us (44%)
  starting transfers between devices  23.3 us (37%)
  waiting for transfers between devices  8.27 us (13%)
  local copies, waits for them, and re-layouts  2.97 us (5%)
  between operations  0.79 us (1%)
    ppermute x12, starting transfers between devices, passed_along(): return lax.ppermute(shard, axis, pairs)  23.3 us
    pallas_call x1, Pallas kernels, on_device(): pl.pallas_call(remote_kernel, out_shape=[whole, whole] + [listed] * 4 + [...  14.1 us
    ppermute x12, waiting for transfers between devices, passed_along(): return lax.ppermute(shard, axis, pairs)  8.27 us
    pallas_call x1, Pallas kernels, on_device(): pl.pallas_call(local_kernel, out_shape=[whole, whole], in_specs=[vmem] *...  5.04 us
    pallas_call x1, Pallas kernels, on_device(): pl.pallas_call(own_kernel, out_shape=whole, in_specs=[vmem] * 5, out_spec...  4.85 us
    unnamed x30, local copies, waits for them, and re-layouts  2.97 us
    pallas_call x1, Pallas kernels, on_device(): pl.pallas_call(final_kernel, out_shape=whole, in_specs=[smem] + [vmem] *...  2.13 us
    pallas_call x1, Pallas kernels, on_device(): pl.pallas_call(payload_kernel, out_shape=[listed] * 4 + [faced] * 2, in_s...  1.59 us
  transfers between devices with their start and end apart: 12, of which 4 were waited for; matrix products, arithmetic and copies ran while one was open for 0% of the time, Pallas kernels for 16%

profile of v2, /device:TPU:8, one launch (start us, length us, event | category | flops | bytes accessed | tf_op | source)
XLA Modules:
  0.0 63.2 jit_solution(736514250067653015)
XLA Ops:
  0.6 0.0 copy-start.14
  0.6 0.0 copy-start.13
  0.7 0.0 copy-start.3
  0.7 0.6 copy-done.14
  1.3 0.0 copy-done.13
  1.3 0.0 copy-start.11
  1.3 0.0 copy-start.12
  1.3 0.6 %copy-done.11 = s32[1,1,4]{2,1,0:T(1,128)S(1)} copy-done((s32[1,1,4]{2,1,0:T(1,128)S(1)}, s32[1,1,4]{2,1,0:T(1,128)}, u32[]{:S(2)}) %copy-start.11) | copy-done | bytes 40
  2.0 0.0 copy-done.12
  2.0 0.1 and_select_fusion.live_ref
  2.1 0.0 copy-start.4
  2.1 0.0 copy-done.3
  2.1 0.7 %copy-done.4 = s32[1,1,2,256]{3,2,1,0:T(2,128)S(1)} copy-done((s32[1,1,2,256]{3,2,1,0:T(2,128)S(1)}, s32[1,1,2,256]{3,2,1,0:T(2,128)}, u32[]{:S(2)}) %copy-start.4) | copy-done | bytes 2072
  2.7 0.0 copy-start
  2.7 0.9 %copy-done = f32[64,1024]{1,0:T(8,128)S(1)} copy-done((f32[64,1024]{1,0:T(8,128)S(1)}, f32[64,1024]{1,0:T(8,128)}, u32[]{:S(2)}) %copy-start) | copy-done | bytes 262168
  3.7 0.0 copy-start.2
  3.7 0.0 copy-start.6
  3.7 0.0 copy-start.8
  3.7 0.0 copy-start.9
  3.7 0.0 copy-start.10
  3.7 1.6 %shard_map.176 = (f32[64,512]{1,0:T(8,128)S(1)}, f32[64,512]{1,0:T(8,128)S(1)}, f32[64,512]{1,0:T(8,128)S(1)}, f32[64,512]{1,0:T(8,128)S(1)}, f32[64,256]{1,0:T(8,128)S(1)}, /*index=5*/f32[64,256]{1,0:T(8,128)S(1)}) custom-call(s32[6]{0:T(128)S(1)} %and_select_fusion.live_ref, f32[64,1024]{1,0:T(8,128)S(1)} %copy-done, s32[4,512]{1,0:T(4,128)S(1)} %bitcast.3, ...), custom_call_target="tpu_custom_call" | custom-call | flops 1500000000 | bytes 6000000 | tf_op jit(solution)/shard_map/pallas_call | solution.py:467
  5.3 0.0 collective-permute-start.4
  5.3 1.7 %collective-permute-start.5 = (f32[64,256]{1,0:T(8,128)S(1)}, f32[64,256]{1,0:T(8,128)S(1)}, u32[]{:S(2)}, u32[]{:S(2)}) collective-permute-start(f32[64,256]{1,0:T(8,128)S(1)} %get-tuple-element.23), channel_id=1, source_target_pairs={{0,7},{1,0},{2,1},{3,2},{4,3},{5,4},{6,5},{7,6},{8,15},{9,8},{10,9... | collective-permute-start | bytes 196616 | tf_op jit(solution)/shard_map/ppermute | solution.py:445
  7.1 8.5 %collective-permute-start = (f32[64,512]{1,0:T(8,128)S(1)}, f32[64,512]{1,0:T(8,128)S(1)}, u32[]{:S(2)}, u32[]{:S(2)}) collective-permute-start(f32[64,512]{1,0:T(8,128)S(1)} %get-tuple-element.18), channel_id=1, source_target_pairs={{0,240},{8,248},{16,0},{24,8},{32,16},{40,24},{48,32},{56,40},{64,... | collective-permute-start | bytes 393224 | tf_op jit(solution)/shard_map/ppermute | solution.py:445
  15.6 1.0 %collective-permute-start.1 = (f32[64,512]{1,0:T(8,128)S(1)}, f32[64,512]{1,0:T(8,128)S(1)}, u32[]{:S(2)}, u32[]{:S(2)}) collective-permute-start(f32[64,512]{1,0:T(8,128)S(1)} %get-tuple-element.19), channel_id=1, source_target_pairs={{0,248},{8,0},{16,8},{24,16},{32,24},{40,32},{48,40},{56,48},{64,5... | collective-permute-start | bytes 393224 | tf_op jit(solution)/shard_map/ppermute | solution.py:445
  16.6 1.0 %collective-permute-start.2 = (f32[64,512]{1,0:T(8,128)S(1)}, f32[64,512]{1,0:T(8,128)S(1)}, u32[]{:S(2)}, u32[]{:S(2)}) collective-permute-start(f32[64,512]{1,0:T(8,128)S(1)} %get-tuple-element.20), channel_id=1, source_target_pairs={{0,8},{8,16},{16,24},{24,32},{32,40},{40,48},{48,56},{56,64},{64,7... | collective-permute-start | bytes 393224 | tf_op jit(solution)/shard_map/ppermute | solution.py:445
  17.6 0.0 collective-permute-done.4.low_ref
  17.6 0.0 copy-start.1
  17.6 0.0 copy-start.5
  17.6 0.0 copy-start.7
  17.6 0.7 %collective-permute-start.3 = (f32[64,512]{1,0:T(8,128)S(1)}, f32[64,512]{1,0:T(8,128)S(1)}, u32[]{:S(2)}, u32[]{:S(2)}) collective-permute-start(f32[64,512]{1,0:T(8,128)S(1)} %get-tuple-element.21), channel_id=1, source_target_pairs={{0,16},{8,24},{16,32},{24,40},{32,48},{40,56},{48,64},{56,72},{64,... | collective-permute-start | bytes 393224 | tf_op jit(solution)/shard_map/ppermute | solution.py:445
  18.3 0.0 copy-done.2
  18.3 0.0 copy-done.6
  18.4 0.0 copy-done.8
  18.4 0.0 copy-done.9
  18.4 0.0 copy-done.10
  18.4 5.0 %shard_map.177 = (f32[64,1024]{1,0:T(8,128)S(1)}, f32[64,1024]{1,0:T(8,128)S(1)}) custom-call(f32[64,1024]{1,0:T(8,128)S(1)} %copy-done, s32[27,1024]{1,0:T(8,128)S(1)} %copy-done.2, bf16[400,192]{1,0:T(8,128)(2,1)S(1)} %copy-done.6, bf16[64,288]{1,0:T(8,128)(2,1)S(1)} %copy-done.8, bf16[64,192]{1,0:T(8,128)(2,1)S(1)} %copy-done.9, bf16[64,54]{1,0:T(8,128)(2,1)S(1)} %copy-done.10), custom_call_target="tpu_custom_call" | custom-call | flops 4000000000 | bytes 16000000 | tf_op jit(solution)/shard_map/pallas_call | solution.py:478
  23.4 0.0 collective-permute-done.5.high_ref
  23.4 0.0 collective-permute-done.r0
  23.4 0.6 collective-permute-done.1.r1
  24.1 3.7 %collective-permute-done.2.r2 = f32[64,512]{1,0:T(8,128)S(1)} collective-permute-done((f32[64,512]{1,0:T(8,128)S(1)}, f32[64,512]{1,0:T(8,128)S(1)}, u32[]{:S(2)}, u32[]{:S(2)}) %collective-permute-start.2) | collective-permute-done | bytes 131104 | tf_op jit(solution)/shard_map/ppermute | solution.py:445
  27.8 1.7 %collective-permute-done.3.r3 = f32[64,512]{1,0:T(8,128)S(1)} collective-permute-done((f32[64,512]{1,0:T(8,128)S(1)}, f32[64,512]{1,0:T(8,128)S(1)}, u32[]{:S(2)}, u32[]{:S(2)}) %collective-permute-start.3) | collective-permute-done | bytes 131104 | tf_op jit(solution)/shard_map/ppermute | solution.py:445
  29.5 0.0 copy-done.1
  29.5 0.0 copy-done.5
  29.5 0.0 copy-done.7
  29.5 14.1 %shard_map.178 = (f32[64,1024]{1,0:T(8,128)}, f32[64,1024]{1,0:T(8,128)S(1)}, f32[64,512]{1,0:T(8,128)S(1)}, f32[64,512]{1,0:T(8,128)S(1)}, f32[64,512]{1,0:T(8,...) custom-call(f32[64,512]{1,0:T(8,128)S(1)} %collective-permute-done.r0, ...), custom_call_target="tpu_custom_call" | custom-call | flops 10000000000 | bytes 40000000 | tf_op jit(solution)/shard_map/pallas_call | solution.py:487
  43.7 0.0 collective-permute-start.10
  43.7 1.7 %collective-permute-start.11 = (f32[64,256]{1,0:T(8,128)S(1)}, f32[64,256]{1,0:T(8,128)S(1)}, u32[]{:S(2)}, u32[]{:S(2)}) collective-permute-start(f32[64,256]{1,0:T(8,128)S(1)} %get-tuple-element.33), channel_id=1, source_target_pairs={{0,7},{1,0},{2,1},{3,2},{4,3},{5,4},{6,5},{7,6},{8,15},{9,8},{10,9... | collective-permute-start | bytes 196616 | tf_op jit(solution)/shard_map/ppermute | solution.py:445
  45.4 0.0 collective-permute-start.6
  45.4 2.3 %collective-permute-start.7 = (f32[64,512]{1,0:T(8,128)S(1)}, f32[64,512]{1,0:T(8,128)S(1)}, u32[]{:S(2)}, u32[]{:S(2)}) collective-permute-start(f32[64,512]{1,0:T(8,128)S(1)} %get-tuple-element.29), channel_id=1, source_target_pairs={{0,8},{8,16},{16,24},{24,32},{32,40},{40,48},{48,56},{56,64},{64,7... | collective-permute-start | bytes 393224 | tf_op jit(solution)/shard_map/ppermute | solution.py:445
  47.7 4.8 %collective-permute-start.8 = (f32[64,512]{1,0:T(8,128)S(1)}, f32[64,512]{1,0:T(8,128)S(1)}, u32[]{:S(2)}, u32[]{:S(2)}) collective-permute-start(f32[64,512]{1,0:T(8,128)S(1)} %get-tuple-element.30), channel_id=1, source_target_pairs={{0,248},{8,0},{16,8},{24,16},{32,24},{40,32},{48,40},{56,48},{64,5... | collective-permute-start | bytes 393224 | tf_op jit(solution)/shard_map/ppermute | solution.py:445
  52.5 0.0 collective-permute-done.10.v4
  52.5 1.5 %collective-permute-start.9 = (f32[64,512]{1,0:T(8,128)S(1)}, f32[64,512]{1,0:T(8,128)S(1)}, u32[]{:S(2)}, u32[]{:S(2)}) collective-permute-start(f32[64,512]{1,0:T(8,128)S(1)} %get-tuple-element.31), channel_id=1, source_target_pairs={{0,240},{8,248},{16,0},{24,8},{32,16},{40,24},{48,32},{56,40},{64,... | collective-permute-start | bytes 393224 | tf_op jit(solution)/shard_map/ppermute | solution.py:445
  54.0 4.9 %shard_map.179.sens_ref = f32[64,1024]{1,0:T(8,128)S(1)} custom-call(f32[64,1024]{1,0:T(8,128)S(1)} %get-tuple-element.27.scaled_ref, s32[27,1024]{1,0:T(8,128)S(1)} %copy-done.2, bf16[512,192]{1,0:T(8,128)(2,1)S(1)} %copy-done.5, bf16[128,384]{1,0:T(8,128)(2,1)S(1)} %copy-done.7, bf16[64,192]{1,0:T(8,128)(2,1)S(1)} %copy-done.9), custom_call_target="tpu_custom_call" | custom-call | flops 4000000000 | bytes 16000000 | tf_op jit(solution)/shard_map/pallas_call | solution.py:502
  58.8 0.0 collective-permute-done.11.v5
  58.9 0.0 collective-permute-done.6.v0
  58.9 2.2 %collective-permute-done.7.v1 = f32[64,512]{1,0:T(8,128)S(1)} collective-permute-done((f32[64,512]{1,0:T(8,128)S(1)}, f32[64,512]{1,0:T(8,128)S(1)}, u32[]{:S(2)}, u32[]{:S(2)}) %collective-permute-start.7) | collective-permute-done | bytes 131104 | tf_op jit(solution)/shard_map/ppermute | solution.py:445
  61.0 0.0 collective-permute-done.8.v2
  61.1 0.0 collective-permute-done.9.v3
  61.1 2.1 %shard_map.180 = f32[64,1024]{1,0:T(8,128)} custom-call(s32[6]{0:T(128)S(1)} %and_select_fusion.live_ref, f32[64,1024]{1,0:T(8,128)S(1)} %shard_map.179.sens_ref, s32[4,512]{1,0:T(4,128)S(1)} %bitcast.4, s32[2,256]{1,0:T(2,128)S(1)} %bitcast.6, f32[64,512]{1,0:T(8,128)S(1)} %collective-permute-done.6.v0, f32[64,512]{1,0:T(8,128)S(1)} %collective-permute-done.7.v1, ...), custom_call_target="tpu_custom_call" | custom-call | flops 1500000000 | bytes 6000000 | tf_op jit(solution)/shard_map/pallas_call | solution.py:511
  (2 shorter events, 0.0 us)
Async XLA Ops:
  0.6 0.7 %copy-start.14 = (s32[2]{0:T(128)S(1)}, s32[2]{0:T(128)}, u32[]{:S(2)}) copy-start(s32[2]{0:T(128)} %constant.39.clone) | copy-start | bytes 28
  0.6 0.7 %copy-start.13 = (s32[4]{0:T(128)S(1)}, s32[4]{0:T(128)}, u32[]{:S(2)}) copy-start(s32[4]{0:T(128)} %constant.38.clone) | copy-start | bytes 52
  0.7 1.4 %copy-start.3 = (s32[1,1,4,512]{3,2,1,0:T(4,128)S(1)}, s32[1,1,4,512]{3,2,1,0:T(4,128)}, u32[]{:S(2)}) copy-start(s32[1,1,4,512]{3,2,1,0:T(4,128)} %param.20) | copy-start | bytes 24580
  1.3 0.7 %copy-start.11 = (s32[1,1,4]{2,1,0:T(1,128)S(1)}, s32[1,1,4]{2,1,0:T(1,128)}, u32[]{:S(2)}) copy-start(s32[1,1,4]{2,1,0:T(1,128)} %param.21) | copy-start | bytes 52
  1.3 0.7 %copy-start.12 = (s32[6]{0:T(128)S(1)}, s32[6]{0:T(128)}, u32[]{:S(2)}) copy-start(s32[6]{0:T(128)} %constant.41.clone) | copy-start | bytes 76
  2.1 0.7 %copy-start.4 = (s32[1,1,2,256]{3,2,1,0:T(2,128)S(1)}, s32[1,1,2,256]{3,2,1,0:T(2,128)}, u32[]{:S(2)}) copy-start(s32[1,1,2,256]{3,2,1,0:T(2,128)} %param.22) | copy-start | bytes 6148
  2.7 0.9 %copy-start = (f32[64,1024]{1,0:T(8,128)S(1)}, f32[64,1024]{1,0:T(8,128)}, u32[]{:S(2)}) copy-start(f32[64,1024]{1,0:T(8,128)} %density_ref.3) | copy-start | bytes 786436
  3.7 14.7 %copy-start.2 = (s32[27,1024]{1,0:T(8,128)S(1)}, s32[27,1024]{1,0:T(8,128)}, u32[]{:S(2)}) copy-start(s32[27,1024]{1,0:T(8,128)} %links_ref.5) | copy-start | bytes 331780
  3.7 14.7 %copy-start.6 = (bf16[400,192]{1,0:T(8,128)(2,1)S(1)}, bf16[400,192]{1,0:T(8,128)(2,1)}, u32[]{:S(2)}) copy-start(bf16[400,192]{1,0:T(8,128)(2,1)} %constant.32.clone.fold_ref) | copy-start | bytes 460804
  3.7 14.7 %copy-start.8 = (bf16[64,288]{1,0:T(8,128)(2,1)S(1)}, bf16[64,288]{1,0:T(8,128)(2,1)}, u32[]{:S(2)}) copy-start(bf16[64,288]{1,0:T(8,128)(2,1)} %constant.35.clone.join_ref) | copy-start | bytes 110596
  3.7 14.7 %copy-start.9 = (bf16[64,192]{1,0:T(8,128)(2,1)S(1)}, bf16[64,192]{1,0:T(8,128)(2,1)}, u32[]{:S(2)}) copy-start(bf16[64,192]{1,0:T(8,128)(2,1)} %constant.34.clone.own_ref) | copy-start | bytes 73732
  3.7 14.7 %copy-start.10 = (bf16[64,54]{1,0:T(8,128)(2,1)S(1)}, bf16[64,54]{1,0:T(8,128)(2,1)}, u32[]{:S(2)}) copy-start(bf16[64,54]{1,0:T(8,128)(2,1)} %constant.37.clone.sums_ref) | copy-start | bytes 20740
  5.3 12.3 %collective-permute-start.4 = (f32[64,256]{1,0:T(8,128)S(1)}, f32[64,256]{1,0:T(8,128)S(1)}, u32[]{:S(2)}, u32[]{:S(2)}) collective-permute-start(f32[64,256]{1,0:T(8,128)S(1)} %get-tuple-element.22), channel_id=1, source_target_pairs={{0,1},{1,2},{2,3},{3,4},{4,5},{5,6},{6,7},{7,0},{8,9},{9,10},{10,1... | collective-permute-start | bytes 196616 | tf_op jit(solution)/shard_map/ppermute | solution.py:445
  5.3 18.1 %collective-permute-start.5 = (f32[64,256]{1,0:T(8,128)S(1)}, f32[64,256]{1,0:T(8,128)S(1)}, u32[]{:S(2)}, u32[]{:S(2)}) collective-permute-start(f32[64,256]{1,0:T(8,128)S(1)} %get-tuple-element.23), channel_id=1, source_target_pairs={{0,7},{1,0},{2,1},{3,2},{4,3},{5,4},{6,5},{7,6},{8,15},{9,8},{10,9... | collective-permute-start | bytes 196616 | tf_op jit(solution)/shard_map/ppermute | solution.py:445
  7.1 16.3 %collective-permute-start = (f32[64,512]{1,0:T(8,128)S(1)}, f32[64,512]{1,0:T(8,128)S(1)}, u32[]{:S(2)}, u32[]{:S(2)}) collective-permute-start(f32[64,512]{1,0:T(8,128)S(1)} %get-tuple-element.18), channel_id=1, source_target_pairs={{0,240},{8,248},{16,0},{24,8},{32,16},{40,24},{48,32},{56,40},{64,... | collective-permute-start | bytes 393224 | tf_op jit(solution)/shard_map/ppermute | solution.py:445
  15.6 8.5 %collective-permute-start.1 = (f32[64,512]{1,0:T(8,128)S(1)}, f32[64,512]{1,0:T(8,128)S(1)}, u32[]{:S(2)}, u32[]{:S(2)}) collective-permute-start(f32[64,512]{1,0:T(8,128)S(1)} %get-tuple-element.19), channel_id=1, source_target_pairs={{0,248},{8,0},{16,8},{24,16},{32,24},{40,32},{48,40},{56,48},{64,5... | collective-permute-start | bytes 393224 | tf_op jit(solution)/shard_map/ppermute | solution.py:445
  16.6 11.2 %collective-permute-start.2 = (f32[64,512]{1,0:T(8,128)S(1)}, f32[64,512]{1,0:T(8,128)S(1)}, u32[]{:S(2)}, u32[]{:S(2)}) collective-permute-start(f32[64,512]{1,0:T(8,128)S(1)} %get-tuple-element.20), channel_id=1, source_target_pairs={{0,8},{8,16},{16,24},{24,32},{32,40},{40,48},{48,56},{56,64},{64,7... | collective-permute-start | bytes 393224 | tf_op jit(solution)/shard_map/ppermute | solution.py:445
  17.6 11.9 %copy-start.1 = (f32[64,1024]{1,0:T(8,128)S(1)}, f32[64,1024]{1,0:T(8,128)}, u32[]{:S(2)}) copy-start(f32[64,1024]{1,0:T(8,128)} %energy_ref.1) | copy-start | bytes 786436
  17.6 11.9 %copy-start.5 = (bf16[512,192]{1,0:T(8,128)(2,1)S(1)}, bf16[512,192]{1,0:T(8,128)(2,1)}, u32[]{:S(2)}) copy-start(bf16[512,192]{1,0:T(8,128)(2,1)} %constant.33.clone.fold_b_ref) | copy-start | bytes 589828
  17.6 11.9 %copy-start.7 = (bf16[128,384]{1,0:T(8,128)(2,1)S(1)}, bf16[128,384]{1,0:T(8,128)(2,1)}, u32[]{:S(2)}) copy-start(bf16[128,384]{1,0:T(8,128)(2,1)} %constant.36.clone.join_b_ref) | copy-start | bytes 294916
  17.6 11.9 %collective-permute-start.3 = (f32[64,512]{1,0:T(8,128)S(1)}, f32[64,512]{1,0:T(8,128)S(1)}, u32[]{:S(2)}, u32[]{:S(2)}) collective-permute-start(f32[64,512]{1,0:T(8,128)S(1)} %get-tuple-element.21), channel_id=1, source_target_pairs={{0,16},{8,24},{16,32},{24,40},{32,48},{40,56},{48,64},{56,72},{64,... | collective-permute-start | bytes 393224 | tf_op jit(solution)/shard_map/ppermute | solution.py:445
  43.7 8.9 %collective-permute-start.10 = (f32[64,256]{1,0:T(8,128)S(1)}, f32[64,256]{1,0:T(8,128)S(1)}, u32[]{:S(2)}, u32[]{:S(2)}) collective-permute-start(f32[64,256]{1,0:T(8,128)S(1)} %get-tuple-element.32), channel_id=1, source_target_pairs={{0,1},{1,2},{2,3},{3,4},{4,5},{5,6},{6,7},{7,0},{8,9},{9,10},{10,1... | collective-permute-start | bytes 196616 | tf_op jit(solution)/shard_map/ppermute | solution.py:445
  43.7 15.2 %collective-permute-start.11 = (f32[64,256]{1,0:T(8,128)S(1)}, f32[64,256]{1,0:T(8,128)S(1)}, u32[]{:S(2)}, u32[]{:S(2)}) collective-permute-start(f32[64,256]{1,0:T(8,128)S(1)} %get-tuple-element.33), channel_id=1, source_target_pairs={{0,7},{1,0},{2,1},{3,2},{4,3},{5,4},{6,5},{7,6},{8,15},{9,8},{10,9... | collective-permute-start | bytes 196616 | tf_op jit(solution)/shard_map/ppermute | solution.py:445
  45.4 13.4 %collective-permute-start.6 = (f32[64,512]{1,0:T(8,128)S(1)}, f32[64,512]{1,0:T(8,128)S(1)}, u32[]{:S(2)}, u32[]{:S(2)}) collective-permute-start(f32[64,512]{1,0:T(8,128)S(1)} %get-tuple-element.28), channel_id=1, source_target_pairs={{0,16},{8,24},{16,32},{24,40},{32,48},{40,56},{48,64},{56,72},{64,... | collective-permute-start | bytes 393224 | tf_op jit(solution)/shard_map/ppermute | solution.py:445
  45.4 15.6 %collective-permute-start.7 = (f32[64,512]{1,0:T(8,128)S(1)}, f32[64,512]{1,0:T(8,128)S(1)}, u32[]{:S(2)}, u32[]{:S(2)}) collective-permute-start(f32[64,512]{1,0:T(8,128)S(1)} %get-tuple-element.29), channel_id=1, source_target_pairs={{0,8},{8,16},{16,24},{24,32},{32,40},{40,48},{48,56},{56,64},{64,7... | collective-permute-start | bytes 393224 | tf_op jit(solution)/shard_map/ppermute | solution.py:445
  47.7 13.3 %collective-permute-start.8 = (f32[64,512]{1,0:T(8,128)S(1)}, f32[64,512]{1,0:T(8,128)S(1)}, u32[]{:S(2)}, u32[]{:S(2)}) collective-permute-start(f32[64,512]{1,0:T(8,128)S(1)} %get-tuple-element.30), channel_id=1, source_target_pairs={{0,248},{8,0},{16,8},{24,16},{32,24},{40,32},{48,40},{56,48},{64,5... | collective-permute-start | bytes 393224 | tf_op jit(solution)/shard_map/ppermute | solution.py:445
  52.5 8.5 %collective-permute-start.9 = (f32[64,512]{1,0:T(8,128)S(1)}, f32[64,512]{1,0:T(8,128)S(1)}, u32[]{:S(2)}, u32[]{:S(2)}) collective-permute-start(f32[64,512]{1,0:T(8,128)S(1)} %get-tuple-element.31), channel_id=1, source_target_pairs={{0,240},{8,248},{16,0},{24,8},{32,16},{40,24},{48,32},{56,40},{64,... | collective-permute-start | bytes 393224 | tf_op jit(solution)/shard_map/ppermute | solution.py:445

commit v3 on v1

v3 whole, which is shorter than its diff:
```python
import jax
import jax.numpy as jnp
import numpy as np
from jax import lax
from jax.experimental import pallas as pl
from jax.experimental.pallas import tpu as pltpu
from jax.sharding import PartitionSpec as P

REACH = 2
TILE = 256
OFFSETS = [offset for offset in range(-REACH, REACH + 1) if offset != 0]
OUTWARD = (2, 3, 1, 0)
BACKWARD = (0, 1, 2, 3)
LANE_LOCAL = 6
LANE_REMOTE = 2
radius = 3.0
floor_value = 0.001
penalty = 3.0

F32 = jnp.float32
BF16 = jnp.bfloat16

ORDERS = ((0, 1, 2), (2, 0, 1), (1, 2, 0))


def cone_table():
    voxels = np.arange(64)
    places = np.stack([voxels // 16, voxels // 4 % 4, voxels % 4], axis=-1)
    slots = np.arange(27)
    moved = np.stack([slots // 9 - 1, slots // 3 % 3 - 1, slots % 3 - 1], axis=-1) * 4
    apart = places[None, :, None, :] - places[None, None, :, :] - moved[:, None, None, :]
    squares = np.sum(apart * apart, axis=-1).astype(np.float32)
    return np.maximum(np.float32(0.0), np.float32(radius) - np.sqrt(squares))


def order_voxels(order):
    rows = np.arange(64)
    coords = np.zeros((3, 64), np.int64)
    coords[order[0]], coords[order[1]], coords[order[2]] = rows // 16, rows // 4 % 4, rows % 4
    return coords[0] * 16 + coords[1] * 4 + coords[2]


def slot_of(offset):
    return (offset[0] + 1) * 9 + (offset[1] + 1) * 3 + offset[2] + 1


def layout():
    faces, edges, corners = [], [], []
    for at, order in enumerate(ORDERS):
        for sign in (-1, 1):
            offset = [0, 0, 0]
            offset[order[0]] = sign
            faces.append((slot_of(offset), at, sign))
    for at, order in enumerate(ORDERS):
        for one in (-1, 1):
            for two in (-1, 1):
                offset = [0, 0, 0]
                offset[order[0]], offset[order[1]] = one, two
                edges.append((slot_of(offset), at, one, two))
    for a in (-1, 1):
        for b in (-1, 1):
            for c in (-1, 1):
                corners.append(slot_of((a, b, c)))
    return faces, edges, corners


FACES, EDGES, CORNERS = layout()
SLOTS = [f[0] for f in FACES] + [e[0] for e in EDGES] + CORNERS


def face_start(sign, forward):
    return 32 if (sign > 0) == forward else 0


def edge_starts(one, two, forward):
    first = 2 if (one > 0) == forward else 0
    second = 2 if (two > 0) == forward else 0
    return [(first + i) * 16 + second * 4 for i in range(2)]


def slot_rows(forward):
    voxels = [order_voxels(order) for order in ORDERS]
    out = []
    for slot, at, sign in FACES:
        start = face_start(sign, forward)
        out.append((slot, voxels[at][start : start + 32]))
    for slot, at, one, two in EDGES:
        rows = np.concatenate([voxels[at][s : s + 8] for s in edge_starts(one, two, forward)])
        out.append((slot, rows))
    return out


def pieces_np(table):
    high = table.astype(jnp.bfloat16)
    low = (table - high.astype(np.float32)).astype(jnp.bfloat16)
    return high, low


def three(table):
    high, low = pieces_np(table)
    return np.concatenate([high, low, high], axis=1)


def corner_rows(table, forward):
    out = []
    for slot in CORNERS:
        part = table[slot] if forward else table[slot].T
        counts = (part > 0).sum(axis=1)
        main = int(np.argmax(counts))
        rest = [int(v) for v in np.nonzero(counts)[0] if v != main]
        out.append((part, main, rest))
    return out


def constants():
    table = cone_table()
    fold_fwd = [table[slot][rows] for slot, rows in slot_rows(True)]
    fold_bwd = [table[slot].T[rows] for slot, rows in slot_rows(False)]
    cor_fwd, cor_bwd = corner_rows(table, True), corner_rows(table, False)
    fold_fwd += [np.stack([part[main] for part, main, rest in cor_fwd])]
    fold_fwd += [np.stack([part[rest[0]] for part, main, rest in cor_fwd])]
    for part, main, rest in cor_bwd:
        fold_bwd += [np.tile(np.stack([part[main], part[rest[0]]]), (8, 1))]
    spots = []
    for at in (1, 2):
        spot = np.zeros((64, 64), np.float32)
        spot[order_voxels(ORDERS[at]), np.arange(64)] = 1
        spots.append(spot)
    cf = np.zeros((64, 16), np.float32)
    for m, (part, main, rest) in enumerate(cor_fwd):
        cf[main, m] = 1
        cf[rest, 8 + m] = 1
    join_fwd = np.concatenate(spots + [cf], axis=1)
    join_fwd = np.concatenate([join_fwd, join_fwd], axis=1).astype(jnp.bfloat16)
    joins = []
    for parity in range(2):
        cb = np.zeros((64, 64), np.float32)
        for m, (part, main, rest) in enumerate(cor_bwd):
            for piece in range(2):
                cb[main, m * 8 + parity * 4 + piece * 2] = 1
                cb[rest, m * 8 + parity * 4 + piece * 2 + 1] = 1
        join = np.concatenate(spots + [cb], axis=1)
        joins.append(np.concatenate([join, join], axis=1))
    sums = table.sum(axis=2).T
    high, low = pieces_np(sums)
    return dict(
        fold_fwd=three(np.concatenate(fold_fwd)),
        fold_bwd=three(np.concatenate(fold_bwd)),
        own=three(table[13]),
        own_t=three(table[13].T),
        join_fwd=join_fwd,
        join_bwd=np.concatenate(joins).astype(jnp.bfloat16),
        sums=np.concatenate([high, low], axis=1),
    )


def split2(value):
    high = value.astype(BF16)
    return high, (value - high.astype(F32)).astype(BF16)


def pieces(value):
    high, low = split2(value)
    return jnp.concatenate([high, high, low], axis=0)


def dot(a, b):
    return jnp.dot(a, b, preferred_element_type=F32)


def dot_nt(a, b):
    return lax.dot_general(a, b, (((1,), (1,)), ((), ())), preferred_element_type=F32)


def one_hot(low):
    shape = (TILE, low.shape[1])
    low = low.astype(jnp.int16)
    hit = lax.broadcasted_iota(jnp.int16, shape, 0) == jnp.broadcast_to(low, shape)
    return jnp.where(hit, jnp.array(1, BF16), jnp.array(0, BF16))


def gather_filtered(chunks, ids, lane_edges, links_ref, fold_ref, join_ref, tf, te, yc):
    count = len(chunks)
    faces, edges = len(FACES), len(EDGES)
    blocks = links_ref.shape[1]
    cut = 192 + (edges - lane_edges) * 16
    for h, chunk in enumerate(chunks):
        y = dot(fold_ref[...], pieces(chunk))
        high, low = split2(y[:cut])
        for f in range(faces):
            tf[f, h * 32 : h * 32 + 32, 0:TILE] = high[f * 32 : f * 32 + 32]
            tf[f, h * 32 : h * 32 + 32, TILE : 2 * TILE] = low[f * 32 : f * 32 + 32]
        for e in range(edges - lane_edges):
            at = 192 + e * 16
            te[e, h * 16 : h * 16 + 16, 0:TILE] = high[at : at + 16]
            te[e, h * 16 : h * 16 + 16, TILE : 2 * TILE] = low[at : at + 16]
        yc[:, h * TILE : h * TILE + TILE] = y[cut:400]

    def by_matmul(slot, table, rows):
        out = []
        for nb in range(blocks // TILE):
            idx = links_ref[slot : slot + 1, nb * TILE : nb * TILE + TILE]
            hot = one_hot(idx & (TILE - 1))
            upper = jnp.broadcast_to(idx >> 8, (rows, TILE))
            got = dot(table[:, 0:TILE], hot) + dot(table[:, TILE : 2 * TILE], hot)
            acc = jnp.zeros((rows, TILE), F32)
            for h in range(count):
                acc = jnp.where(upper == ids[h], got[h * rows : h * rows + rows], acc)
            out.append(acc)
        return jnp.concatenate(out, axis=1)

    def by_lanes(index_of, at, groups):
        out = [[] for _ in range(groups)]
        for bg in range(blocks // 128):
            idx = index_of(slice(bg * 128, bg * 128 + 128))
            low, upper = idx & 127, idx >> 7
            acc = [jnp.zeros((8, 128), F32) for _ in range(groups)]
            for h in range(2 * count):
                hit = upper == 2 * ids[h // 2] + h % 2
                for c in range(groups):
                    rows = slice(at + c * 8, at + c * 8 + 8)
                    got = jnp.take_along_axis(yc[rows, h * 128 : h * 128 + 128], low, axis=1)
                    acc[c] = jnp.where(hit, got, acc[c])
            for c in range(groups):
                out[c].append(acc[c])
        return jnp.concatenate([jnp.concatenate(c, axis=1) for c in out], axis=0)

    def edge_lanes(e):
        slot = EDGES[e][0]
        at = (e - edges + lane_edges) * 16
        return by_lanes(
            lambda cols: jnp.broadcast_to(links_ref[slot : slot + 1, cols], (8, 128)), at, 2
        )

    def corner_index(cols):
        return jnp.concatenate([links_ref[slot : slot + 1, cols] for slot in CORNERS], axis=0)

    lanes = [(edge_lanes, e) for e in range(edges - lane_edges, edges)]
    lanes.append((lambda _: by_lanes(corner_index, lane_edges * 16, 2), "corner"))
    matmuls = [(FACES[f][0], tf.at[f], 32, f) for f in range(faces)]
    matmuls += [(EDGES[e][0], te.at[e], 16, faces + e) for e in range(edges - lane_edges)]
    found = {}
    done = 0
    for i, (slot, table, rows, name) in enumerate(matmuls):
        found[name] = by_matmul(slot, table, rows)
        while done < len(lanes) and done * len(matmuls) <= i * len(lanes):
            fn, e = lanes[done]
            found[e if e == "corner" else faces + e] = fn(e)
            done += 1
    for fn, e in lanes[done:]:
        found[e if e == "corner" else faces + e] = fn(e)
    totals = order_totals(lambda f: found[f], lambda e: found[faces + e], True)
    high, low = split2(jnp.concatenate([totals[1], totals[2], found["corner"]], axis=0))
    return totals[0] + dot(join_ref[...], jnp.concatenate([high, low], axis=0))


def order_totals(face, edge, forward):
    totals = []
    for at in range(3):
        runs = [None] * 8
        for f, (_, order, sign) in enumerate(FACES):
            if order == at:
                value, start = face(f), face_start(sign, forward)
                for i in range(4):
                    runs[start // 8 + i] = value[i * 8 : i * 8 + 8]
        for e, (_, order, one, two) in enumerate(EDGES):
            if order == at:
                value = edge(e)
                for i, start in enumerate(edge_starts(one, two, forward)):
                    runs[start // 8] = runs[start // 8] + value[i * 8 : i * 8 + 8]
        totals.append(jnp.concatenate(runs, axis=0))
    return totals


def scatter_back(scaled, ids, links_ref, fold_ref, join_ref):
    count = len(ids)
    blocks = links_ref.shape[1]
    spread = dot(fold_ref[...], pieces(scaled))

    quarter = lax.broadcasted_iota(jnp.int32, (16, blocks), 0) // 4
    quarters = []
    for q in range((count + 3) // 4):
        rows_for = jnp.full((16, blocks), -1, jnp.int32)
        for i, h in enumerate(ids[4 * q : 4 * q + 4]):
            rows_for = jnp.where(quarter == i, h, rows_for)
        quarters.append(rows_for)

    def one_slot(slot, value, rows):
        idx = links_ref[slot : slot + 1, :]
        hot = one_hot(idx & (TILE - 1))
        upper = idx >> 8
        parts = [value * (upper == h).astype(F32).astype(BF16) for h in ids]
        got = dot_nt(jnp.concatenate(parts, axis=0), hot)
        return [
            got[h * 2 * rows : h * 2 * rows + rows] + got[h * 2 * rows + rows : h * 2 * rows + 2 * rows]
            for h in range(count)
        ]

    def one_corner(m):
        idx = links_ref[CORNERS[m] : CORNERS[m] + 1, :]
        hot = one_hot(idx & (TILE - 1))
        upper = jnp.broadcast_to(idx >> 8, (16, blocks))
        is_high = lax.broadcasted_iota(jnp.int32, (16, blocks), 0) % 4 < 2
        part = spread[384 + m * 16 : 384 + m * 16 + 16]
        top = part.astype(BF16).astype(F32)
        value = jnp.where(is_high, top, part - top).astype(BF16)
        parts = [
            value * (upper == quarters[q]).astype(F32).astype(BF16) for q in range(len(quarters))
        ]
        return dot_nt(jnp.concatenate(parts, axis=0), hot)

    def both(at, rows):
        return jnp.concatenate(split2(spread[at : at + rows]), axis=0)

    faces = [one_slot(face[0], both(f * 32, 32), 32) for f, face in enumerate(FACES)]
    edges = [one_slot(edge[0], both(192 + e * 16, 16), 16) for e, edge in enumerate(EDGES)]
    corners = [one_corner(m) for m in range(len(CORNERS))]
    out = []
    for h in range(count):
        totals = order_totals(lambda f: faces[f][h], lambda e: edges[e][h], False)
        tops = [corner[h // 2 * 8 : h // 2 * 8 + 8] for corner in corners]
        high, low = split2(jnp.concatenate([totals[1], totals[2]] + tops, axis=0))
        join = join_ref[h % 2 * 64 : h % 2 * 64 + 64, :]
        out.append(totals[0] + dot(join, jnp.concatenate([high, low], axis=0)))
    return out


def chunk_ids(order, heads):
    out = []
    for g in order:
        out += [heads + 2 * g, heads + 2 * g + 1]
    return out + [heads + 8, heads + 9]


def list_uppers(order, live_ref, index_ref, face_ref):
    place, places = lax.axis_index("plane"), lax.axis_size("plane")
    level, levels = lax.axis_index("depth"), lax.axis_size("depth")
    out = []
    for g in order:
        offset = OFFSETS[g]
        idx = index_ref[0, 0, g : g + 1, :]
        target = place + offset
        live = jnp.where((target >= 0) & (target < places), live_ref[0, 0, g], 0)
        at = lax.broadcasted_iota(jnp.int32, idx.shape, 1)
        out.append((idx, jnp.where(at < live, idx >> 8, -1)))
    for side, by in enumerate((-1, 1)):
        idx = face_ref[0, 0, side : side + 1, :]
        target = level + by
        live = jnp.where((target >= 0) & (target < levels), idx.shape[1], 0)
        at = lax.broadcasted_iota(jnp.int32, idx.shape, 1)
        out.append((idx, jnp.where(at < live, idx >> 8, -1)))
    return out


def payload_kernel(live_hbm, density_hbm, index_hbm, face_hbm, *refs):
    outs = refs[:6]
    live_ref, density_ref, index_ref, face_ref, sems = refs[6:]
    copies = [
        pltpu.make_async_copy(source, target, sems.at[at])
        for at, (source, target) in enumerate(
            [(density_hbm, density_ref), (live_hbm, live_ref), (index_hbm, index_ref), (face_hbm, face_ref)]
        )
    ]
    for copy in copies:
        copy.start()
    for copy in copies:
        copy.wait()
    density = density_ref[...]
    high, low = split2(density)
    heads = density.shape[1] // TILE
    table = jnp.concatenate(
        [
            jnp.concatenate([p[:, h * TILE : h * TILE + TILE] for h in range(heads)], axis=0)
            for p in (high, low)
        ],
        axis=1,
    )
    for ref, (idx, upper) in zip(outs, list_uppers(OUTWARD, live_ref, index_ref, face_ref)):
        hot = one_hot(idx & (TILE - 1))
        got = dot(table[:, 0:TILE], hot) + dot(table[:, TILE : 2 * TILE], hot)
        upper = jnp.broadcast_to(upper, (64, idx.shape[1]))
        acc = jnp.zeros((64, idx.shape[1]), F32)
        for h in range(heads):
            acc = jnp.where(upper == h, got[h * 64 : h * 64 + 64], acc)
        ref[...] = acc


def local_kernel(
    density_ref, links_ref, fold_ref, join_ref, own_ref, sums_ref, part_ref, weight_ref, *scratch
):
    density = density_ref[...]
    heads = density.shape[1] // TILE
    chunks = [density[:, h * TILE : h * TILE + TILE] for h in range(heads)]
    part = gather_filtered(chunks, list(range(heads)), LANE_LOCAL, links_ref, fold_ref, join_ref, *scratch)
    part_ref[...] = part + dot(own_ref[...], pieces(density))
    valid = (links_ref[...] != 14 * TILE).astype(F32).astype(BF16)
    weight_ref[...] = dot(sums_ref[...], jnp.concatenate([valid, valid], axis=0))


def remote_kernel(
    r0, r1, r2, r3, low_ref, high_ref, links_ref, part_ref, weight_ref, energy_ref,
    fold_ref, join_ref, fold_b_ref, join_b_ref,
    cond_ref, scaled_ref, b0, b1, b2, b3, lb, ub, *scratch,
):
    heads = part_ref.shape[1] // TILE
    chunks = []
    for ref in (r0, r1, r2, r3, low_ref, high_ref):
        for at in range(0, ref.shape[1], TILE):
            chunks.append(ref[:, at : at + TILE])
    total = gather_filtered(chunks, chunk_ids(OUTWARD, heads), LANE_REMOTE, links_ref, fold_ref, join_ref, *scratch)
    weight = weight_ref[...]
    filtered = (part_ref[...] + total) / weight
    square = filtered * filtered
    cond_ref[...] = floor_value + square * filtered * (1.0 - floor_value)
    scaled = -penalty * (1.0 - floor_value) * square * energy_ref[...] / weight
    scaled_ref[...] = scaled
    back = scatter_back(scaled, chunk_ids(BACKWARD, heads), links_ref, fold_b_ref, join_b_ref)
    at = 0
    for ref in (b0, b1, b2, b3, lb, ub):
        for start in range(0, ref.shape[1], TILE):
            ref[:, start : start + TILE] = back[at]
            at += 1


def own_kernel(scaled_ref, links_ref, fold_b_ref, join_b_ref, own_ref, sens_ref):
    scaled = scaled_ref[...]
    heads = scaled.shape[1] // TILE
    back = scatter_back(scaled, list(range(heads)), links_ref, fold_b_ref, join_b_ref)
    sens_ref[...] = jnp.concatenate(back, axis=1) + dot(own_ref[...], pieces(scaled))


def final_kernel(live_ref, sens_ref, index_ref, face_ref, v0, v1, v2, v3, v4, v5, out_ref):
    heads = sens_ref.shape[1] // TILE
    total = jnp.zeros((heads * 128, TILE), F32)
    lists = list_uppers(BACKWARD, live_ref, index_ref, face_ref)
    for ref, (idx, upper) in zip((v0, v1, v2, v3, v4, v5), lists):
        hot = one_hot(idx & (TILE - 1))
        value = jnp.concatenate(split2(ref[...]), axis=0)
        parts = [value * (upper == h).astype(F32).astype(BF16) for h in range(heads)]
        total = total + dot_nt(jnp.concatenate(parts, axis=0), hot)
    for h in range(heads):
        cols = slice(h * TILE, h * TILE + TILE)
        both = total[h * 128 : h * 128 + 64] + total[h * 128 + 64 : h * 128 + 128]
        out_ref[:, cols] = sens_ref[:, cols] + both


def params():
    return pltpu.CompilerParams(vmem_limit_bytes=48 * 1024 * 1024)


def cost(us):
    return pl.CostEstimate(flops=int(us * 5e8), bytes_accessed=int(us * 2e6), transcendentals=0)


def gather_scratch(count, lane_edges):
    return [
        pltpu.VMEM((6, count * 32, 2 * TILE), BF16),
        pltpu.VMEM((12 - lane_edges, count * 16, 2 * TILE), BF16),
        pltpu.VMEM((16 + lane_edges * 16, count * TILE), F32),
    ]


def passed_along(shard, axis, by):
    count = lax.axis_size(axis)
    pairs = [(i, (i + by) % count) for i in range(count)]
    return lax.ppermute(shard, axis, pairs)


def on_device(density, energy, links, send_index, send_live, face_index):
    const = {name: jnp.asarray(value) for name, value in constants().items()}
    blocks = density.shape[1]
    capacity, face_count = send_index.shape[3], face_index.shape[3]
    whole = jax.ShapeDtypeStruct((64, blocks), F32)
    listed = jax.ShapeDtypeStruct((64, capacity), F32)
    faced = jax.ShapeDtypeStruct((64, face_count), F32)
    vmem = pl.BlockSpec(memory_space=pltpu.VMEM)
    smem = pl.BlockSpec(memory_space=pltpu.SMEM)

    loads = pl.pallas_call(
        payload_kernel,
        out_shape=[listed] * 4 + [faced] * 2,
        in_specs=[pl.BlockSpec(memory_space=pl.ANY)] * 4,
        out_specs=[vmem] * 6,
        scratch_shapes=[
            pltpu.SMEM(send_live.shape, jnp.int32),
            pltpu.VMEM(density.shape, F32),
            pltpu.VMEM(send_index.shape, jnp.int32),
            pltpu.VMEM(face_index.shape, jnp.int32),
            pltpu.SemaphoreType.DMA((4,)),
        ],
        compiler_params=pltpu.CompilerParams(vmem_limit_bytes=63 * 1024 * 1024),
        cost_estimate=cost(3),
    )(send_live, density, send_index, face_index)
    received = [passed_along(loads[at], "plane", OFFSETS[g]) for at, g in enumerate(OUTWARD)]
    from_low = passed_along(loads[5], "depth", 1)
    from_high = passed_along(loads[4], "depth", -1)
    part, weight = pl.pallas_call(
        local_kernel,
        out_shape=[whole, whole],
        in_specs=[vmem] * 6,
        out_specs=[vmem] * 2,
        scratch_shapes=gather_scratch(4, LANE_LOCAL),
        compiler_params=params(),
        cost_estimate=cost(8),
    )(density, links, const["fold_fwd"], const["join_fwd"], const["own"], const["sums"])
    conductivity, scaled, *groups_back = pl.pallas_call(
        remote_kernel,
        out_shape=[whole, whole] + [listed] * 4 + [faced] * 2,
        in_specs=[vmem] * 14,
        out_specs=[vmem] * 8,
        scratch_shapes=gather_scratch(10, LANE_REMOTE),
        compiler_params=params(),
        cost_estimate=cost(20),
    )(
        *received, from_low, from_high, links, part, weight, energy,
        const["fold_fwd"], const["join_fwd"], const["fold_bwd"], const["join_bwd"],
    )
    returned = [passed_along(groups_back[at], "plane", -OFFSETS[g]) for at, g in enumerate(BACKWARD)]
    to_one = passed_along(groups_back[4], "depth", -1)
    to_zero = passed_along(groups_back[5], "depth", 1)
    sens = pl.pallas_call(
        own_kernel,
        out_shape=whole,
        in_specs=[vmem] * 5,
        out_specs=vmem,
        compiler_params=params(),
        cost_estimate=cost(8),
    )(scaled, links, const["fold_bwd"], const["join_bwd"], const["own_t"])
    sens = pl.pallas_call(
        final_kernel,
        out_shape=whole,
        in_specs=[smem] + [vmem] * 9,
        out_specs=vmem,
        compiler_params=params(),
        cost_estimate=cost(3),
    )(send_live, sens, send_index, face_index, *returned, to_zero, to_one)
    return (conductivity, sens)


def solution(mesh):
    in_specs = (
        P(None, ("plane", "depth")),
        P(None, ("plane", "depth")),
        P(None, ("plane", "depth")),
        P("plane", "depth", None, None),
        P("plane", "depth", None),
        P("plane", "depth", None, None),
    )
    out_specs = (P(None, ("plane", "depth")), P(None, ("plane", "depth")))
    return jax.shard_map(
        on_device, mesh=mesh, in_specs=in_specs, out_specs=out_specs, check_vma=False
    )
```

time: 91.3 us -> 54.8 us (0.60)
  the two profiles are of different devices: /device:TPU:14 before, /device:TPU:8 now
where the time goes in v3:
time: 54.8 us; the launch traced here: 54.7 us
  Pallas kernels  23.5 us (43%)
  starting transfers between devices  23 us (42%)
  waiting for transfers between devices  7.29 us (13%)
  between operations  0.79 us (1%)
    ppermute x12, starting transfers between devices, passed_along(): return lax.ppermute(shard, axis, pairs)  23 us
    pallas_call x1, Pallas kernels, on_device(): pl.pallas_call(remote_kernel, out_shape=[whole, whole] + [listed] * 4 + [...  11.6 us
    ppermute x12, waiting for transfers between devices, passed_along(): return lax.ppermute(shard, axis, pairs)  7.29 us
    pallas_call x1, Pallas kernels, on_device(): pl.pallas_call(own_kernel, out_shape=whole, in_specs=[vmem] * 5, out_spec...  4.55 us
    pallas_call x1, Pallas kernels, on_device(): pl.pallas_call(local_kernel, out_shape=[whole, whole], in_specs=[vmem] *...  2.63 us
    pallas_call x1, Pallas kernels, on_device(): pl.pallas_call(payload_kernel, out_shape=[listed] * 4 + [faced] * 2, in_s...  2.59 us
    pallas_call x1, Pallas kernels, on_device(): pl.pallas_call(final_kernel, out_shape=whole, in_specs=[smem] + [vmem] *...  2.13 us
  transfers between devices with their start and end apart: 12, of which 4 were waited for; matrix products, arithmetic and copies ran while one was open for 0% of the time, Pallas kernels for 13%

profile of v3, /device:TPU:8, one launch (start us, length us, event | category | flops | bytes accessed | tf_op | source)
XLA Modules:
  0.0 54.7 jit_solution(3734717322867565194)
XLA Ops:
  0.6 0.0 copy-start.7
  0.6 0.0 copy-start.9
  0.7 0.0 copy-start.10
  0.7 0.0 copy-start.11
  0.7 0.0 copy-start
  0.7 0.0 copy-start.2
  0.7 2.6 %shard_map.140 = (f32[64,512]{1,0:T(8,128)}, f32[64,512]{1,0:T(8,128)}, f32[64,512]{1,0:T(8,128)}, f32[64,512]{1,0:T(8,128)}, f32[64,256]{1,0:T(8,128)}, /*index=5*/f32[64,256]{1,0:T(8,128)}) custom-call(s32[1,1,4]{2,1,0:T(1,128)} %live_ref.1, f32[64,1024]{1,0:T(8,128)} %density_ref.1, s32[1,1,4,512]{3,2,1,0:T(4,128)} %index_ref.1, s32[1,1,2,256]{3,2,1,0:T(2,128)} %face_ref.1), custom_call_target="tpu_custom_call" | custom-call | flops 1500000000 | bytes 6000000 | tf_op jit(solution)/shard_map/pallas_call | solution.py:479
  3.3 0.0 collective-permute-start.4
  3.3 1.7 %collective-permute-start.5 = (f32[64,256]{1,0:T(8,128)}, f32[64,256]{1,0:T(8,128)S(1)}, u32[]{:S(2)}, u32[]{:S(2)}) collective-permute-start(f32[64,256]{1,0:T(8,128)} %get-tuple-element.23), channel_id=1, source_target_pairs={{0,7},{1,0},{2,1},{3,2},{4,3},{5,4},{6,5},{7,6},{8,15},{9,8},{10,9... | collective-permute-start | bytes 196616 | tf_op jit(solution)/shard_map/ppermute | solution.py:466
  5.1 1.9 %collective-permute-start = (f32[64,512]{1,0:T(8,128)}, f32[64,512]{1,0:T(8,128)S(1)}, u32[]{:S(2)}, u32[]{:S(2)}) collective-permute-start(f32[64,512]{1,0:T(8,128)} %get-tuple-element.18), channel_id=1, source_target_pairs={{0,8},{8,16},{16,24},{24,32},{32,40},{40,48},{48,56},{56,64},{64,7... | collective-permute-start | bytes 393224 | tf_op jit(solution)/shard_map/ppermute | solution.py:466
  7.0 3.3 %collective-permute-start.1 = (f32[64,512]{1,0:T(8,128)}, f32[64,512]{1,0:T(8,128)S(1)}, u32[]{:S(2)}, u32[]{:S(2)}) collective-permute-start(f32[64,512]{1,0:T(8,128)} %get-tuple-element.19), channel_id=1, source_target_pairs={{0,16},{8,24},{16,32},{24,40},{32,48},{40,56},{48,64},{56,72},{64,... | collective-permute-start | bytes 393224 | tf_op jit(solution)/shard_map/ppermute | solution.py:466
  10.2 3.4 %collective-permute-start.2 = (f32[64,512]{1,0:T(8,128)}, f32[64,512]{1,0:T(8,128)S(1)}, u32[]{:S(2)}, u32[]{:S(2)}) collective-permute-start(f32[64,512]{1,0:T(8,128)} %get-tuple-element.20), channel_id=1, source_target_pairs={{0,248},{8,0},{16,8},{24,16},{32,24},{40,32},{48,40},{56,48},{64,5... | collective-permute-start | bytes 393224 | tf_op jit(solution)/shard_map/ppermute | solution.py:466
  13.7 0.0 collective-permute-done.4.low_ref
  13.7 0.0 copy-start.1
  13.7 0.0 copy-start.6
  13.7 0.0 copy-start.8
  13.7 2.6 %collective-permute-start.3 = (f32[64,512]{1,0:T(8,128)}, f32[64,512]{1,0:T(8,128)S(1)}, u32[]{:S(2)}, u32[]{:S(2)}) collective-permute-start(f32[64,512]{1,0:T(8,128)} %get-tuple-element.21), channel_id=1, source_target_pairs={{0,240},{8,248},{16,0},{24,8},{32,16},{40,24},{48,32},{56,40},{64,... | collective-permute-start | bytes 393224 | tf_op jit(solution)/shard_map/ppermute | solution.py:466
  16.3 0.0 copy-done.7
  16.3 0.0 copy-done.9
  16.3 0.0 copy-done.10
  16.3 0.0 copy-done.11
  16.3 0.0 copy-done
  16.3 0.0 copy-done.2
  16.3 2.6 %shard_map.141 = (f32[64,1024]{1,0:T(8,128)S(1)}, f32[64,1024]{1,0:T(8,128)S(1)}) custom-call(f32[64,1024]{1,0:T(8,128)S(1)} %copy-done, s32[27,1024]{1,0:T(8,128)S(1)} %copy-done.2, bf16[400,192]{1,0:T(8,128)(2,1)S(1)} %copy-done.7, bf16[64,288]{1,0:T(8,128)(2,1)S(1)} %copy-done.9, bf16[64,192]{1,0:T(8,128)(2,1)S(1)} %copy-done.10, ...), custom_call_target="tpu_custom_call" | custom-call | flops 4000000000 | bytes 16000000 | tf_op jit(solution)/shard_map/pallas_call | solution.py:497
  19.0 0.0 collective-permute-done.5.high_ref
  19.0 0.0 collective-permute-done.r0
  19.0 2.7 %collective-permute-done.1.r1 = f32[64,512]{1,0:T(8,128)S(1)} collective-permute-done((f32[64,512]{1,0:T(8,128)}, f32[64,512]{1,0:T(8,128)S(1)}, u32[]{:S(2)}, u32[]{:S(2)}) %collective-permute-start.1) | collective-permute-done | bytes 131104 | tf_op jit(solution)/shard_map/ppermute | solution.py:466
  21.7 0.0 collective-permute-done.2.r2
  21.7 1.9 %collective-permute-done.3.r3 = f32[64,512]{1,0:T(8,128)S(1)} collective-permute-done((f32[64,512]{1,0:T(8,128)}, f32[64,512]{1,0:T(8,128)S(1)}, u32[]{:S(2)}, u32[]{:S(2)}) %collective-permute-start.3) | collective-permute-done | bytes 131104 | tf_op jit(solution)/shard_map/ppermute | solution.py:466
  23.6 0.0 copy-done.1
  23.6 0.0 copy-done.6
  23.6 0.0 copy-done.8
  23.6 11.6 %shard_map.142 = (f32[64,1024]{1,0:T(8,128)}, f32[64,1024]{1,0:T(8,128)S(1)}, f32[64,512]{1,0:T(8,128)S(1)}, f32[64,512]{1,0:T(8,128)S(1)}, f32[64,512]{1,0:T(8,...) custom-call(f32[64,512]{1,0:T(8,128)S(1)} %collective-permute-done.r0, ...), custom_call_target="tpu_custom_call" | custom-call | flops 10000000000 | bytes 40000000 | tf_op jit(solution)/shard_map/pallas_call | solution.py:506
  35.3 0.0 collective-permute-start.10
  35.3 1.7 %collective-permute-start.11 = (f32[64,256]{1,0:T(8,128)S(1)}, f32[64,256]{1,0:T(8,128)S(1)}, u32[]{:S(2)}, u32[]{:S(2)}) collective-permute-start(f32[64,256]{1,0:T(8,128)S(1)} %get-tuple-element.33), channel_id=1, source_target_pairs={{0,7},{1,0},{2,1},{3,2},{4,3},{5,4},{6,5},{7,6},{8,15},{9,8},{10,9... | collective-permute-start | bytes 196616 | tf_op jit(solution)/shard_map/ppermute | solution.py:466
  37.0 2.5 %collective-permute-start.6 = (f32[64,512]{1,0:T(8,128)S(1)}, f32[64,512]{1,0:T(8,128)S(1)}, u32[]{:S(2)}, u32[]{:S(2)}) collective-permute-start(f32[64,512]{1,0:T(8,128)S(1)} %get-tuple-element.28), channel_id=1, source_target_pairs={{0,16},{8,24},{16,32},{24,40},{32,48},{40,56},{48,64},{56,72},{64,... | collective-permute-start | bytes 393224 | tf_op jit(solution)/shard_map/ppermute | solution.py:466
  39.6 0.1 collective-permute-start.7
  39.6 5.3 %collective-permute-start.8 = (f32[64,512]{1,0:T(8,128)S(1)}, f32[64,512]{1,0:T(8,128)S(1)}, u32[]{:S(2)}, u32[]{:S(2)}) collective-permute-start(f32[64,512]{1,0:T(8,128)S(1)} %get-tuple-element.30), channel_id=1, source_target_pairs={{0,248},{8,0},{16,8},{24,16},{32,24},{40,32},{48,40},{56,48},{64,5... | collective-permute-start | bytes 393224 | tf_op jit(solution)/shard_map/ppermute | solution.py:466
  44.9 0.0 collective-permute-done.10.v4
  44.9 0.4 collective-permute-start.9
  45.3 0.0 copy-start.3
  45.3 0.0 copy-start.4
  45.3 0.0 copy-start.5
  45.3 4.5 %shard_map.143.sens_ref = f32[64,1024]{1,0:T(8,128)S(1)} custom-call(f32[64,1024]{1,0:T(8,128)S(1)} %get-tuple-element.27.scaled_ref, s32[27,1024]{1,0:T(8,128)S(1)} %copy-done.2, bf16[512,192]{1,0:T(8,128)(2,1)S(1)} %copy-done.6, bf16[128,384]{1,0:T(8,128)(2,1)S(1)} %copy-done.8, bf16[64,192]{1,0:T(8,128)(2,1)S(1)} %copy-done.10), custom_call_target="tpu_custom_call" | custom-call | flops 4000000000 | bytes 16000000 | tf_op jit(solution)/shard_map/pallas_call | solution.py:521
  49.9 0.0 collective-permute-done.11.v5
  49.9 0.0 collective-permute-done.6.v0
  49.9 1.0 %collective-permute-done.7.v1 = f32[64,512]{1,0:T(8,128)S(1)} collective-permute-done((f32[64,512]{1,0:T(8,128)S(1)}, f32[64,512]{1,0:T(8,128)S(1)}, u32[]{:S(2)}, u32[]{:S(2)}) %collective-permute-start.7) | collective-permute-done | bytes 131104 | tf_op jit(solution)/shard_map/ppermute | solution.py:466
  50.9 0.0 collective-permute-done.8.v2
  50.9 1.7 %collective-permute-done.9.v3 = f32[64,512]{1,0:T(8,128)S(1)} collective-permute-done((f32[64,512]{1,0:T(8,128)S(1)}, f32[64,512]{1,0:T(8,128)S(1)}, u32[]{:S(2)}, u32[]{:S(2)}) %collective-permute-start.9) | collective-permute-done | bytes 131104 | tf_op jit(solution)/shard_map/ppermute | solution.py:466
  52.6 0.0 copy-done.3
  52.6 0.0 copy-done.4
  52.6 0.0 copy-done.5
  52.6 2.1 %shard_map.144 = f32[64,1024]{1,0:T(8,128)} custom-call(s32[1,1,4]{2,1,0:T(1,128)S(1)} %copy-done.5, f32[64,1024]{1,0:T(8,128)S(1)} %shard_map.143.sens_ref, s32[1,1,4,512]{3,2,1,0:T(4,128)S(1)} %copy-done.3, s32[1,1,2,256]{3,2,1,0:T(2,128)S(1)} %copy-done.4, f32[64,512]{1,0:T(8,128)S(1)} %collective-permute-done.6.v0, ...), custom_call_target="tpu_custom_call" | custom-call | flops 1500000000 | bytes 6000000 | tf_op jit(solution)/shard_map/pallas_call | solution.py:529
Async XLA Ops:
  0.6 15.7 %copy-start.7 = (bf16[400,192]{1,0:T(8,128)(2,1)S(1)}, bf16[400,192]{1,0:T(8,128)(2,1)}, u32[]{:S(2)}) copy-start(bf16[400,192]{1,0:T(8,128)(2,1)} %constant.12.clone.fold_ref) | copy-start | bytes 460804
  0.6 15.7 %copy-start.9 = (bf16[64,288]{1,0:T(8,128)(2,1)S(1)}, bf16[64,288]{1,0:T(8,128)(2,1)}, u32[]{:S(2)}) copy-start(bf16[64,288]{1,0:T(8,128)(2,1)} %constant.15.clone.join_ref) | copy-start | bytes 110596
  0.7 15.7 %copy-start.10 = (bf16[64,192]{1,0:T(8,128)(2,1)S(1)}, bf16[64,192]{1,0:T(8,128)(2,1)}, u32[]{:S(2)}) copy-start(bf16[64,192]{1,0:T(8,128)(2,1)} %constant.14.clone.own_ref) | copy-start | bytes 73732
  0.7 15.7 %copy-start.11 = (bf16[64,54]{1,0:T(8,128)(2,1)S(1)}, bf16[64,54]{1,0:T(8,128)(2,1)}, u32[]{:S(2)}) copy-start(bf16[64,54]{1,0:T(8,128)(2,1)} %constant.17.clone.sums_ref) | copy-start | bytes 20740
  0.7 15.6 %copy-start = (f32[64,1024]{1,0:T(8,128)S(1)}, f32[64,1024]{1,0:T(8,128)}, u32[]{:S(2)}) copy-start(f32[64,1024]{1,0:T(8,128)} %density_ref.1) | copy-start | bytes 786436
  0.7 15.6 %copy-start.2 = (s32[27,1024]{1,0:T(8,128)S(1)}, s32[27,1024]{1,0:T(8,128)}, u32[]{:S(2)}) copy-start(s32[27,1024]{1,0:T(8,128)} %links_ref.5) | copy-start | bytes 331780
  3.3 10.4 %collective-permute-start.4 = (f32[64,256]{1,0:T(8,128)}, f32[64,256]{1,0:T(8,128)S(1)}, u32[]{:S(2)}, u32[]{:S(2)}) collective-permute-start(f32[64,256]{1,0:T(8,128)} %get-tuple-element.22), channel_id=1, source_target_pairs={{0,1},{1,2},{2,3},{3,4},{4,5},{5,6},{6,7},{7,0},{8,9},{9,10},{10,1... | collective-permute-start | bytes 196616 | tf_op jit(solution)/shard_map/ppermute | solution.py:466
  3.3 15.7 %collective-permute-start.5 = (f32[64,256]{1,0:T(8,128)}, f32[64,256]{1,0:T(8,128)S(1)}, u32[]{:S(2)}, u32[]{:S(2)}) collective-permute-start(f32[64,256]{1,0:T(8,128)} %get-tuple-element.23), channel_id=1, source_target_pairs={{0,7},{1,0},{2,1},{3,2},{4,3},{5,4},{6,5},{7,6},{8,15},{9,8},{10,9... | collective-permute-start | bytes 196616 | tf_op jit(solution)/shard_map/ppermute | solution.py:466
  5.1 13.9 %collective-permute-start = (f32[64,512]{1,0:T(8,128)}, f32[64,512]{1,0:T(8,128)S(1)}, u32[]{:S(2)}, u32[]{:S(2)}) collective-permute-start(f32[64,512]{1,0:T(8,128)} %get-tuple-element.18), channel_id=1, source_target_pairs={{0,8},{8,16},{16,24},{24,32},{32,40},{40,48},{48,56},{56,64},{64,7... | collective-permute-start | bytes 393224 | tf_op jit(solution)/shard_map/ppermute | solution.py:466
  7.0 14.7 %collective-permute-start.1 = (f32[64,512]{1,0:T(8,128)}, f32[64,512]{1,0:T(8,128)S(1)}, u32[]{:S(2)}, u32[]{:S(2)}) collective-permute-start(f32[64,512]{1,0:T(8,128)} %get-tuple-element.19), channel_id=1, source_target_pairs={{0,16},{8,24},{16,32},{24,40},{32,48},{40,56},{48,64},{56,72},{64,... | collective-permute-start | bytes 393224 | tf_op jit(solution)/shard_map/ppermute | solution.py:466
  10.2 11.5 %collective-permute-start.2 = (f32[64,512]{1,0:T(8,128)}, f32[64,512]{1,0:T(8,128)S(1)}, u32[]{:S(2)}, u32[]{:S(2)}) collective-permute-start(f32[64,512]{1,0:T(8,128)} %get-tuple-element.20), channel_id=1, source_target_pairs={{0,248},{8,0},{16,8},{24,16},{32,24},{40,32},{48,40},{56,48},{64,5... | collective-permute-start | bytes 393224 | tf_op jit(solution)/shard_map/ppermute | solution.py:466
  13.7 9.9 %copy-start.1 = (f32[64,1024]{1,0:T(8,128)S(1)}, f32[64,1024]{1,0:T(8,128)}, u32[]{:S(2)}) copy-start(f32[64,1024]{1,0:T(8,128)} %energy_ref.1) | copy-start | bytes 786436
  13.7 9.9 %copy-start.6 = (bf16[512,192]{1,0:T(8,128)(2,1)S(1)}, bf16[512,192]{1,0:T(8,128)(2,1)}, u32[]{:S(2)}) copy-start(bf16[512,192]{1,0:T(8,128)(2,1)} %constant.13.clone.fold_b_ref) | copy-start | bytes 589828
  13.7 9.9 %copy-start.8 = (bf16[128,384]{1,0:T(8,128)(2,1)S(1)}, bf16[128,384]{1,0:T(8,128)(2,1)}, u32[]{:S(2)}) copy-start(bf16[128,384]{1,0:T(8,128)(2,1)} %constant.16.clone.join_b_ref) | copy-start | bytes 294916
  13.7 9.9 %collective-permute-start.3 = (f32[64,512]{1,0:T(8,128)}, f32[64,512]{1,0:T(8,128)S(1)}, u32[]{:S(2)}, u32[]{:S(2)}) collective-permute-start(f32[64,512]{1,0:T(8,128)} %get-tuple-element.21), channel_id=1, source_target_pairs={{0,240},{8,248},{16,0},{24,8},{32,16},{40,24},{48,32},{56,40},{64,... | collective-permute-start | bytes 393224 | tf_op jit(solution)/shard_map/ppermute | solution.py:466
  35.3 9.7 %collective-permute-start.10 = (f32[64,256]{1,0:T(8,128)S(1)}, f32[64,256]{1,0:T(8,128)S(1)}, u32[]{:S(2)}, u32[]{:S(2)}) collective-permute-start(f32[64,256]{1,0:T(8,128)S(1)} %get-tuple-element.32), channel_id=1, source_target_pairs={{0,1},{1,2},{2,3},{3,4},{4,5},{5,6},{6,7},{7,0},{8,9},{9,10},{10,1... | collective-permute-start | bytes 196616 | tf_op jit(solution)/shard_map/ppermute | solution.py:466
  35.3 14.6 %collective-permute-start.11 = (f32[64,256]{1,0:T(8,128)S(1)}, f32[64,256]{1,0:T(8,128)S(1)}, u32[]{:S(2)}, u32[]{:S(2)}) collective-permute-start(f32[64,256]{1,0:T(8,128)S(1)} %get-tuple-element.33), channel_id=1, source_target_pairs={{0,7},{1,0},{2,1},{3,2},{4,3},{5,4},{6,5},{7,6},{8,15},{9,8},{10,9... | collective-permute-start | bytes 196616 | tf_op jit(solution)/shard_map/ppermute | solution.py:466
  37.0 12.8 %collective-permute-start.6 = (f32[64,512]{1,0:T(8,128)S(1)}, f32[64,512]{1,0:T(8,128)S(1)}, u32[]{:S(2)}, u32[]{:S(2)}) collective-permute-start(f32[64,512]{1,0:T(8,128)S(1)} %get-tuple-element.28), channel_id=1, source_target_pairs={{0,16},{8,24},{16,32},{24,40},{32,48},{40,56},{48,64},{56,72},{64,... | collective-permute-start | bytes 393224 | tf_op jit(solution)/shard_map/ppermute | solution.py:466
  39.6 11.3 %collective-permute-start.7 = (f32[64,512]{1,0:T(8,128)S(1)}, f32[64,512]{1,0:T(8,128)S(1)}, u32[]{:S(2)}, u32[]{:S(2)}) collective-permute-start(f32[64,512]{1,0:T(8,128)S(1)} %get-tuple-element.29), channel_id=1, source_target_pairs={{0,8},{8,16},{16,24},{24,32},{32,40},{40,48},{48,56},{56,64},{64,7... | collective-permute-start | bytes 393224 | tf_op jit(solution)/shard_map/ppermute | solution.py:466
  39.6 11.3 %collective-permute-start.8 = (f32[64,512]{1,0:T(8,128)S(1)}, f32[64,512]{1,0:T(8,128)S(1)}, u32[]{:S(2)}, u32[]{:S(2)}) collective-permute-start(f32[64,512]{1,0:T(8,128)S(1)} %get-tuple-element.30), channel_id=1, source_target_pairs={{0,248},{8,0},{16,8},{24,16},{32,24},{40,32},{48,40},{56,48},{64,5... | collective-permute-start | bytes 393224 | tf_op jit(solution)/shard_map/ppermute | solution.py:466
  44.9 7.6 %collective-permute-start.9 = (f32[64,512]{1,0:T(8,128)S(1)}, f32[64,512]{1,0:T(8,128)S(1)}, u32[]{:S(2)}, u32[]{:S(2)}) collective-permute-start(f32[64,512]{1,0:T(8,128)S(1)} %get-tuple-element.31), channel_id=1, source_target_pairs={{0,240},{8,248},{16,0},{24,8},{32,16},{40,24},{48,32},{56,40},{64,... | collective-permute-start | bytes 393224 | tf_op jit(solution)/shard_map/ppermute | solution.py:466
  45.3 7.2 %copy-start.3 = (s32[1,1,4,512]{3,2,1,0:T(4,128)S(1)}, s32[1,1,4,512]{3,2,1,0:T(4,128)}, u32[]{:S(2)}) copy-start(s32[1,1,4,512]{3,2,1,0:T(4,128)} %index_ref.1) | copy-start | bytes 24580
  45.3 7.2 %copy-start.4 = (s32[1,1,2,256]{3,2,1,0:T(2,128)S(1)}, s32[1,1,2,256]{3,2,1,0:T(2,128)}, u32[]{:S(2)}) copy-start(s32[1,1,2,256]{3,2,1,0:T(2,128)} %face_ref.1) | copy-start | bytes 6148
  45.3 7.2 %copy-start.5 = (s32[1,1,4]{2,1,0:T(1,128)S(1)}, s32[1,1,4]{2,1,0:T(1,128)}, u32[]{:S(2)}) copy-start(s32[1,1,4]{2,1,0:T(1,128)} %live_ref.1) | copy-start | bytes 52

commit v4 on v3

--- a/solution.py
+++ b/solution.py
@@ -12,7 +12,8 @@
 OUTWARD = (2, 3, 1, 0)
 BACKWARD = (0, 1, 2, 3)
 LANE_LOCAL = 6
-LANE_REMOTE = 2
+LANE_EARLY = 5
+LANE_REMOTE = 6
 radius = 3.0
 floor_value = 0.001
 penalty = 3.0
@@ -272,10 +273,17 @@
     return totals
 
 
-def scatter_back(scaled, ids, links_ref, fold_ref, join_ref):
+def scatter_back(scaled, ids, kind, links_ref, fold_ref, join_ref):
     count = len(ids)
     blocks = links_ref.shape[1]
     spread = dot(fold_ref[...], pieces(scaled))
+    lows = jnp.transpose((links_ref[...] & (TILE - 1)).astype(F32))
+    lane = lax.broadcasted_iota(jnp.int32, (blocks, TILE), 1).astype(F32).astype(kind)
+
+    def hot_rows(slot):
+        low = jnp.broadcast_to(lows[:, slot : slot + 1], (blocks, TILE)).astype(kind)
+        return jnp.where(lane == low, jnp.array(1, kind), jnp.array(0, kind)).astype(BF16)
+
 
     quarter = lax.broadcasted_iota(jnp.int32, (16, blocks), 0) // 4
     quarters = []
@@ -287,10 +295,10 @@
 
     def one_slot(slot, value, rows):
         idx = links_ref[slot : slot + 1, :]
-        hot = one_hot(idx & (TILE - 1))
+        hot = hot_rows(slot)
         upper = idx >> 8
         parts = [value * (upper == h).astype(F32).astype(BF16) for h in ids]
-        got = dot_nt(jnp.concatenate(parts, axis=0), hot)
+        got = dot(jnp.concatenate(parts, axis=0), hot)
         return [
             got[h * 2 * rows : h * 2 * rows + rows] + got[h * 2 * rows + rows : h * 2 * rows + 2 * rows]
             for h in range(count)
@@ -298,7 +306,7 @@
 
     def one_corner(m):
         idx = links_ref[CORNERS[m] : CORNERS[m] + 1, :]
-        hot = one_hot(idx & (TILE - 1))
+        hot = hot_rows(CORNERS[m])
         upper = jnp.broadcast_to(idx >> 8, (16, blocks))
         is_high = lax.broadcasted_iota(jnp.int32, (16, blocks), 0) % 4 < 2
         part = spread[384 + m * 16 : 384 + m * 16 + 16]
@@ -307,7 +315,7 @@
         parts = [
             value * (upper == quarters[q]).astype(F32).astype(BF16) for q in range(len(quarters))
         ]
-        return dot_nt(jnp.concatenate(parts, axis=0), hot)
+        return dot(jnp.concatenate(parts, axis=0), hot)
 
     def both(at, rows):
         return jnp.concatenate(split2(spread[at : at + rows]), axis=0)
@@ -397,24 +405,32 @@
     weight_ref[...] = dot(sums_ref[...], jnp.concatenate([valid, valid], axis=0))
 
 
+def tile_chunks(refs):
+    return [ref[:, at : at + TILE] for ref in refs for at in range(0, ref.shape[1], TILE)]
+
+
+def early_kernel(r0, r1, low_ref, high_ref, links_ref, part_ref, fold_ref, join_ref, out_ref, *scratch):
+    ids = chunk_ids(OUTWARD, part_ref.shape[1] // TILE)
+    chunks = tile_chunks((r0, r1, low_ref, high_ref))
+    total = gather_filtered(chunks, ids[:4] + ids[8:], LANE_EARLY, links_ref, fold_ref, join_ref, *scratch)
+    out_ref[...] = part_ref[...] + total
+
+
 def remote_kernel(
-    r0, r1, r2, r3, low_ref, high_ref, links_ref, part_ref, weight_ref, energy_ref,
+    r0, r1, r2, r3, links_ref, part_ref, weight_ref, energy_ref,
     fold_ref, join_ref, fold_b_ref, join_b_ref,
     cond_ref, scaled_ref, b0, b1, b2, b3, lb, ub, *scratch,
 ):
     heads = part_ref.shape[1] // TILE
-    chunks = []
-    for ref in (r0, r1, r2, r3, low_ref, high_ref):
-        for at in range(0, ref.shape[1], TILE):
-            chunks.append(ref[:, at : at + TILE])
-    total = gather_filtered(chunks, chunk_ids(OUTWARD, heads), LANE_REMOTE, links_ref, fold_ref, join_ref, *scratch)
+    chunks = tile_chunks((r2, r3))
+    total = gather_filtered(chunks, chunk_ids(OUTWARD, heads)[4:8], LANE_REMOTE, links_ref, fold_ref, join_ref, *scratch)
     weight = weight_ref[...]
     filtered = (part_ref[...] + total) / weight
     square = filtered * filtered
     cond_ref[...] = floor_value + square * filtered * (1.0 - floor_value)
     scaled = -penalty * (1.0 - floor_value) * square * energy_ref[...] / weight
     scaled_ref[...] = scaled
-    back = scatter_back(scaled, chunk_ids(BACKWARD, heads), links_ref, fold_b_ref, join_b_ref)
+    back = scatter_back(scaled, chunk_ids(BACKWARD, heads), F32, links_ref, fold_b_ref, join_b_ref)
     at = 0
     for ref in (b0, b1, b2, b3, lb, ub):
         for start in range(0, ref.shape[1], TILE):
@@ -425,7 +441,7 @@
 def own_kernel(scaled_ref, links_ref, fold_b_ref, join_b_ref, own_ref, sens_ref):
     scaled = scaled_ref[...]
     heads = scaled.shape[1] // TILE
-    back = scatter_back(scaled, list(range(heads)), links_ref, fold_b_ref, join_b_ref)
+    back = scatter_back(scaled, list(range(heads)), BF16, links_ref, fold_b_ref, join_b_ref)
     sens_ref[...] = jnp.concatenate(back, axis=1) + dot(own_ref[...], pieces(scaled))
 
 
@@ -503,16 +519,25 @@
         compiler_params=params(),
         cost_estimate=cost(8),
     )(density, links, const["fold_fwd"], const["join_fwd"], const["own"], const["sums"])
+    part = pl.pallas_call(
+        early_kernel,
+        out_shape=whole,
+        in_specs=[vmem] * 8,
+        out_specs=vmem,
+        scratch_shapes=gather_scratch(6, LANE_EARLY),
+        compiler_params=params(),
+        cost_estimate=cost(4),
+    )(received[0], received[1], from_low, from_high, links, part, const["fold_fwd"], const["join_fwd"])
     conductivity, scaled, *groups_back = pl.pallas_call(
         remote_kernel,
         out_shape=[whole, whole] + [listed] * 4 + [faced] * 2,
-        in_specs=[vmem] * 14,
+        in_specs=[pl.BlockSpec(memory_space=pl.ANY)] * 2 + [vmem] * 10,
         out_specs=[vmem] * 8,
-        scratch_shapes=gather_scratch(10, LANE_REMOTE),
+        scratch_shapes=gather_scratch(4, LANE_REMOTE),
         compiler_params=params(),
         cost_estimate=cost(20),
     )(
-        *received, from_low, from_high, links, part, weight, energy,
+        *received, links, part, weight, energy,
         const["fold_fwd"], const["join_fwd"], const["fold_bwd"], const["join_bwd"],
     )
     returned = [passed_along(groups_back[at], "plane", -OFFSETS[g]) for at, g in enumerate(BACKWARD)]

time: 54.8 us -> 53.2 us (0.971)
  waiting for transfers between devices: 7.29 us -> 5.84 us
    pallas_call x0 -> x1, Pallas kernels: none -> 3.12 us  [on_device(): pl.pallas_call(early_kernel, out_shape=whole, in_specs=[vmem] * 8, out_sp...]
    pallas_call x1, Pallas kernels: 11.6 us -> 9.05 us  [on_device(): pl.pallas_call(remote_kernel, out_shape=[whole, whole] + [listed] * 4 + [...]
    ppermute x12, waiting for transfers between devices: 7.29 us -> 5.84 us  [passed_along(): return lax.ppermute(shard, axis, pairs)]
    pallas_call x1, Pallas kernels: 4.55 us -> 3.54 us  [on_device(): pl.pallas_call(own_kernel, out_shape=whole, in_specs=[vmem] * 5, out_spec...]
  transfers between devices with their start and end apart: 12 -> 12, of which waited for: 4 -> 3; matrix products, arithmetic and copies ran while one was open for 0% -> 0% of each run, Pallas kernels for 13% -> 17%
where the time goes in v4:
time: 53.2 us; the launch traced here: 53.1 us
  starting transfers between devices  23.3 us (44%)
  Pallas kernels  23.1 us (43%)
  waiting for transfers between devices  5.84 us (11%)
  between operations  0.84 us (2%)
    ppermute x12, starting transfers between devices, passed_along(): return lax.ppermute(shard, axis, pairs)  23.3 us
    pallas_call x1, Pallas kernels, on_device(): pl.pallas_call(remote_kernel, out_shape=[whole, whole] + [listed] * 4 + [...  9.05 us
    ppermute x12, waiting for transfers between devices, passed_along(): return lax.ppermute(shard, axis, pairs)  5.84 us
    pallas_call x1, Pallas kernels, on_device(): pl.pallas_call(own_kernel, out_shape=whole, in_specs=[vmem] * 5, out_spec...  3.54 us
    pallas_call x1, Pallas kernels, on_device(): pl.pallas_call(early_kernel, out_shape=whole, in_specs=[vmem] * 8, out_sp...  3.12 us
    pallas_call x1, Pallas kernels, on_device(): pl.pallas_call(local_kernel, out_shape=[whole, whole], in_specs=[vmem] *...  2.63 us
    pallas_call x1, Pallas kernels, on_device(): pl.pallas_call(payload_kernel, out_shape=[listed] * 4 + [faced] * 2, in_s...  2.59 us
    pallas_call x1, Pallas kernels, on_device(): pl.pallas_call(final_kernel, out_shape=whole, in_specs=[smem] + [vmem] *...  2.13 us
  transfers between devices with their start and end apart: 12, of which 3 were waited for; matrix products, arithmetic and copies ran while one was open for 0% of the time, Pallas kernels for 17%

profile of v4, /device:TPU:8, one launch (start us, length us, event | category | flops | bytes accessed | tf_op | source)
XLA Modules:
  0.0 53.1 jit_solution(12336937978525231098)
XLA Ops:
  0.6 0.0 copy-start.7
  0.6 0.0 copy-start.9
  0.7 0.0 copy-start.10
  0.7 0.0 copy-start.11
  0.7 0.0 copy-start
  0.7 0.0 copy-start.2
  0.7 2.6 %shard_map.140 = (f32[64,512]{1,0:T(8,128)}, f32[64,512]{1,0:T(8,128)}, f32[64,512]{1,0:T(8,128)}, f32[64,512]{1,0:T(8,128)}, f32[64,256]{1,0:T(8,128)}, /*index=5*/f32[64,256]{1,0:T(8,128)}) custom-call(s32[1,1,4]{2,1,0:T(1,128)} %live_ref.1, f32[64,1024]{1,0:T(8,128)} %density_ref.1, s32[1,1,4,512]{3,2,1,0:T(4,128)} %index_ref.1, s32[1,1,2,256]{3,2,1,0:T(2,128)} %face_ref.1), custom_call_target="tpu_custom_call" | custom-call | flops 1500000000 | bytes 6000000 | tf_op jit(solution)/shard_map/pallas_call | solution.py:495
  3.3 0.0 collective-permute-start.4
  3.3 1.7 %collective-permute-start.5 = (f32[64,256]{1,0:T(8,128)}, f32[64,256]{1,0:T(8,128)S(1)}, u32[]{:S(2)}, u32[]{:S(2)}) collective-permute-start(f32[64,256]{1,0:T(8,128)} %get-tuple-element.23), channel_id=1, source_target_pairs={{0,7},{1,0},{2,1},{3,2},{4,3},{5,4},{6,5},{7,6},{8,15},{9,8},{10,9... | collective-permute-start | bytes 196616 | tf_op jit(solution)/shard_map/ppermute | solution.py:482
  5.1 1.9 %collective-permute-start = (f32[64,512]{1,0:T(8,128)}, f32[64,512]{1,0:T(8,128)S(1)}, u32[]{:S(2)}, u32[]{:S(2)}) collective-permute-start(f32[64,512]{1,0:T(8,128)} %get-tuple-element.18), channel_id=1, source_target_pairs={{0,8},{8,16},{16,24},{24,32},{32,40},{40,48},{48,56},{56,64},{64,7... | collective-permute-start | bytes 393224 | tf_op jit(solution)/shard_map/ppermute | solution.py:482
  7.0 3.3 %collective-permute-start.1 = (f32[64,512]{1,0:T(8,128)}, f32[64,512]{1,0:T(8,128)S(1)}, u32[]{:S(2)}, u32[]{:S(2)}) collective-permute-start(f32[64,512]{1,0:T(8,128)} %get-tuple-element.19), channel_id=1, source_target_pairs={{0,16},{8,24},{16,32},{24,40},{32,48},{40,56},{48,64},{56,72},{64,... | collective-permute-start | bytes 393224 | tf_op jit(solution)/shard_map/ppermute | solution.py:482
  10.2 0.0 copy-start.12
  10.2 3.4 %collective-permute-start.2 = (f32[64,512]{1,0:T(8,128)}, f32[64,512]{1,0:T(8,128)S(1)}, u32[]{:S(2)}, u32[]{:S(2)}) collective-permute-start(f32[64,512]{1,0:T(8,128)} %get-tuple-element.20), channel_id=1, source_target_pairs={{0,248},{8,0},{16,8},{24,16},{32,24},{40,32},{48,40},{56,48},{64,5... | collective-permute-start | bytes 393224 | tf_op jit(solution)/shard_map/ppermute | solution.py:482
  13.7 0.0 copy-done.7
  13.7 0.0 copy-done.9
  13.7 0.0 copy-done.10
  13.7 0.0 copy-done.11
  13.7 0.0 copy-done
  13.7 0.0 copy-done.2
  13.7 2.6 %shard_map.141 = (f32[64,1024]{1,0:T(8,128)S(1)}, f32[64,1024]{1,0:T(8,128)S(1)}) custom-call(f32[64,1024]{1,0:T(8,128)S(1)} %copy-done, s32[27,1024]{1,0:T(8,128)S(1)} %copy-done.2, bf16[400,192]{1,0:T(8,128)(2,1)S(1)} %copy-done.7, bf16[64,288]{1,0:T(8,128)(2,1)S(1)} %copy-done.9, bf16[64,192]{1,0:T(8,128)(2,1)S(1)} %copy-done.10, ...), custom_call_target="tpu_custom_call" | custom-call | flops 4000000000 | bytes 16000000 | tf_op jit(solution)/shard_map/pallas_call | solution.py:513
  16.3 0.0 collective-permute-done.4.low_ref
  16.3 0.0 copy-done.12
  16.4 2.6 %collective-permute-start.3 = (f32[64,512]{1,0:T(8,128)S(1)}, f32[64,512]{1,0:T(8,128)S(1)}, u32[]{:S(2)}, u32[]{:S(2)}) collective-permute-start(f32[64,512]{1,0:T(8,128)S(1)} %copy-done.12), channel_id=1, source_target_pairs={{0,240},{8,248},{16,0},{24,8},{32,16},{40,24},{48,32},{56,40},{64,... | collective-permute-start | bytes 393224 | tf_op jit(solution)/shard_map/ppermute | solution.py:482
  19.0 0.0 collective-permute-done.5.high_ref
  19.0 0.0 collective-permute-done.r0
  19.0 2.7 %collective-permute-done.1.r1 = f32[64,512]{1,0:T(8,128)S(1)} collective-permute-done((f32[64,512]{1,0:T(8,128)}, f32[64,512]{1,0:T(8,128)S(1)}, u32[]{:S(2)}, u32[]{:S(2)}) %collective-permute-start.1) | collective-permute-done | bytes 131104 | tf_op jit(solution)/shard_map/ppermute | solution.py:482
  21.7 0.0 copy-start.1
  21.7 0.0 copy-start.6
  21.7 0.0 copy-start.8
  21.7 3.1 %shard_map.142.part_ref = f32[64,1024]{1,0:T(8,128)S(1)} custom-call(f32[64,512]{1,0:T(8,128)S(1)} %collective-permute-done.r0, f32[64,512]{1,0:T(8,128)S(1)} %collective-permute-done.1.r1, f32[64,256]{1,0:T(8,128)S(1)} %collective-permute-done.4.low_ref, f32[64,256]{1,0:T(8,128)S(1)} %collective-permute-done.5.high_ref, s32[27,1024]{1,0:T(8,128)S(1)} %copy-done.2, ...), custom_call_target="tpu_custom_call" | custom-call | flops 2000000000 | bytes 8000000 | tf_op jit(solution)/shard_map/pallas_call | solution.py:522
  24.9 0.0 collective-permute-done.2.r2
  24.9 0.0 collective-permute-done.3.r3
  24.9 0.0 copy-done.1
  24.9 0.0 copy-done.6
  24.9 0.0 copy-done.8
  24.9 9.0 %shard_map.143 = (f32[64,1024]{1,0:T(8,128)}, f32[64,1024]{1,0:T(8,128)S(1)}, f32[64,512]{1,0:T(8,128)S(1)}, f32[64,512]{1,0:T(8,128)S(1)}, f32[64,512]{1,0:T(8,...) custom-call(f32[64,512]{1,0:T(8,128)S(1)} %collective-permute-done.r0, ...), custom_call_target="tpu_custom_call" | custom-call | flops 10000000000 | bytes 40000000 | tf_op jit(solution)/shard_map/pallas_call | solution.py:531
  34.0 0.0 collective-permute-start.10
  34.0 1.7 %collective-permute-start.11 = (f32[64,256]{1,0:T(8,128)S(1)}, f32[64,256]{1,0:T(8,128)S(1)}, u32[]{:S(2)}, u32[]{:S(2)}) collective-permute-start(f32[64,256]{1,0:T(8,128)S(1)} %get-tuple-element.33), channel_id=1, source_target_pairs={{0,7},{1,0},{2,1},{3,2},{4,3},{5,4},{6,5},{7,6},{8,15},{9,8},{10,9... | collective-permute-start | bytes 196616 | tf_op jit(solution)/shard_map/ppermute | solution.py:482
  35.7 2.1 %collective-permute-start.6 = (f32[64,512]{1,0:T(8,128)S(1)}, f32[64,512]{1,0:T(8,128)S(1)}, u32[]{:S(2)}, u32[]{:S(2)}) collective-permute-start(f32[64,512]{1,0:T(8,128)S(1)} %get-tuple-element.28), channel_id=1, source_target_pairs={{0,16},{8,24},{16,32},{24,40},{32,48},{40,56},{48,64},{56,72},{64,... | collective-permute-start | bytes 393224 | tf_op jit(solution)/shard_map/ppermute | solution.py:482
  37.8 1.2 %collective-permute-start.7 = (f32[64,512]{1,0:T(8,128)S(1)}, f32[64,512]{1,0:T(8,128)S(1)}, u32[]{:S(2)}, u32[]{:S(2)}) collective-permute-start(f32[64,512]{1,0:T(8,128)S(1)} %get-tuple-element.29), channel_id=1, source_target_pairs={{0,8},{8,16},{16,24},{24,32},{32,40},{40,48},{48,56},{56,64},{64,7... | collective-permute-start | bytes 393224 | tf_op jit(solution)/shard_map/ppermute | solution.py:482
  39.1 4.1 %collective-permute-start.8 = (f32[64,512]{1,0:T(8,128)S(1)}, f32[64,512]{1,0:T(8,128)S(1)}, u32[]{:S(2)}, u32[]{:S(2)}) collective-permute-start(f32[64,512]{1,0:T(8,128)S(1)} %get-tuple-element.30), channel_id=1, source_target_pairs={{0,248},{8,0},{16,8},{24,16},{32,24},{40,32},{48,40},{56,48},{64,5... | collective-permute-start | bytes 393224 | tf_op jit(solution)/shard_map/ppermute | solution.py:482
  43.2 0.0 collective-permute-done.10.v4
  43.2 1.1 %collective-permute-start.9 = (f32[64,512]{1,0:T(8,128)S(1)}, f32[64,512]{1,0:T(8,128)S(1)}, u32[]{:S(2)}, u32[]{:S(2)}) collective-permute-start(f32[64,512]{1,0:T(8,128)S(1)} %get-tuple-element.31), channel_id=1, source_target_pairs={{0,240},{8,248},{16,0},{24,8},{32,16},{40,24},{48,32},{56,40},{64,... | collective-permute-start | bytes 393224 | tf_op jit(solution)/shard_map/ppermute | solution.py:482
  44.3 0.0 copy-start.3
  44.3 0.0 copy-start.4
  44.3 0.0 copy-start.5
  44.3 3.5 %shard_map.144.sens_ref = f32[64,1024]{1,0:T(8,128)S(1)} custom-call(f32[64,1024]{1,0:T(8,128)S(1)} %get-tuple-element.27.scaled_ref, s32[27,1024]{1,0:T(8,128)S(1)} %copy-done.2, bf16[512,192]{1,0:T(8,128)(2,1)S(1)} %copy-done.6, bf16[128,384]{1,0:T(8,128)(2,1)S(1)} %copy-done.8, bf16[64,192]{1,0:T(8,128)(2,1)S(1)} %copy-done.10), custom_call_target="tpu_custom_call" | custom-call | flops 4000000000 | bytes 16000000 | tf_op jit(solution)/shard_map/pallas_call | solution.py:546
  47.8 0.0 collective-permute-done.11.v5
  47.8 1.2 %collective-permute-done.6.v0 = f32[64,512]{1,0:T(8,128)S(1)} collective-permute-done((f32[64,512]{1,0:T(8,128)S(1)}, f32[64,512]{1,0:T(8,128)S(1)}, u32[]{:S(2)}, u32[]{:S(2)}) %collective-permute-start.6) | collective-permute-done | bytes 131104 | tf_op jit(solution)/shard_map/ppermute | solution.py:482
  49.0 1.9 %collective-permute-done.7.v1 = f32[64,512]{1,0:T(8,128)S(1)} collective-permute-done((f32[64,512]{1,0:T(8,128)S(1)}, f32[64,512]{1,0:T(8,128)S(1)}, u32[]{:S(2)}, u32[]{:S(2)}) %collective-permute-start.7) | collective-permute-done | bytes 131104 | tf_op jit(solution)/shard_map/ppermute | solution.py:482
  50.9 0.0 collective-permute-done.8.v2
  50.9 0.0 collective-permute-done.9.v3
  50.9 0.0 copy-done.3
  50.9 0.0 copy-done.4
  50.9 0.0 copy-done.5
  51.0 2.1 %shard_map.145 = f32[64,1024]{1,0:T(8,128)} custom-call(s32[1,1,4]{2,1,0:T(1,128)S(1)} %copy-done.5, f32[64,1024]{1,0:T(8,128)S(1)} %shard_map.144.sens_ref, s32[1,1,4,512]{3,2,1,0:T(4,128)S(1)} %copy-done.3, s32[1,1,2,256]{3,2,1,0:T(2,128)S(1)} %copy-done.4, f32[64,512]{1,0:T(8,128)S(1)} %collective-permute-done.6.v0, ...), custom_call_target="tpu_custom_call" | custom-call | flops 1500000000 | bytes 6000000 | tf_op jit(solution)/shard_map/pallas_call | solution.py:554
Async XLA Ops:
  0.6 13.1 %copy-start.7 = (bf16[400,192]{1,0:T(8,128)(2,1)S(1)}, bf16[400,192]{1,0:T(8,128)(2,1)}, u32[]{:S(2)}) copy-start(bf16[400,192]{1,0:T(8,128)(2,1)} %constant.12.clone.fold_ref) | copy-start | bytes 460804
  0.6 13.0 %copy-start.9 = (bf16[64,288]{1,0:T(8,128)(2,1)S(1)}, bf16[64,288]{1,0:T(8,128)(2,1)}, u32[]{:S(2)}) copy-start(bf16[64,288]{1,0:T(8,128)(2,1)} %constant.15.clone.join_ref) | copy-start | bytes 110596
  0.7 13.0 %copy-start.10 = (bf16[64,192]{1,0:T(8,128)(2,1)S(1)}, bf16[64,192]{1,0:T(8,128)(2,1)}, u32[]{:S(2)}) copy-start(bf16[64,192]{1,0:T(8,128)(2,1)} %constant.14.clone.own_ref) | copy-start | bytes 73732
  0.7 13.0 %copy-start.11 = (bf16[64,54]{1,0:T(8,128)(2,1)S(1)}, bf16[64,54]{1,0:T(8,128)(2,1)}, u32[]{:S(2)}) copy-start(bf16[64,54]{1,0:T(8,128)(2,1)} %constant.17.clone.sums_ref) | copy-start | bytes 20740
  0.7 13.0 %copy-start = (f32[64,1024]{1,0:T(8,128)S(1)}, f32[64,1024]{1,0:T(8,128)}, u32[]{:S(2)}) copy-start(f32[64,1024]{1,0:T(8,128)} %density_ref.1) | copy-start | bytes 786436
  0.7 13.0 %copy-start.2 = (s32[27,1024]{1,0:T(8,128)S(1)}, s32[27,1024]{1,0:T(8,128)}, u32[]{:S(2)}) copy-start(s32[27,1024]{1,0:T(8,128)} %links_ref.7) | copy-start | bytes 331780
  3.3 13.0 %collective-permute-start.4 = (f32[64,256]{1,0:T(8,128)}, f32[64,256]{1,0:T(8,128)S(1)}, u32[]{:S(2)}, u32[]{:S(2)}) collective-permute-start(f32[64,256]{1,0:T(8,128)} %get-tuple-element.22), channel_id=1, source_target_pairs={{0,1},{1,2},{2,3},{3,4},{4,5},{5,6},{6,7},{7,0},{8,9},{9,10},{10,1... | collective-permute-start | bytes 196616 | tf_op jit(solution)/shard_map/ppermute | solution.py:482
  3.3 15.7 %collective-permute-start.5 = (f32[64,256]{1,0:T(8,128)}, f32[64,256]{1,0:T(8,128)S(1)}, u32[]{:S(2)}, u32[]{:S(2)}) collective-permute-start(f32[64,256]{1,0:T(8,128)} %get-tuple-element.23), channel_id=1, source_target_pairs={{0,7},{1,0},{2,1},{3,2},{4,3},{5,4},{6,5},{7,6},{8,15},{9,8},{10,9... | collective-permute-start | bytes 196616 | tf_op jit(solution)/shard_map/ppermute | solution.py:482
  5.1 13.9 %collective-permute-start = (f32[64,512]{1,0:T(8,128)}, f32[64,512]{1,0:T(8,128)S(1)}, u32[]{:S(2)}, u32[]{:S(2)}) collective-permute-start(f32[64,512]{1,0:T(8,128)} %get-tuple-element.18), channel_id=1, source_target_pairs={{0,8},{8,16},{16,24},{24,32},{32,40},{40,48},{48,56},{56,64},{64,7... | collective-permute-start | bytes 393224 | tf_op jit(solution)/shard_map/ppermute | solution.py:482
  7.0 14.7 %collective-permute-start.1 = (f32[64,512]{1,0:T(8,128)}, f32[64,512]{1,0:T(8,128)S(1)}, u32[]{:S(2)}, u32[]{:S(2)}) collective-permute-start(f32[64,512]{1,0:T(8,128)} %get-tuple-element.19), channel_id=1, source_target_pairs={{0,16},{8,24},{16,32},{24,40},{32,48},{40,56},{48,64},{56,72},{64,... | collective-permute-start | bytes 393224 | tf_op jit(solution)/shard_map/ppermute | solution.py:482
  10.2 6.1 %copy-start.12 = (f32[64,512]{1,0:T(8,128)S(1)}, f32[64,512]{1,0:T(8,128)}, u32[]{:S(2)}) copy-start(f32[64,512]{1,0:T(8,128)} %get-tuple-element.21) | copy-start | bytes 393220
  10.2 14.6 %collective-permute-start.2 = (f32[64,512]{1,0:T(8,128)}, f32[64,512]{1,0:T(8,128)S(1)}, u32[]{:S(2)}, u32[]{:S(2)}) collective-permute-start(f32[64,512]{1,0:T(8,128)} %get-tuple-element.20), channel_id=1, source_target_pairs={{0,248},{8,0},{16,8},{24,16},{32,24},{40,32},{48,40},{56,48},{64,5... | collective-permute-start | bytes 393224 | tf_op jit(solution)/shard_map/ppermute | solution.py:482
  16.4 8.5 %collective-permute-start.3 = (f32[64,512]{1,0:T(8,128)S(1)}, f32[64,512]{1,0:T(8,128)S(1)}, u32[]{:S(2)}, u32[]{:S(2)}) collective-permute-start(f32[64,512]{1,0:T(8,128)S(1)} %copy-done.12), channel_id=1, source_target_pairs={{0,240},{8,248},{16,0},{24,8},{32,16},{40,24},{48,32},{56,40},{64,... | collective-permute-start | bytes 393224 | tf_op jit(solution)/shard_map/ppermute | solution.py:482
  21.7 3.2 %copy-start.1 = (f32[64,1024]{1,0:T(8,128)S(1)}, f32[64,1024]{1,0:T(8,128)}, u32[]{:S(2)}) copy-start(f32[64,1024]{1,0:T(8,128)} %energy_ref.1) | copy-start | bytes 786436
  21.7 3.2 %copy-start.6 = (bf16[512,192]{1,0:T(8,128)(2,1)S(1)}, bf16[512,192]{1,0:T(8,128)(2,1)}, u32[]{:S(2)}) copy-start(bf16[512,192]{1,0:T(8,128)(2,1)} %constant.13.clone.fold_b_ref) | copy-start | bytes 589828
  21.7 3.2 %copy-start.8 = (bf16[128,384]{1,0:T(8,128)(2,1)S(1)}, bf16[128,384]{1,0:T(8,128)(2,1)}, u32[]{:S(2)}) copy-start(bf16[128,384]{1,0:T(8,128)(2,1)} %constant.16.clone.join_b_ref) | copy-start | bytes 294916
  34.0 9.2 %collective-permute-start.10 = (f32[64,256]{1,0:T(8,128)S(1)}, f32[64,256]{1,0:T(8,128)S(1)}, u32[]{:S(2)}, u32[]{:S(2)}) collective-permute-start(f32[64,256]{1,0:T(8,128)S(1)} %get-tuple-element.32), channel_id=1, source_target_pairs={{0,1},{1,2},{2,3},{3,4},{4,5},{5,6},{6,7},{7,0},{8,9},{9,10},{10,1... | collective-permute-start | bytes 196616 | tf_op jit(solution)/shard_map/ppermute | solution.py:482
  34.0 13.8 %collective-permute-start.11 = (f32[64,256]{1,0:T(8,128)S(1)}, f32[64,256]{1,0:T(8,128)S(1)}, u32[]{:S(2)}, u32[]{:S(2)}) collective-permute-start(f32[64,256]{1,0:T(8,128)S(1)} %get-tuple-element.33), channel_id=1, source_target_pairs={{0,7},{1,0},{2,1},{3,2},{4,3},{5,4},{6,5},{7,6},{8,15},{9,8},{10,9... | collective-permute-start | bytes 196616 | tf_op jit(solution)/shard_map/ppermute | solution.py:482
  35.7 13.3 %collective-permute-start.6 = (f32[64,512]{1,0:T(8,128)S(1)}, f32[64,512]{1,0:T(8,128)S(1)}, u32[]{:S(2)}, u32[]{:S(2)}) collective-permute-start(f32[64,512]{1,0:T(8,128)S(1)} %get-tuple-element.28), channel_id=1, source_target_pairs={{0,16},{8,24},{16,32},{24,40},{32,48},{40,56},{48,64},{56,72},{64,... | collective-permute-start | bytes 393224 | tf_op jit(solution)/shard_map/ppermute | solution.py:482
  37.8 13.1 %collective-permute-start.7 = (f32[64,512]{1,0:T(8,128)S(1)}, f32[64,512]{1,0:T(8,128)S(1)}, u32[]{:S(2)}, u32[]{:S(2)}) collective-permute-start(f32[64,512]{1,0:T(8,128)S(1)} %get-tuple-element.29), channel_id=1, source_target_pairs={{0,8},{8,16},{16,24},{24,32},{32,40},{40,48},{48,56},{56,64},{64,7... | collective-permute-start | bytes 393224 | tf_op jit(solution)/shard_map/ppermute | solution.py:482
  39.1 11.9 %collective-permute-start.8 = (f32[64,512]{1,0:T(8,128)S(1)}, f32[64,512]{1,0:T(8,128)S(1)}, u32[]{:S(2)}, u32[]{:S(2)}) collective-permute-start(f32[64,512]{1,0:T(8,128)S(1)} %get-tuple-element.30), channel_id=1, source_target_pairs={{0,248},{8,0},{16,8},{24,16},{32,24},{40,32},{48,40},{56,48},{64,5... | collective-permute-start | bytes 393224 | tf_op jit(solution)/shard_map/ppermute | solution.py:482
  43.2 7.7 %collective-permute-start.9 = (f32[64,512]{1,0:T(8,128)S(1)}, f32[64,512]{1,0:T(8,128)S(1)}, u32[]{:S(2)}, u32[]{:S(2)}) collective-permute-start(f32[64,512]{1,0:T(8,128)S(1)} %get-tuple-element.31), channel_id=1, source_target_pairs={{0,240},{8,248},{16,0},{24,8},{32,16},{40,24},{48,32},{56,40},{64,... | collective-permute-start | bytes 393224 | tf_op jit(solution)/shard_map/ppermute | solution.py:482
  44.3 6.7 %copy-start.3 = (s32[1,1,4,512]{3,2,1,0:T(4,128)S(1)}, s32[1,1,4,512]{3,2,1,0:T(4,128)}, u32[]{:S(2)}) copy-start(s32[1,1,4,512]{3,2,1,0:T(4,128)} %index_ref.1) | copy-start | bytes 24580
  44.3 6.7 %copy-start.4 = (s32[1,1,2,256]{3,2,1,0:T(2,128)S(1)}, s32[1,1,2,256]{3,2,1,0:T(2,128)}, u32[]{:S(2)}) copy-start(s32[1,1,2,256]{3,2,1,0:T(2,128)} %face_ref.1) | copy-start | bytes 6148
  44.3 6.7 %copy-start.5 = (s32[1,1,4]{2,1,0:T(1,128)S(1)}, s32[1,1,4]{2,1,0:T(1,128)}, u32[]{:S(2)}) copy-start(s32[1,1,4]{2,1,0:T(1,128)} %live_ref.1) | copy-start | bytes 52

commit v5 on v4

--- a/solution.py
+++ b/solution.py
@@ -12,8 +12,8 @@
 OUTWARD = (2, 3, 1, 0)
 BACKWARD = (0, 1, 2, 3)
 LANE_LOCAL = 6
-LANE_EARLY = 5
-LANE_REMOTE = 6
+LANE_EARLY = 7
+LANE_REMOTE = 8
 radius = 3.0
 floor_value = 0.001
 penalty = 3.0

time: 53.2 us -> 52.7 us (level)
  Pallas kernels: 23.1 us -> 22.5 us
  transfers between devices with their start and end apart: 12 -> 12, of which waited for: 3 -> 4; matrix products, arithmetic and copies ran while one was open for 0% -> 0% of each run, Pallas kernels for 17% -> 17%
where the time goes in v5:
time: 52.7 us; the launch traced here: 52.6 us
  starting transfers between devices  23.3 us (44%)
  Pallas kernels  22.5 us (43%)
  waiting for transfers between devices  5.97 us (11%)
  between operations  0.82 us (2%)
    ppermute x12, starting transfers between devices, passed_along(): return lax.ppermute(shard, axis, pairs)  23.3 us
    pallas_call x1, Pallas kernels, on_device(): pl.pallas_call(remote_kernel, out_shape=[whole, whole] + [listed] * 4 + [...  8.64 us
    ppermute x12, waiting for transfers between devices, passed_along(): return lax.ppermute(shard, axis, pairs)  5.97 us
    pallas_call x1, Pallas kernels, on_device(): pl.pallas_call(own_kernel, out_shape=whole, in_specs=[vmem] * 5, out_spec...  3.56 us
    pallas_call x1, Pallas kernels, on_device(): pl.pallas_call(early_kernel, out_shape=whole, in_specs=[vmem] * 8, out_sp...  2.92 us
    pallas_call x1, Pallas kernels, on_device(): pl.pallas_call(local_kernel, out_shape=[whole, whole], in_specs=[vmem] *...  2.63 us
    pallas_call x1, Pallas kernels, on_device(): pl.pallas_call(payload_kernel, out_shape=[listed] * 4 + [faced] * 2, in_s...  2.59 us
    pallas_call x1, Pallas kernels, on_device(): pl.pallas_call(final_kernel, out_shape=whole, in_specs=[smem] + [vmem] *...  2.13 us
  transfers between devices with their start and end apart: 12, of which 4 were waited for; matrix products, arithmetic and copies ran while one was open for 0% of the time, Pallas kernels for 17%

profile of v5, /device:TPU:8, one launch (start us, length us, event | category | flops | bytes accessed | tf_op | source)
XLA Modules:
  0.0 52.6 jit_solution(13749780188542978204)
XLA Ops:
  0.6 0.0 copy-start.7
  0.6 0.0 copy-start.9
  0.7 0.0 copy-start.10
  0.7 0.0 copy-start.11
  0.7 0.0 copy-start
  0.7 0.0 copy-start.2
  0.7 2.6 %shard_map.140 = (f32[64,512]{1,0:T(8,128)}, f32[64,512]{1,0:T(8,128)}, f32[64,512]{1,0:T(8,128)}, f32[64,512]{1,0:T(8,128)}, f32[64,256]{1,0:T(8,128)}, /*index=5*/f32[64,256]{1,0:T(8,128)}) custom-call(s32[1,1,4]{2,1,0:T(1,128)} %live_ref.1, f32[64,1024]{1,0:T(8,128)} %density_ref.1, s32[1,1,4,512]{3,2,1,0:T(4,128)} %index_ref.1, s32[1,1,2,256]{3,2,1,0:T(2,128)} %face_ref.1), custom_call_target="tpu_custom_call" | custom-call | flops 1500000000 | bytes 6000000 | tf_op jit(solution)/shard_map/pallas_call | solution.py:495
  3.3 0.0 collective-permute-start.4
  3.3 1.7 %collective-permute-start.5 = (f32[64,256]{1,0:T(8,128)}, f32[64,256]{1,0:T(8,128)S(1)}, u32[]{:S(2)}, u32[]{:S(2)}) collective-permute-start(f32[64,256]{1,0:T(8,128)} %get-tuple-element.23), channel_id=1, source_target_pairs={{0,7},{1,0},{2,1},{3,2},{4,3},{5,4},{6,5},{7,6},{8,15},{9,8},{10,9... | collective-permute-start | bytes 196616 | tf_op jit(solution)/shard_map/ppermute | solution.py:482
  5.1 1.9 %collective-permute-start = (f32[64,512]{1,0:T(8,128)}, f32[64,512]{1,0:T(8,128)S(1)}, u32[]{:S(2)}, u32[]{:S(2)}) collective-permute-start(f32[64,512]{1,0:T(8,128)} %get-tuple-element.18), channel_id=1, source_target_pairs={{0,8},{8,16},{16,24},{24,32},{32,40},{40,48},{48,56},{56,64},{64,7... | collective-permute-start | bytes 393224 | tf_op jit(solution)/shard_map/ppermute | solution.py:482
  7.0 3.3 %collective-permute-start.1 = (f32[64,512]{1,0:T(8,128)}, f32[64,512]{1,0:T(8,128)S(1)}, u32[]{:S(2)}, u32[]{:S(2)}) collective-permute-start(f32[64,512]{1,0:T(8,128)} %get-tuple-element.19), channel_id=1, source_target_pairs={{0,16},{8,24},{16,32},{24,40},{32,48},{40,56},{48,64},{56,72},{64,... | collective-permute-start | bytes 393224 | tf_op jit(solution)/shard_map/ppermute | solution.py:482
  10.2 0.0 copy-start.12
  10.2 3.4 %collective-permute-start.2 = (f32[64,512]{1,0:T(8,128)}, f32[64,512]{1,0:T(8,128)S(1)}, u32[]{:S(2)}, u32[]{:S(2)}) collective-permute-start(f32[64,512]{1,0:T(8,128)} %get-tuple-element.20), channel_id=1, source_target_pairs={{0,248},{8,0},{16,8},{24,16},{32,24},{40,32},{48,40},{56,48},{64,5... | collective-permute-start | bytes 393224 | tf_op jit(solution)/shard_map/ppermute | solution.py:482
  13.7 0.0 copy-done.7
  13.7 0.0 copy-done.9
  13.7 0.0 copy-done.10
  13.7 0.0 copy-done.11
  13.7 0.0 copy-done
  13.7 0.0 copy-done.2
  13.7 2.6 %shard_map.141 = (f32[64,1024]{1,0:T(8,128)S(1)}, f32[64,1024]{1,0:T(8,128)S(1)}) custom-call(f32[64,1024]{1,0:T(8,128)S(1)} %copy-done, s32[27,1024]{1,0:T(8,128)S(1)} %copy-done.2, bf16[400,192]{1,0:T(8,128)(2,1)S(1)} %copy-done.7, bf16[64,288]{1,0:T(8,128)(2,1)S(1)} %copy-done.9, bf16[64,192]{1,0:T(8,128)(2,1)S(1)} %copy-done.10, ...), custom_call_target="tpu_custom_call" | custom-call | flops 4000000000 | bytes 16000000 | tf_op jit(solution)/shard_map/pallas_call | solution.py:513
  16.3 0.0 collective-permute-done.4.low_ref
  16.3 0.0 copy-done.12
  16.4 2.6 %collective-permute-start.3 = (f32[64,512]{1,0:T(8,128)S(1)}, f32[64,512]{1,0:T(8,128)S(1)}, u32[]{:S(2)}, u32[]{:S(2)}) collective-permute-start(f32[64,512]{1,0:T(8,128)S(1)} %copy-done.12), channel_id=1, source_target_pairs={{0,240},{8,248},{16,0},{24,8},{32,16},{40,24},{48,32},{56,40},{64,... | collective-permute-start | bytes 393224 | tf_op jit(solution)/shard_map/ppermute | solution.py:482
  19.0 0.0 collective-permute-done.5.high_ref
  19.0 0.0 collective-permute-done.r0
  19.0 2.7 %collective-permute-done.1.r1 = f32[64,512]{1,0:T(8,128)S(1)} collective-permute-done((f32[64,512]{1,0:T(8,128)}, f32[64,512]{1,0:T(8,128)S(1)}, u32[]{:S(2)}, u32[]{:S(2)}) %collective-permute-start.1) | collective-permute-done | bytes 131104 | tf_op jit(solution)/shard_map/ppermute | solution.py:482
  21.7 0.0 copy-start.1
  21.7 0.0 copy-start.6
  21.7 0.0 copy-start.8
  21.7 2.9 %shard_map.142.part_ref = f32[64,1024]{1,0:T(8,128)S(1)} custom-call(f32[64,512]{1,0:T(8,128)S(1)} %collective-permute-done.r0, f32[64,512]{1,0:T(8,128)S(1)} %collective-permute-done.1.r1, f32[64,256]{1,0:T(8,128)S(1)} %collective-permute-done.4.low_ref, f32[64,256]{1,0:T(8,128)S(1)} %collective-permute-done.5.high_ref, s32[27,1024]{1,0:T(8,128)S(1)} %copy-done.2, ...), custom_call_target="tpu_custom_call" | custom-call | flops 2000000000 | bytes 8000000 | tf_op jit(solution)/shard_map/pallas_call | solution.py:522
  24.6 0.0 collective-permute-done.2.r2
  24.7 0.0 collective-permute-done.3.r3
  24.7 0.0 copy-done.1
  24.7 0.0 copy-done.6
  24.7 0.0 copy-done.8
  24.7 8.6 %shard_map.143 = (f32[64,1024]{1,0:T(8,128)}, f32[64,1024]{1,0:T(8,128)S(1)}, f32[64,512]{1,0:T(8,128)S(1)}, f32[64,512]{1,0:T(8,128)S(1)}, f32[64,512]{1,0:T(8,...) custom-call(f32[64,512]{1,0:T(8,128)S(1)} %collective-permute-done.r0, ...), custom_call_target="tpu_custom_call" | custom-call | flops 10000000000 | bytes 40000000 | tf_op jit(solution)/shard_map/pallas_call | solution.py:531
  33.3 0.0 collective-permute-start.10
  33.4 1.7 %collective-permute-start.11 = (f32[64,256]{1,0:T(8,128)S(1)}, f32[64,256]{1,0:T(8,128)S(1)}, u32[]{:S(2)}, u32[]{:S(2)}) collective-permute-start(f32[64,256]{1,0:T(8,128)S(1)} %get-tuple-element.33), channel_id=1, source_target_pairs={{0,7},{1,0},{2,1},{3,2},{4,3},{5,4},{6,5},{7,6},{8,15},{9,8},{10,9... | collective-permute-start | bytes 196616 | tf_op jit(solution)/shard_map/ppermute | solution.py:482
  35.1 2.3 %collective-permute-start.6 = (f32[64,512]{1,0:T(8,128)S(1)}, f32[64,512]{1,0:T(8,128)S(1)}, u32[]{:S(2)}, u32[]{:S(2)}) collective-permute-start(f32[64,512]{1,0:T(8,128)S(1)} %get-tuple-element.28), channel_id=1, source_target_pairs={{0,16},{8,24},{16,32},{24,40},{32,48},{40,56},{48,64},{56,72},{64,... | collective-permute-start | bytes 393224 | tf_op jit(solution)/shard_map/ppermute | solution.py:482
  37.4 1.2 %collective-permute-start.7 = (f32[64,512]{1,0:T(8,128)S(1)}, f32[64,512]{1,0:T(8,128)S(1)}, u32[]{:S(2)}, u32[]{:S(2)}) collective-permute-start(f32[64,512]{1,0:T(8,128)S(1)} %get-tuple-element.29), channel_id=1, source_target_pairs={{0,8},{8,16},{16,24},{24,32},{32,40},{40,48},{48,56},{56,64},{64,7... | collective-permute-start | bytes 393224 | tf_op jit(solution)/shard_map/ppermute | solution.py:482
  38.6 4.1 %collective-permute-start.8 = (f32[64,512]{1,0:T(8,128)S(1)}, f32[64,512]{1,0:T(8,128)S(1)}, u32[]{:S(2)}, u32[]{:S(2)}) collective-permute-start(f32[64,512]{1,0:T(8,128)S(1)} %get-tuple-element.30), channel_id=1, source_target_pairs={{0,248},{8,0},{16,8},{24,16},{32,24},{40,32},{48,40},{56,48},{64,5... | collective-permute-start | bytes 393224 | tf_op jit(solution)/shard_map/ppermute | solution.py:482
  42.8 0.0 collective-permute-done.10.v4
  42.8 0.9 %collective-permute-start.9 = (f32[64,512]{1,0:T(8,128)S(1)}, f32[64,512]{1,0:T(8,128)S(1)}, u32[]{:S(2)}, u32[]{:S(2)}) collective-permute-start(f32[64,512]{1,0:T(8,128)S(1)} %get-tuple-element.31), channel_id=1, source_target_pairs={{0,240},{8,248},{16,0},{24,8},{32,16},{40,24},{48,32},{56,40},{64,... | collective-permute-start | bytes 393224 | tf_op jit(solution)/shard_map/ppermute | solution.py:482
  43.7 0.0 copy-start.3
  43.7 0.0 copy-start.4
  43.7 0.0 copy-start.5
  43.7 3.6 %shard_map.144.sens_ref = f32[64,1024]{1,0:T(8,128)S(1)} custom-call(f32[64,1024]{1,0:T(8,128)S(1)} %get-tuple-element.27.scaled_ref, s32[27,1024]{1,0:T(8,128)S(1)} %copy-done.2, bf16[512,192]{1,0:T(8,128)(2,1)S(1)} %copy-done.6, bf16[128,384]{1,0:T(8,128)(2,1)S(1)} %copy-done.8, bf16[64,192]{1,0:T(8,128)(2,1)S(1)} %copy-done.10), custom_call_target="tpu_custom_call" | custom-call | flops 4000000000 | bytes 16000000 | tf_op jit(solution)/shard_map/pallas_call | solution.py:546
  47.2 0.0 collective-permute-done.11.v5
  47.2 1.3 %collective-permute-done.6.v0 = f32[64,512]{1,0:T(8,128)S(1)} collective-permute-done((f32[64,512]{1,0:T(8,128)S(1)}, f32[64,512]{1,0:T(8,128)S(1)}, u32[]{:S(2)}, u32[]{:S(2)}) %collective-permute-start.6) | collective-permute-done | bytes 131104 | tf_op jit(solution)/shard_map/ppermute | solution.py:482
  48.5 1.8 %collective-permute-done.7.v1 = f32[64,512]{1,0:T(8,128)S(1)} collective-permute-done((f32[64,512]{1,0:T(8,128)S(1)}, f32[64,512]{1,0:T(8,128)S(1)}, u32[]{:S(2)}, u32[]{:S(2)}) %collective-permute-start.7) | collective-permute-done | bytes 131104 | tf_op jit(solution)/shard_map/ppermute | solution.py:482
  50.3 0.0 collective-permute-done.8.v2
  50.3 0.1 collective-permute-done.9.v3
  50.4 0.0 copy-done.3
  50.5 0.0 copy-done.4
  50.5 0.0 copy-done.5
  50.5 2.1 %shard_map.145 = f32[64,1024]{1,0:T(8,128)} custom-call(s32[1,1,4]{2,1,0:T(1,128)S(1)} %copy-done.5, f32[64,1024]{1,0:T(8,128)S(1)} %shard_map.144.sens_ref, s32[1,1,4,512]{3,2,1,0:T(4,128)S(1)} %copy-done.3, s32[1,1,2,256]{3,2,1,0:T(2,128)S(1)} %copy-done.4, f32[64,512]{1,0:T(8,128)S(1)} %collective-permute-done.6.v0, ...), custom_call_target="tpu_custom_call" | custom-call | flops 1500000000 | bytes 6000000 | tf_op jit(solution)/shard_map/pallas_call | solution.py:554
Async XLA Ops:
  0.6 13.1 %copy-start.7 = (bf16[400,192]{1,0:T(8,128)(2,1)S(1)}, bf16[400,192]{1,0:T(8,128)(2,1)}, u32[]{:S(2)}) copy-start(bf16[400,192]{1,0:T(8,128)(2,1)} %constant.12.clone.fold_ref) | copy-start | bytes 460804
  0.6 13.0 %copy-start.9 = (bf16[64,288]{1,0:T(8,128)(2,1)S(1)}, bf16[64,288]{1,0:T(8,128)(2,1)}, u32[]{:S(2)}) copy-start(bf16[64,288]{1,0:T(8,128)(2,1)} %constant.15.clone.join_ref) | copy-start | bytes 110596
  0.7 13.0 %copy-start.10 = (bf16[64,192]{1,0:T(8,128)(2,1)S(1)}, bf16[64,192]{1,0:T(8,128)(2,1)}, u32[]{:S(2)}) copy-start(bf16[64,192]{1,0:T(8,128)(2,1)} %constant.14.clone.own_ref) | copy-start | bytes 73732
  0.7 13.0 %copy-start.11 = (bf16[64,54]{1,0:T(8,128)(2,1)S(1)}, bf16[64,54]{1,0:T(8,128)(2,1)}, u32[]{:S(2)}) copy-start(bf16[64,54]{1,0:T(8,128)(2,1)} %constant.17.clone.sums_ref) | copy-start | bytes 20740
  0.7 13.0 %copy-start = (f32[64,1024]{1,0:T(8,128)S(1)}, f32[64,1024]{1,0:T(8,128)}, u32[]{:S(2)}) copy-start(f32[64,1024]{1,0:T(8,128)} %density_ref.1) | copy-start | bytes 786436
  0.7 13.0 %copy-start.2 = (s32[27,1024]{1,0:T(8,128)S(1)}, s32[27,1024]{1,0:T(8,128)}, u32[]{:S(2)}) copy-start(s32[27,1024]{1,0:T(8,128)} %links_ref.7) | copy-start | bytes 331780
  3.3 13.0 %collective-permute-start.4 = (f32[64,256]{1,0:T(8,128)}, f32[64,256]{1,0:T(8,128)S(1)}, u32[]{:S(2)}, u32[]{:S(2)}) collective-permute-start(f32[64,256]{1,0:T(8,128)} %get-tuple-element.22), channel_id=1, source_target_pairs={{0,1},{1,2},{2,3},{3,4},{4,5},{5,6},{6,7},{7,0},{8,9},{9,10},{10,1... | collective-permute-start | bytes 196616 | tf_op jit(solution)/shard_map/ppermute | solution.py:482
  3.3 15.7 %collective-permute-start.5 = (f32[64,256]{1,0:T(8,128)}, f32[64,256]{1,0:T(8,128)S(1)}, u32[]{:S(2)}, u32[]{:S(2)}) collective-permute-start(f32[64,256]{1,0:T(8,128)} %get-tuple-element.23), channel_id=1, source_target_pairs={{0,7},{1,0},{2,1},{3,2},{4,3},{5,4},{6,5},{7,6},{8,15},{9,8},{10,9... | collective-permute-start | bytes 196616 | tf_op jit(solution)/shard_map/ppermute | solution.py:482
  5.1 13.9 %collective-permute-start = (f32[64,512]{1,0:T(8,128)}, f32[64,512]{1,0:T(8,128)S(1)}, u32[]{:S(2)}, u32[]{:S(2)}) collective-permute-start(f32[64,512]{1,0:T(8,128)} %get-tuple-element.18), channel_id=1, source_target_pairs={{0,8},{8,16},{16,24},{24,32},{32,40},{40,48},{48,56},{56,64},{64,7... | collective-permute-start | bytes 393224 | tf_op jit(solution)/shard_map/ppermute | solution.py:482
  7.0 14.7 %collective-permute-start.1 = (f32[64,512]{1,0:T(8,128)}, f32[64,512]{1,0:T(8,128)S(1)}, u32[]{:S(2)}, u32[]{:S(2)}) collective-permute-start(f32[64,512]{1,0:T(8,128)} %get-tuple-element.19), channel_id=1, source_target_pairs={{0,16},{8,24},{16,32},{24,40},{32,48},{40,56},{48,64},{56,72},{64,... | collective-permute-start | bytes 393224 | tf_op jit(solution)/shard_map/ppermute | solution.py:482
  10.2 6.1 %copy-start.12 = (f32[64,512]{1,0:T(8,128)S(1)}, f32[64,512]{1,0:T(8,128)}, u32[]{:S(2)}) copy-start(f32[64,512]{1,0:T(8,128)} %get-tuple-element.21) | copy-start | bytes 393220
  10.2 14.4 %collective-permute-start.2 = (f32[64,512]{1,0:T(8,128)}, f32[64,512]{1,0:T(8,128)S(1)}, u32[]{:S(2)}, u32[]{:S(2)}) collective-permute-start(f32[64,512]{1,0:T(8,128)} %get-tuple-element.20), channel_id=1, source_target_pairs={{0,248},{8,0},{16,8},{24,16},{32,24},{40,32},{48,40},{56,48},{64,5... | collective-permute-start | bytes 393224 | tf_op jit(solution)/shard_map/ppermute | solution.py:482
  16.4 8.3 %collective-permute-start.3 = (f32[64,512]{1,0:T(8,128)S(1)}, f32[64,512]{1,0:T(8,128)S(1)}, u32[]{:S(2)}, u32[]{:S(2)}) collective-permute-start(f32[64,512]{1,0:T(8,128)S(1)} %copy-done.12), channel_id=1, source_target_pairs={{0,240},{8,248},{16,0},{24,8},{32,16},{40,24},{48,32},{56,40},{64,... | collective-permute-start | bytes 393224 | tf_op jit(solution)/shard_map/ppermute | solution.py:482
  21.7 3.0 %copy-start.1 = (f32[64,1024]{1,0:T(8,128)S(1)}, f32[64,1024]{1,0:T(8,128)}, u32[]{:S(2)}) copy-start(f32[64,1024]{1,0:T(8,128)} %energy_ref.1) | copy-start | bytes 786436
  21.7 3.0 %copy-start.6 = (bf16[512,192]{1,0:T(8,128)(2,1)S(1)}, bf16[512,192]{1,0:T(8,128)(2,1)}, u32[]{:S(2)}) copy-start(bf16[512,192]{1,0:T(8,128)(2,1)} %constant.13.clone.fold_b_ref) | copy-start | bytes 589828
  21.7 3.0 %copy-start.8 = (bf16[128,384]{1,0:T(8,128)(2,1)S(1)}, bf16[128,384]{1,0:T(8,128)(2,1)}, u32[]{:S(2)}) copy-start(bf16[128,384]{1,0:T(8,128)(2,1)} %constant.16.clone.join_b_ref) | copy-start | bytes 294916
  33.3 9.4 %collective-permute-start.10 = (f32[64,256]{1,0:T(8,128)S(1)}, f32[64,256]{1,0:T(8,128)S(1)}, u32[]{:S(2)}, u32[]{:S(2)}) collective-permute-start(f32[64,256]{1,0:T(8,128)S(1)} %get-tuple-element.32), channel_id=1, source_target_pairs={{0,1},{1,2},{2,3},{3,4},{4,5},{5,6},{6,7},{7,0},{8,9},{9,10},{10,1... | collective-permute-start | bytes 196616 | tf_op jit(solution)/shard_map/ppermute | solution.py:482
  33.4 13.9 %collective-permute-start.11 = (f32[64,256]{1,0:T(8,128)S(1)}, f32[64,256]{1,0:T(8,128)S(1)}, u32[]{:S(2)}, u32[]{:S(2)}) collective-permute-start(f32[64,256]{1,0:T(8,128)S(1)} %get-tuple-element.33), channel_id=1, source_target_pairs={{0,7},{1,0},{2,1},{3,2},{4,3},{5,4},{6,5},{7,6},{8,15},{9,8},{10,9... | collective-permute-start | bytes 196616 | tf_op jit(solution)/shard_map/ppermute | solution.py:482
  35.1 13.4 %collective-permute-start.6 = (f32[64,512]{1,0:T(8,128)S(1)}, f32[64,512]{1,0:T(8,128)S(1)}, u32[]{:S(2)}, u32[]{:S(2)}) collective-permute-start(f32[64,512]{1,0:T(8,128)S(1)} %get-tuple-element.28), channel_id=1, source_target_pairs={{0,16},{8,24},{16,32},{24,40},{32,48},{40,56},{48,64},{56,72},{64,... | collective-permute-start | bytes 393224 | tf_op jit(solution)/shard_map/ppermute | solution.py:482
  37.4 12.9 %collective-permute-start.7 = (f32[64,512]{1,0:T(8,128)S(1)}, f32[64,512]{1,0:T(8,128)S(1)}, u32[]{:S(2)}, u32[]{:S(2)}) collective-permute-start(f32[64,512]{1,0:T(8,128)S(1)} %get-tuple-element.29), channel_id=1, source_target_pairs={{0,8},{8,16},{16,24},{24,32},{32,40},{40,48},{48,56},{56,64},{64,7... | collective-permute-start | bytes 393224 | tf_op jit(solution)/shard_map/ppermute | solution.py:482
  38.6 11.7 %collective-permute-start.8 = (f32[64,512]{1,0:T(8,128)S(1)}, f32[64,512]{1,0:T(8,128)S(1)}, u32[]{:S(2)}, u32[]{:S(2)}) collective-permute-start(f32[64,512]{1,0:T(8,128)S(1)} %get-tuple-element.30), channel_id=1, source_target_pairs={{0,248},{8,0},{16,8},{24,16},{32,24},{40,32},{48,40},{56,48},{64,5... | collective-permute-start | bytes 393224 | tf_op jit(solution)/shard_map/ppermute | solution.py:482
  42.8 7.7 %collective-permute-start.9 = (f32[64,512]{1,0:T(8,128)S(1)}, f32[64,512]{1,0:T(8,128)S(1)}, u32[]{:S(2)}, u32[]{:S(2)}) collective-permute-start(f32[64,512]{1,0:T(8,128)S(1)} %get-tuple-element.31), channel_id=1, source_target_pairs={{0,240},{8,248},{16,0},{24,8},{32,16},{40,24},{48,32},{56,40},{64,... | collective-permute-start | bytes 393224 | tf_op jit(solution)/shard_map/ppermute | solution.py:482
  43.7 6.8 %copy-start.3 = (s32[1,1,4,512]{3,2,1,0:T(4,128)S(1)}, s32[1,1,4,512]{3,2,1,0:T(4,128)}, u32[]{:S(2)}) copy-start(s32[1,1,4,512]{3,2,1,0:T(4,128)} %index_ref.1) | copy-start | bytes 24580
  43.7 6.8 %copy-start.4 = (s32[1,1,2,256]{3,2,1,0:T(2,128)S(1)}, s32[1,1,2,256]{3,2,1,0:T(2,128)}, u32[]{:S(2)}) copy-start(s32[1,1,2,256]{3,2,1,0:T(2,128)} %face_ref.1) | copy-start | bytes 6148
  43.7 6.8 %copy-start.5 = (s32[1,1,4]{2,1,0:T(1,128)S(1)}, s32[1,1,4]{2,1,0:T(1,128)}, u32[]{:S(2)}) copy-start(s32[1,1,4]{2,1,0:T(1,128)} %live_ref.1) | copy-start | bytes 52
